TPU v7x, 256 devices: a whole 4x4x8 slice. The times are simulated.
256 devices in a mesh: seq: 16 (over z, core), dp: 16 (over x, y).
Axes of the slice: x: 4, y: 4, z: 8, core: 2. Of those that a mesh axis runs over, the one named last changes fastest.
Arguments:
- q_proj: bfloat16 [16, 3072, 16, 128], P('dp', 'seq'), may hold values from -6 to 6
- k_proj: bfloat16 [16, 3072, 4, 128], P('dp', 'seq'), may hold values from -6 to 6
- v_proj: bfloat16 [16, 3072, 4, 128], P('dp', 'seq'), may hold values from -6 to 6
- upstream: bfloat16 [16, 3072, 16, 128], P('dp', 'seq'), may hold values from -6 to 6
- segment_ids: int32 [16, 3072], P('dp', 'seq'), may hold values from 0 to 6, as said below
- tree_tiles: int32 [16, 140, 3], P('dp'), may hold values from 0 to 23, as said below
- rewards: float32 [16, 5], P('dp'), may hold values from 0 to 1
- q_gain: float32 [128], replicated, may hold values from 0.1 to 1.9
- k_gain: float32 [128], replicated, may hold values from 0.1 to 1.9
Outputs:
- attn_out: bfloat16 [16, 3072, 16, 128], P('dp', 'seq')
- dq_proj: bfloat16 [16, 3072, 16, 128], P('dp', 'seq')
- dk_proj: bfloat16 [16, 3072, 4, 128], P('dp', 'seq')
- dv_proj: bfloat16 [16, 3072, 4, 128], P('dp', 'seq')
- q_gain_grad: float32 [128], replicated
- k_gain_grad: float32 [128], replicated
Inputs may be any that keep to these rules, and one draw needn't show every extreme that they name: `tree_tiles`: kind 0 entries are padding. Each response fills 1 to 4 whole tiles right after the prompt or the previous response; its tokens see all prompt tiles fully, earlier tiles of the same response fully and their own tile by kind 2; the prompt's 4 tiles see each other causally. Live entries are distinct and in no fixed order. `segment_ids`: agrees with tree_tiles: segments follow the tile order of the tree; empty slots come last.
All inputs are finite; a program needn't handle non-finite values.
Results may differ from a plain program's by a relative error of at most 0.012.
Values may be sent and summed in bfloat16 or wider, within the bound.
No kernel may reach another device: no remote copies, remote signals or barrier semaphores. Data moves between devices by JAX's collectives and lax.ppermute only.
A program may use at most 128 MiB of HBM per device.

v0:
```python
import math

import jax
import jax.numpy as jnp
from jax import lax
from jax.sharding import PartitionSpec as P

BLOCK = 128
RESPONSES = 5


norm_eps = 1e-06
rope_base = 1000000.0


def tree_table(tile_list, block_count):
    query_tile = tile_list[:, 0]
    key_tile = tile_list[:, 1]
    tile_kind = tile_list[:, 2]
    tile_ids = jnp.arange(block_count, dtype=jnp.int32)
    row_hits = (query_tile[:, None] == tile_ids[None, :]).astype(jnp.int32) * tile_kind[:, None]
    col_hits = (key_tile[:, None] == tile_ids[None, :]).astype(jnp.int32)
    table = jnp.einsum("tq,tk->qk", row_hits, col_hits)
    candidate = jnp.where((table > 0) & (tile_ids[None, :] >= 4), tile_ids[None, :], block_count)
    return (table, jnp.min(candidate, axis=1))


def positions(token_at, first_tile, block_count):
    tile_of = token_at // BLOCK
    tile_ids = jnp.arange(block_count, dtype=jnp.int32)
    begins = jnp.sum(
        (tile_of[:, None] == tile_ids[None, :]).astype(jnp.int32) * first_tile[None, :], axis=1
    )
    inside = (tile_of >= 4) & (begins < block_count)
    return jnp.where(inside, 4 * BLOCK + token_at - begins * BLOCK, token_at)


def rope_tables(place, head_width):
    half_width = head_width // 2
    freq = jnp.exp(
        jnp.arange(half_width, dtype=jnp.float32) * (-2.0 * math.log(rope_base) / head_width)
    )
    angle = place.astype(jnp.float32)[:, None] * freq[None, :]
    cosine = jnp.cos(angle)
    sine = jnp.sin(angle)
    return (jnp.concatenate([cosine, cosine], axis=1), jnp.concatenate([sine, sine], axis=1))


def prepare(values, gain, cosine, sine):
    factor = lax.rsqrt(jnp.mean(values * values, axis=-1, keepdims=True) + norm_eps)
    normed = values * factor * gain
    half_width = normed.shape[-1] // 2
    turned = jnp.concatenate([-normed[..., half_width:], normed[..., :half_width]], axis=-1)
    return normed * cosine[:, None, :] + turned * sine[:, None, :]


def block_mask(table, row_start, key_begin):
    upper = table[row_start // BLOCK : row_start // BLOCK + 4]
    kinds = jnp.concatenate(
        [upper[:, :4], upper[:, key_begin // BLOCK : key_begin // BLOCK + 7]], axis=1
    )
    kinds = jnp.repeat(jnp.repeat(kinds, BLOCK, axis=0), BLOCK, axis=1)
    query_at = row_start + jnp.arange(4 * BLOCK, dtype=jnp.int32)
    key_at = jnp.concatenate(
        [jnp.arange(4 * BLOCK, dtype=jnp.int32), key_begin + jnp.arange(7 * BLOCK, dtype=jnp.int32)]
    )
    return (kinds == 1) | (kinds == 2) & (key_at[None, :] <= query_at[:, None])


def block_step(query_rows, key_rows, value_rows, grad_rows, allowed, factor):
    scores = (
        jnp.einsum("qd,kd->qk", query_rows, key_rows, preferred_element_type=jnp.float32) * factor
    )
    unnormed = jnp.where(allowed, jnp.exp(scores), 0.0)
    totals = jnp.sum(unnormed, axis=1, keepdims=True)
    weights = (unnormed / jnp.where(totals > 0, totals, 1.0)).astype(jnp.bfloat16)
    out_rows = jnp.dot(weights, value_rows, preferred_element_type=jnp.float32).astype(jnp.bfloat16)
    dweights = jnp.einsum("qd,kd->qk", grad_rows, value_rows, preferred_element_type=jnp.float32)
    weights_wide = weights.astype(jnp.float32)
    deltas = jnp.sum(weights_wide * dweights, axis=1, keepdims=True)
    dscores = (weights_wide * (dweights - deltas) * factor).astype(jnp.bfloat16)
    dq_rows = jnp.dot(dscores, key_rows, preferred_element_type=jnp.float32).astype(jnp.bfloat16)
    dk_rows = jnp.einsum("qk,qd->kd", dscores, query_rows, preferred_element_type=jnp.float32)
    dv_rows = jnp.einsum("qk,qd->kd", weights, grad_rows, preferred_element_type=jnp.float32)
    return (out_rows, dq_rows, dk_rows, dv_rows)


def head_attention(query_head, key_head, value_head, grad_head, table):
    seq_len, head_width = query_head.shape
    factor = 1.0 / math.sqrt(head_width)
    prompt_len = 4 * BLOCK
    window = 7 * BLOCK
    out_parts = []
    dq_parts = []
    dk_total = jnp.zeros((seq_len, head_width), jnp.float32)
    dv_total = jnp.zeros((seq_len, head_width), jnp.float32)
    for row_start in range(0, seq_len, 4 * BLOCK):
        key_begin = min(max(row_start - 3 * BLOCK, prompt_len), seq_len - window)
        key_rows = jnp.concatenate(
            [key_head[:prompt_len], key_head[key_begin : key_begin + window]], axis=0
        )
        value_rows = jnp.concatenate(
            [value_head[:prompt_len], value_head[key_begin : key_begin + window]], axis=0
        )
        allowed = block_mask(table, row_start, key_begin)
        query_rows = query_head[row_start : row_start + 4 * BLOCK]
        grad_rows = grad_head[row_start : row_start + 4 * BLOCK]
        out_rows, dq_rows, dk_rows, dv_rows = block_step(
            query_rows, key_rows, value_rows, grad_rows, allowed, factor
        )
        out_parts.append(out_rows)
        dq_parts.append(dq_rows)
        dk_total = (
            dk_total.at[:prompt_len]
            .add(dk_rows[:prompt_len])
            .at[key_begin : key_begin + window]
            .add(dk_rows[prompt_len:])
        )
        dv_total = (
            dv_total.at[:prompt_len]
            .add(dv_rows[:prompt_len])
            .at[key_begin : key_begin + window]
            .add(dv_rows[prompt_len:])
        )
    return (
        jnp.concatenate(out_parts, axis=0),
        jnp.concatenate(dq_parts, axis=0),
        dk_total,
        dv_total,
    )


def per_device(q_proj, k_proj, v_proj, upstream, segment_ids, tree_tiles, rewards, q_gain, k_gain):
    local_tokens = q_proj.shape[1]
    head_count = q_proj.shape[2]
    head_width = q_proj.shape[3]
    kv_count = k_proj.shape[2]
    group_size = head_count // kv_count
    seq_len = local_tokens * lax.axis_size("seq")
    block_count = seq_len // BLOCK
    table, first_tile = tree_table(tree_tiles[0], block_count)
    token_at = lax.axis_index("seq") * local_tokens + jnp.arange(local_tokens, dtype=jnp.int32)
    place = positions(token_at, first_tile, block_count)
    cosine, sine = rope_tables(place, head_width)

    def rotate(values, gain):
        return prepare(values, gain, cosine, sine)

    q_turned, q_pull = jax.vjp(rotate, q_proj[0].astype(jnp.float32), q_gain)
    k_turned, k_pull = jax.vjp(rotate, k_proj[0].astype(jnp.float32), k_gain)
    query_send = q_turned.astype(jnp.bfloat16)
    key_rotated = k_turned.astype(jnp.bfloat16)
    advantage = rewards[0] - jnp.mean(rewards[0])
    labels = jnp.arange(1, RESPONSES + 1, dtype=jnp.int32)
    token_adv = jnp.sum(
        jnp.where(segment_ids[0][:, None] == labels[None, :], advantage[None, :], 0.0), axis=1
    )
    grad_send = (upstream[0].astype(jnp.float32) * token_adv[:, None, None]).astype(jnp.bfloat16)
    key_send = jnp.repeat(key_rotated, group_size, axis=1)
    value_send = jnp.repeat(v_proj[0], group_size, axis=1)
    query_heads = lax.all_to_all(query_send, "seq", split_axis=1, concat_axis=0, tiled=True)
    key_heads, value_heads = (
        lax.all_to_all(key_send, "seq", split_axis=1, concat_axis=0, tiled=True),
        lax.all_to_all(value_send, "seq", split_axis=1, concat_axis=0, tiled=True),
    )
    grad_heads = lax.all_to_all(grad_send, "seq", split_axis=1, concat_axis=0, tiled=True)
    results = [
        head_attention(
            query_heads[:, 0], key_heads[:, 0], value_heads[:, 0], grad_heads[:, 0], table
        )
    ]
    out_heads = jnp.stack([item[0] for item in results], axis=1)
    dq_heads = jnp.stack([item[1] for item in results], axis=1)
    dk_heads = jnp.stack([item[2] for item in results], axis=1)
    dv_heads = jnp.stack([item[3] for item in results], axis=1)
    attn_tokens = lax.all_to_all(out_heads, "seq", split_axis=0, concat_axis=1, tiled=True)
    dq_tokens = lax.all_to_all(dq_heads, "seq", split_axis=0, concat_axis=1, tiled=True)
    dk_tokens, dv_tokens = (
        lax.all_to_all(dk_heads, "seq", split_axis=0, concat_axis=1, tiled=True),
        lax.all_to_all(dv_heads, "seq", split_axis=0, concat_axis=1, tiled=True),
    )
    dk_summed = jnp.sum(dk_tokens.reshape(local_tokens, kv_count, group_size, head_width), axis=2)
    dv_summed = jnp.sum(dv_tokens.reshape(local_tokens, kv_count, group_size, head_width), axis=2)
    dq_inner, dq_gain = q_pull(dq_tokens.astype(jnp.float32))
    dk_inner, dk_gain = k_pull(dk_summed)
    q_total, k_total = lax.psum((dq_gain, dk_gain), ("seq", "dp"))
    return (
        attn_tokens[None],
        dq_inner.astype(jnp.bfloat16)[None],
        dk_inner.astype(jnp.bfloat16)[None],
        dv_summed.astype(jnp.bfloat16)[None],
        q_total,
        k_total,
    )


def solution(mesh):
    return jax.shard_map(
        per_device,
        mesh=mesh,
        in_specs=(
            P("dp", "seq", None, None),
            P("dp", "seq", None, None),
            P("dp", "seq", None, None),
            P("dp", "seq", None, None),
            P("dp", "seq"),
            P("dp", None, None),
            P("dp", None),
            P(),
            P(),
        ),
        out_specs=(
            P("dp", "seq", None, None),
            P("dp", "seq", None, None),
            P("dp", "seq", None, None),
            P("dp", "seq", None, None),
            P(),
            P(),
        ),
        check_vma=False,
    )
```

profile of v0, /device:TPU:1, one launch (start us, length us, event | category | flops | bytes accessed | tf_op | source)
XLA Modules:
  0.0 387.3 jit_solution(8557227053167079491)
XLA Ops:
  7.8 10.1 %all-to-all-start = ((bf16[192,16,128]{2,0,1:T(8,128)(2,1)}), bf16[192,16,128]{2,0,1:T(8,128)(2,1)S(1)}, u32[]{:S(2)}, u32[]{:S(2)}) async-start(bf16[192,16,128]{2,0,1:T(8,128)(2,1)} %fusion.39), calls=%async_computation | async-start | bytes 1572864 | tf_op jit(solution)/shard_map/all_to_all | solution.py:161
  22.0 18.6 %all-to-all-done = bf16[192,16,128]{2,0,1:T(8,128)(2,1)S(1)} async-done(((bf16[192,16,128]{2,0,1:T(8,128)(2,1)}), bf16[192,16,128]{2,0,1:T(8,128)(2,1)S(1)}, u32[]{:S(2)}, u32[]{:S(2)}) %all-to-all-start) | async-done | bytes 786464 | tf_op jit(solution)/shard_map/all_to_all | solution.py:161
  41.8 3.7 all-to-all-start.1
  69.8 7.0 %all-to-all-start.2 = ((bf16[192,16,128]{2,0,1:T(8,128)(2,1)}), bf16[192,16,128]{2,0,1:T(8,128)(2,1)S(1)}, u32[]{:S(2)}, u32[]{:S(2)}) async-start(bf16[192,16,128]{2,0,1:T(8,128)(2,1)} %bitcast.17), calls=%async_computation.2 | async-start | bytes 1572864 | tf_op jit(solution)/shard_map/all_to_all | solution.py:164
  85.4 14.0 %all-to-all-done.2 = bf16[192,16,128]{2,0,1:T(8,128)(2,1)S(1)} async-done(((bf16[192,16,128]{2,0,1:T(8,128)(2,1)}), bf16[192,16,128]{2,0,1:T(8,128)(2,1)S(1)}, u32[]{:S(2)}, u32[]{:S(2)}) %all-to-all-start.2) | async-done | bytes 786464 | tf_op jit(solution)/shard_map/all_to_all | solution.py:164
  99.4 3.5 all-to-all-start.4
  106.1 4.2 %fusion.168 = (f32[512]{0:T(512)S(1)}, f32[512,1408]{1,0:T(8,128)}) fusion(bf16[3072,128]{1,0:T(8,128)(2,1)S(1)} %bitcast.209, bf16[3072,128]{1,0:T(8,128)(2,1)S(1)} %bitcast.220, pred[512,1408]{1,0:T(32,128)(4,1)} %copy.122, pred[512,1408]{1,0:T(32,128)(4,1)} %copy.121, s32[1408]{0:T(1024)S(1)} %get-tuple-element.381), kind=kOutput, calls=%fused_computation.331 | convolution fusion | flops 188874240 | bytes 4827136 | tf_op jit(solution)/shard_map/qd,kd->qk/dot_general | solution.py:72
  112.8 12.4 %all-to-all-done.4 = bf16[192,16,128]{2,0,1:T(8,128)(2,1)S(1)} async-done(((bf16[192,16,128]{2,0,1:T(8,128)(2,1)}), bf16[192,16,128]{2,0,1:T(8,128)(2,1)S(1)}, u32[]{:S(2)}, u32[]{:S(2)}) %all-to-all-start.4) | async-done | bytes 786464 | tf_op jit(solution)/shard_map/all_to_all | solution.py:166
  165.6 3.0 reduce.50
  168.6 3.0 reshape.836
  171.6 4.2 %all-to-all-start.5 = ((bf16[16,2,12288]{2,1,0:T(2,128)(2,1)}), bf16[16,2,12288]{2,1,0:T(2,128)(2,1)}, u32[]{:S(2)}, u32[]{:S(2)}) async-start(bf16[16,2,12288]{2,1,0:T(2,128)(2,1)} %reshape.836), calls=%async_computation.5 | async-start | bytes 1572864 | tf_op jit(solution)/shard_map/all_to_all | solution.py:177
  184.8 3.0 reduce.49
  187.8 2.8 reshape.834
  190.6 7.0 %all-to-all-done.5 = bf16[16,2,12288]{2,1,0:T(2,128)(2,1)} async-done(((bf16[16,2,12288]{2,1,0:T(2,128)(2,1)}), bf16[16,2,12288]{2,1,0:T(2,128)(2,1)}, u32[]{:S(2)}, u32[]{:S(2)}) %all-to-all-start.5) | async-done | bytes 786464 | tf_op jit(solution)/shard_map/all_to_all | solution.py:177
  197.6 4.2 %all-to-all-start.3 = ((bf16[16,2,12288]{2,1,0:T(2,128)(2,1)}), bf16[16,2,12288]{2,1,0:T(2,128)(2,1)}, u32[]{:S(2)}, u32[]{:S(2)}) async-start(bf16[16,2,12288]{2,1,0:T(2,128)(2,1)} %reshape.834), calls=%async_computation.3 | async-start | bytes 1572864 | tf_op jit(solution)/shard_map/all_to_all | solution.py:176
  210.3 13.2 %all-to-all-done.3 = bf16[16,2,12288]{2,1,0:T(2,128)(2,1)} async-done(((bf16[16,2,12288]{2,1,0:T(2,128)(2,1)}), bf16[16,2,12288]{2,1,0:T(2,128)(2,1)}, u32[]{:S(2)}, u32[]{:S(2)}) %all-to-all-start.3) | async-done | bytes 786464 | tf_op jit(solution)/shard_map/all_to_all | solution.py:176
  223.5 3.6 all-to-all-start.6
  237.1 28.1 %all-to-all-done.6 = f32[3072,1,128]{2,1,0:T(1,128)S(1)} async-done(((f32[3072,1,128]{2,1,0:T(1,128)}), f32[3072,1,128]{2,1,0:T(1,128)S(1)}, u32[]{:S(2)}, u32[]{:S(2)}) %all-to-all-start.6) | async-done | bytes 1572896 | tf_op jit(solution)/shard_map/all_to_all | solution.py:179
  265.2 4.6 %all-to-all-start.7 = ((f32[3072,1,128]{2,1,0:T(1,128)}), f32[3072,1,128]{2,1,0:T(1,128)S(1)}, u32[]{:S(2)}, u32[]{:S(2)}) async-start(f32[3072,1,128]{2,1,0:T(1,128)} %bitcast.64), calls=%async_computation.7 | async-start | bytes 3145728 | tf_op jit(solution)/shard_map/all_to_all | solution.py:180
  269.8 5.2 %reshape.837 = bf16[3072,1,128]{2,1,0:T(2,128)(2,1)} reshape(bf16[16,2,12288]{2,1,0:T(2,128)(2,1)} %all-to-all-done.5) | data formatting | bytes 1572864
  275.0 3.2 convert_element_type.211
  284.2 5.2 %reshape.835 = bf16[3072,1,128]{2,1,0:T(2,128)(2,1)} reshape(bf16[16,2,12288]{2,1,0:T(2,128)(2,1)} %all-to-all-done.3) | data formatting | bytes 1572864
  294.4 13.7 %all-to-all-done.7 = f32[3072,1,128]{2,1,0:T(1,128)S(1)} async-done(((f32[3072,1,128]{2,1,0:T(1,128)}), f32[3072,1,128]{2,1,0:T(1,128)S(1)}, u32[]{:S(2)}, u32[]{:S(2)}) %all-to-all-start.7) | async-done | bytes 1572896 | tf_op jit(solution)/shard_map/all_to_all | solution.py:180
  310.6 76.4 %all-reduce.6 = (f32[128]{0:T(128)}, f32[128]{0:T(128)}) all-reduce(f32[128]{0:T(128)S(1)} %copy-done.86, f32[128]{0:T(128)S(1)} %get-tuple-element.320), channel_id=1, replica_groups=mesh['seq'=16,'dp'=16] {'seq','dp'}, use_global_device_ids=true, to_apply=%region_23.24 | all-reduce | flops 256 | bytes 2048 | tf_op jit(solution)/shard_map/psum | solution.py:186
  (389 shorter events, 130.2 us)
Async XLA Ops:
  7.8 12.7 %copy-start.17 = (bf16[1,192,4,128]{3,2,1,0:T(4,128)(2,1)S(1)}, bf16[1,192,4,128]{3,2,1,0:T(4,128)(2,1)}, u32[]{:S(2)}) copy-start(bf16[1,192,4,128]{3,2,1,0:T(4,128)(2,1)} %param.58) | copy-start | bytes 589828
  7.8 13.5 %copy-start.63 = (f32[128]{0:T(128)S(1)}, f32[128]{0:T(128)}, u32[]{:S(2)}) copy-start(f32[128]{0:T(128)} %param.65) | copy-start | bytes 1540
  7.8 32.8 %all-to-all-start = ((bf16[192,16,128]{2,0,1:T(8,128)(2,1)}), bf16[192,16,128]{2,0,1:T(8,128)(2,1)S(1)}, u32[]{:S(2)}, u32[]{:S(2)}) async-start(bf16[192,16,128]{2,0,1:T(8,128)(2,1)} %fusion.39), calls=%async_computation | async-start | bytes 1572864 | tf_op jit(solution)/shard_map/all_to_all | solution.py:161
  40.6 65.5 %copy-start.22 = (bf16[192,16,128]{2,0,1:T(8,128)(2,1)}, bf16[192,16,128]{2,0,1:T(8,128)(2,1)S(1)}, u32[]{:S(2)}) copy-start(bf16[192,16,128]{2,0,1:T(8,128)(2,1)S(1)} %all-to-all-done) | copy-start | bytes 2359300
  41.8 26.6 %all-to-all-start.1 = ((bf16[192,16,128]{2,0,1:T(8,128)(2,1)}), bf16[192,16,128]{2,0,1:T(8,128)(2,1)S(1)}, u32[]{:S(2)}, u32[]{:S(2)}) async-start(bf16[192,16,128]{2,0,1:T(8,128)(2,1)} %bitcast.12), calls=%async_computation.1 | async-start | bytes 1572864 | tf_op jit(solution)/shard_map/all_to_all | solution.py:163
  55.7 3.9 copy-start.77
  57.8 3.9 %copy-start.65 = (s32[4,4]{1,0:T(4,128)S(1)}, s32[4,4]{1,0:T(4,128)}, u32[]{:S(2)}) copy-start(s32[4,4]{1,0:T(4,128)} %get-tuple-element.354) | copy-start | bytes 196
  57.8 3.9 %copy-start.66 = (s32[4,4]{1,0:T(4,128)S(1)}, s32[4,4]{1,0:T(4,128)}, u32[]{:S(2)}) copy-start(s32[4,4]{1,0:T(4,128)} %get-tuple-element.355) | copy-start | bytes 196
  57.8 3.9 %copy-start.67 = (s32[4,7]{1,0:T(4,128)S(1)}, s32[4,7]{1,0:T(4,128)}, u32[]{:S(2)}) copy-start(s32[4,7]{1,0:T(4,128)} %get-tuple-element.358) | copy-start | bytes 340
  57.8 3.9 %copy-start.68 = (s32[4,7]{1,0:T(4,128)S(1)}, s32[4,7]{1,0:T(4,128)}, u32[]{:S(2)}) copy-start(s32[4,7]{1,0:T(4,128)} %get-tuple-element.359) | copy-start | bytes 340
  68.3 62.2 %copy-start.18 = (bf16[192,16,128]{2,0,1:T(8,128)(2,1)}, bf16[192,16,128]{2,0,1:T(8,128)(2,1)S(1)}, u32[]{:S(2)}) copy-start(bf16[192,16,128]{2,0,1:T(8,128)(2,1)S(1)} %all-to-all-done.1) | copy-start | bytes 2359300
  69.8 9.1 %copy-start.87 = (f32[1,5]{1,0:T(1,128)S(1)}, f32[1,5]{1,0:T(1,128)}, u32[]{:S(2)}) copy-start(f32[1,5]{1,0:T(1,128)} %param.63) | copy-start | bytes 64
  69.8 13.3 %copy-start.85 = (s32[1,192]{1,0:T(1,128)S(1)}, s32[1,192]{1,0:T(1,128)}, u32[]{:S(2)}) copy-start(s32[1,192]{1,0:T(1,128)} %param.61) | copy-start | bytes 2308
  69.8 29.7 %all-to-all-start.2 = ((bf16[192,16,128]{2,0,1:T(8,128)(2,1)}), bf16[192,16,128]{2,0,1:T(8,128)(2,1)S(1)}, u32[]{:S(2)}, u32[]{:S(2)}) async-start(bf16[192,16,128]{2,0,1:T(8,128)(2,1)} %bitcast.17), calls=%async_computation.2 | async-start | bytes 1572864 | tf_op jit(solution)/shard_map/all_to_all | solution.py:164
  99.4 26.7 %copy-start.20 = (bf16[192,16,128]{2,0,1:T(8,128)(2,1)}, bf16[192,16,128]{2,0,1:T(8,128)(2,1)S(1)}, u32[]{:S(2)}) copy-start(bf16[192,16,128]{2,0,1:T(8,128)(2,1)S(1)} %all-to-all-done.2) | copy-start | bytes 2359300
  99.4 25.8 %all-to-all-start.4 = ((bf16[192,16,128]{2,0,1:T(8,128)(2,1)}), bf16[192,16,128]{2,0,1:T(8,128)(2,1)S(1)}, u32[]{:S(2)}, u32[]{:S(2)}) async-start(bf16[192,16,128]{2,0,1:T(8,128)(2,1)} %fusion.40), calls=%async_computation.4 | async-start | bytes 1572864 | tf_op jit(solution)/shard_map/all_to_all | solution.py:166
  104.8 5.6 %copy-start.73 = (s32[1408]{0:T(1024)}, s32[1408]{0:T(1024)S(1)}, u32[]{:S(2)}) copy-start(s32[1408]{0:T(1024)S(1)} %get-tuple-element.381) | copy-start | bytes 16900
  171.6 25.9 %all-to-all-start.5 = ((bf16[16,2,12288]{2,1,0:T(2,128)(2,1)}), bf16[16,2,12288]{2,1,0:T(2,128)(2,1)}, u32[]{:S(2)}, u32[]{:S(2)}) async-start(bf16[16,2,12288]{2,1,0:T(2,128)(2,1)} %reshape.836), calls=%async_computation.5 | async-start | bytes 1572864 | tf_op jit(solution)/shard_map/all_to_all | solution.py:177
  197.6 25.9 %all-to-all-start.3 = ((bf16[16,2,12288]{2,1,0:T(2,128)(2,1)}), bf16[16,2,12288]{2,1,0:T(2,128)(2,1)}, u32[]{:S(2)}, u32[]{:S(2)}) async-start(bf16[16,2,12288]{2,1,0:T(2,128)(2,1)} %reshape.834), calls=%async_computation.3 | async-start | bytes 1572864 | tf_op jit(solution)/shard_map/all_to_all | solution.py:176
  223.5 41.6 %all-to-all-start.6 = ((f32[3072,1,128]{2,1,0:T(1,128)}), f32[3072,1,128]{2,1,0:T(1,128)S(1)}, u32[]{:S(2)}, u32[]{:S(2)}) async-start(f32[3072,1,128]{2,1,0:T(1,128)} %bitcast.57), calls=%async_computation.6 | async-start | bytes 3145728 | tf_op jit(solution)/shard_map/all_to_all | solution.py:179
  265.2 42.9 %all-to-all-start.7 = ((f32[3072,1,128]{2,1,0:T(1,128)}), f32[3072,1,128]{2,1,0:T(1,128)S(1)}, u32[]{:S(2)}, u32[]{:S(2)}) async-start(f32[3072,1,128]{2,1,0:T(1,128)} %bitcast.64), calls=%async_computation.7 | async-start | bytes 3145728 | tf_op jit(solution)/shard_map/all_to_all | solution.py:180
  294.2 14.8 %copy-start.21 = (f32[192,4,128]{2,0,1:T(8,128)S(1)}, f32[192,4,128]{2,0,1:T(8,128)}, u32[]{:S(2)}) copy-start(f32[192,4,128]{2,0,1:T(8,128)} %reduce_sum.241) | copy-start | bytes 1179652
  294.2 14.8 %copy-start.60 = (f32[192,4]{0,1:T(4,128)S(1)}, f32[192,4]{0,1:T(4,128)}, u32[]{:S(2)}) copy-start(f32[192,4]{0,1:T(4,128)} %copy-done.59) | copy-start | bytes 9220
  294.2 14.8 %copy-start.64 = (f32[128]{0:T(128)S(1)}, f32[128]{0:T(128)}, u32[]{:S(2)}) copy-start(f32[128]{0:T(128)} %param.65) | copy-start | bytes 1540
  (72 other events, 107.2 us)
where the time goes:
time: 393 us; the launch traced here: 387 us
  waiting for transfers between devices  107 us (27%)
  local copies, waits for them, and re-layouts  79.6 us (20%)
  blocking collectives  76.4 us (19%)
  other arithmetic  41 us (10%)
  starting transfers between devices  40.9 us (10%)
  matrix products  39.2 us (10%)
    psum x1, blocking collectives, per_device(): q_total, k_total = lax.psum((dq_gain, dk_gain), ('seq', 'dp'))  76.4 us
    unnamed x224, local copies, waits for them, and re-layouts  47.7 us
    all_to_all x1, waiting for transfers between devices, per_device(): lax.all_to_all(dk_heads, 'seq', split_axis=0, concat_axis=1, tiled=True)  28.1 us
    eq x24, local copies, waits for them, and re-layouts, block_mask(): return (kinds == 1) | (kinds == 2) & (key_at[None, :] <= query_at[:, None])  21.8 us
    all_to_all x1, waiting for transfers between devices, per_device(): lax.all_to_all(query_send, 'seq', split_axis=1, concat_axis=0, tiled=True)  18.6 us
    all_to_all x1, waiting for transfers between devices, per_device(): lax.all_to_all(value_send, 'seq', split_axis=1, concat_axis=0, tiled=True)  14 us
    all_to_all x1, waiting for transfers between devices, per_device(): lax.all_to_all(dv_heads, 'seq', split_axis=0, concat_axis=1, tiled=True)  13.7 us
    all_to_all x1, waiting for transfers between devices, per_device(): lax.all_to_all(out_heads, 'seq', split_axis=0, concat_axis=1, tiled=True)  13.2 us
  transfers between devices with their start and end apart: 8, of which 7 were waited for; matrix products, arithmetic and copies ran while one was open for 24% of the time, Pallas kernels for 0%

commit v1 on v0

v1 whole, which is shorter than its diff:
```python
import functools
import math

import jax
import jax.numpy as jnp
import numpy as np
from jax import lax
from jax.experimental import pallas as pl
from jax.experimental.pallas import tpu as pltpu
from jax.sharding import PartitionSpec as P

TILE = 128
PROMPT = 4
WINDOW = 5
SPAN = PROMPT + WINDOW
RESPONSES = 5
HEADS = 16
KV = 4
GROUP = HEADS // KV
WIDTH = 128
HALF = 64
EPS = 1e-06
ROPE_BASE = 1000000.0
F32 = jnp.float32
BF16 = jnp.bfloat16


def rope_tables(count):
    freq = np.exp(
        np.arange(WIDTH // 2, dtype=np.float32) * np.float32(-2.0 * math.log(ROPE_BASE) / WIDTH)
    ).astype(np.float32)
    angle = (np.arange(count, dtype=np.float32)[:, None] * freq[None, :]).astype(np.float64)
    cosine, sine = np.cos(angle), np.sin(angle)
    return (
        np.concatenate([cosine, cosine], axis=1).astype(np.float32),
        np.concatenate([-sine, sine], axis=1).astype(np.float32),
    )


def swap_halves(x):
    return pltpu.roll(x, WIDTH // 2, 1)


def mean_lanes(x):
    return jnp.sum(x, axis=1, keepdims=True) * (1.0 / WIDTH)


def rows_to_eight(x):
    return jnp.sum(x.reshape(-1, 8, WIDTH), axis=0)


def attention_kernel(
    blocks,
    tile_count,
    tiles_ref,
    rewards_ref,
    seg_ref,
    qgain_ref,
    kgain_ref,
    cos_ref,
    sin_ref,
    q_ref,
    up_ref,
    kv_hbm,
    out_ref,
    dq_ref,
    gains_ref,
    dkv_hbm,
    table,
    kvb,
    xkv,
    ykv,
    xq,
    xu,
    os_,
    dqs,
    kr,
    kt,
    vr,
    vt,
    dk,
    dv,
    ebuf,
    pbuf,
    qsum,
    ksum,
    zeros,
    in_sem,
    out_sem,
):
    me = lax.axis_index("seq")
    first_tile = (blocks * me) // 2
    wb = jnp.clip(first_tile - 3, PROMPT, tile_count - WINDOW)
    load_prompt = pltpu.make_async_copy(
        kv_hbm.at[pl.ds(0, PROMPT * TILE)], kvb.at[pl.ds(0, PROMPT * TILE)], in_sem.at[0]
    )
    load_window = pltpu.make_async_copy(
        kv_hbm.at[pl.ds(wb * TILE, WINDOW * TILE)],
        kvb.at[pl.ds(PROMPT * TILE, WINDOW * TILE)],
        in_sem.at[1],
    )
    load_prompt.start()
    load_window.start()

    zeros[...] = jnp.zeros_like(zeros)

    def zero_copy(tile):
        return pltpu.make_async_copy(
            zeros, dkv_hbm.at[pl.ds(tile * TILE, TILE)], out_sem.at[2 + tile]
        )

    for tile in range(PROMPT, tile_count):

        @pl.when((tile < wb) | (tile >= wb + WINDOW))
        def _(tile=tile):
            zero_copy(tile).start()

    def clear(at, carry):
        table[at] = 0
        return carry

    lax.fori_loop(0, tile_count * tile_count, clear, 0)

    def fill(at, carry):
        slot = tiles_ref[3 * at] * tile_count + tiles_ref[3 * at + 1]
        table[slot] = table[slot] + tiles_ref[3 * at + 2]
        return carry

    lax.fori_loop(0, tiles_ref.shape[0] // 3, fill, 0)

    def place_tile(a):
        def look(b, found):
            hit = table[a * tile_count + tile_count - 1 - b] > 0
            return jnp.where(hit, tile_count - 1 - b, found)

        found = lax.fori_loop(0, tile_count - PROMPT, look, tile_count)
        inside = (a >= PROMPT) & (found < tile_count)
        return jnp.minimum(jnp.where(inside, PROMPT + a - found, a), 2 * PROMPT - 1)

    key_place = [tile * TILE for tile in range(PROMPT)]
    key_place += [pl.multiple_of(place_tile(wb + j) * TILE, TILE) for j in range(WINDOW)]

    xq[...] = q_ref[...].astype(F32).reshape(xq.shape)
    xu[...] = up_ref[...].astype(F32).reshape(xu.shape)
    qgain = qgain_ref[...]
    kgain = kgain_ref[...]
    qsum[...] = jnp.zeros_like(qsum)
    ksum[...] = jnp.zeros_like(ksum)

    reward = [rewards_ref[r] for r in range(RESPONSES)]
    centre = (reward[0] + reward[1] + reward[2] + reward[3] + reward[4]) * (1.0 / RESPONSES)
    seg = seg_ref[...]
    adv_row = jnp.zeros(seg.shape, F32)
    for r in range(RESPONSES):
        adv_row = adv_row + jnp.where(seg == r + 1, reward[r] - centre, 0.0)

    load_prompt.wait()
    load_window.wait()

    def widen(tile, carry):
        rows = kvb[pl.ds(tile * TILE, TILE)].astype(F32).reshape(TILE * 2 * KV, WIDTH)
        xkv[pl.ds(pl.multiple_of(tile * TILE * 2 * KV, TILE * 2 * KV), TILE * 2 * KV), :] = rows
        return carry

    lax.fori_loop(0, SPAN, widen, 0)

    scale = 1.0 / math.sqrt(WIDTH)
    key_at = lax.broadcasted_iota(jnp.int32, (TILE, GROUP * HALF), 0)
    lane = lax.broadcasted_iota(jnp.int32, (1, GROUP * HALF), 1)

    def per_kv(g, carry):
        for tile in range(SPAN):
            x = xkv[pl.ds(tile * TILE * 2 * KV + g, TILE, stride=2 * KV), :]
            factor = lax.rsqrt(mean_lanes(x * x) + EPS)
            normed = x * factor * kgain
            cosine = cos_ref[pl.ds(key_place[tile], TILE), :]
            sine = sin_ref[pl.ds(key_place[tile], TILE), :]
            turned = normed * cosine + swap_halves(normed) * sine
            kr[tile] = turned.astype(BF16)
            kt[tile] = turned.T.astype(BF16)
            value = xkv[pl.ds(tile * TILE * 2 * KV + KV + g, TILE, stride=2 * KV), :]
            vr[tile] = value.astype(BF16)
            vt[tile] = value.T.astype(BF16)
        dk[...] = jnp.zeros_like(dk)
        dv[...] = jnp.zeros_like(dv)
        for i in range(blocks):
            block = blocks * me + i
            a = block // 2
            half = lax.rem(block, 2) * HALF
            off = jnp.maximum(a - 3 - wb, 0)
            starts = [0, 2, PROMPT + off, PROMPT + off + 2]
            names = [0, 2, wb + off, wb + off + 2]
            place = pl.multiple_of(place_tile(a) * TILE + half, HALF)
            cosine = jnp.concatenate([cos_ref[pl.ds(place, HALF), :]] * GROUP, axis=0)
            sine = jnp.concatenate([sin_ref[pl.ds(place, HALF), :]] * GROUP, axis=0)

            def rows(ref):
                return jnp.concatenate(
                    [
                        ref[pl.ds(i * HALF * HEADS + GROUP * g + h, HALF, stride=HEADS), :]
                        for h in range(GROUP)
                    ],
                    axis=0,
                )

            x = rows(xq)
            factor = lax.rsqrt(mean_lanes(x * x) + EPS)
            unit = x * factor
            normed = unit * qgain
            turned = normed * cosine + swap_halves(normed) * sine
            query = turned.astype(BF16)
            query_t = turned.T.astype(BF16)
            adv = jnp.concatenate([adv_row[:, i * HALF : (i + 1) * HALF]] * GROUP, axis=1)
            grad_f = rows(xu).T * adv
            grad_t = grad_f.astype(BF16)
            grad = grad_f.T.astype(BF16)

            slot = half + lax.rem(lane, HALF)
            total = jnp.zeros((1, GROUP * HALF), F32)
            for c in range(4):
                score = jnp.dot(
                    kr[pl.ds(starts[c], 2)].reshape(2 * TILE, WIDTH),
                    query_t,
                    preferred_element_type=F32,
                )
                for t in range(2):
                    kind = table[a * tile_count + names[c] + t]
                    one = (kind == 1).astype(jnp.int32)
                    two = (kind == 2).astype(jnp.int32)
                    limit = two * slot + (one * (TILE + 1) - 1 + two)
                    raw = jnp.where(
                        key_at <= limit,
                        jnp.exp2(score[t * TILE : (t + 1) * TILE] * (scale * math.log2(math.e))),
                        0.0,
                    )
                    ebuf[c, t * TILE : (t + 1) * TILE] = raw
                    total = total + jnp.sum(raw, axis=0, keepdims=True)
            share = jnp.where(total > 0, 1.0 / total, 0.0)
            out_t = jnp.zeros((WIDTH, GROUP * HALF), F32)
            for c in range(4):
                weights = (ebuf[c] * share).astype(BF16)
                pbuf[c] = weights
                value_t = jnp.concatenate([vt[starts[c]], vt[starts[c] + 1]], axis=1)
                out_t = out_t + jnp.dot(value_t, weights, preferred_element_type=F32)
            delta = jnp.sum(grad_t.astype(F32) * out_t, axis=0, keepdims=True)
            dq_t = jnp.zeros((WIDTH, GROUP * HALF), F32)
            for c in range(4):
                dweights = jnp.dot(
                    vr[pl.ds(starts[c], 2)].reshape(2 * TILE, WIDTH),
                    grad_t,
                    preferred_element_type=F32,
                )
                weights = pbuf[c]
                ds = (weights.astype(F32) * ((dweights - delta) * scale)).astype(BF16)
                key_t = jnp.concatenate([kt[starts[c]], kt[starts[c] + 1]], axis=1)
                dq_t = dq_t + jnp.dot(key_t, ds, preferred_element_type=F32)
                dk_c = jnp.dot(ds, query, preferred_element_type=F32)
                dv_c = jnp.dot(weights, grad, preferred_element_type=F32)
                dk[pl.ds(starts[c], 2)] += dk_c.reshape(2, TILE, WIDTH)
                dv[pl.ds(starts[c], 2)] += dv_c.reshape(2, TILE, WIDTH)

            dturned = dq_t.T.astype(BF16).astype(F32)
            dnormed = dturned * cosine - swap_halves(dturned) * sine
            qsum[...] += rows_to_eight(dnormed * unit)
            dunit = dnormed * qgain
            dx = factor * (dunit - unit * mean_lanes(dunit * unit))
            out = out_t.T
            for h in range(GROUP):
                spot = pl.ds(i * HALF * HEADS + GROUP * g + h, HALF, stride=HEADS)
                os_[spot, :] = out[h * HALF : (h + 1) * HALF]
                dqs[spot, :] = dx[h * HALF : (h + 1) * HALF]

        for tile in range(SPAN):
            x = xkv[pl.ds(tile * TILE * 2 * KV + g, TILE, stride=2 * KV), :]
            factor = lax.rsqrt(mean_lanes(x * x) + EPS)
            unit = x * factor
            cosine = cos_ref[pl.ds(key_place[tile], TILE), :]
            sine = sin_ref[pl.ds(key_place[tile], TILE), :]
            dturned = dk[tile]
            dnormed = dturned * cosine - swap_halves(dturned) * sine
            ksum[...] += rows_to_eight(dnormed * unit)
            dunit = dnormed * kgain
            dx = factor * (dunit - unit * mean_lanes(dunit * unit))
            ykv[pl.ds(tile * TILE * 2 * KV + g, TILE, stride=2 * KV), :] = dx
            ykv[pl.ds(tile * TILE * 2 * KV + KV + g, TILE, stride=2 * KV), :] = dv[tile]
        return carry

    lax.fori_loop(0, KV, per_kv, 0)

    def narrow(tile, carry):
        at = pl.multiple_of(tile * TILE * 2 * KV, TILE * 2 * KV)
        rows = ykv[pl.ds(at, TILE * 2 * KV), :]
        kvb[pl.ds(tile * TILE, TILE)] = rows.reshape(TILE, 2 * KV, WIDTH).astype(BF16)
        return carry

    lax.fori_loop(0, SPAN, narrow, 0)
    store_prompt = pltpu.make_async_copy(
        kvb.at[pl.ds(0, PROMPT * TILE)], dkv_hbm.at[pl.ds(0, PROMPT * TILE)], out_sem.at[0]
    )
    store_window = pltpu.make_async_copy(
        kvb.at[pl.ds(PROMPT * TILE, WINDOW * TILE)],
        dkv_hbm.at[pl.ds(wb * TILE, WINDOW * TILE)],
        out_sem.at[1],
    )
    store_prompt.start()
    store_window.start()
    out_ref[...] = os_[...].reshape(out_ref.shape).astype(BF16)
    dq_ref[...] = dqs[...].reshape(dq_ref.shape).astype(BF16)
    gains_ref[0:1, :] = jnp.sum(qsum[...], axis=0, keepdims=True)
    gains_ref[1:2, :] = jnp.sum(ksum[...], axis=0, keepdims=True)
    for tile in range(PROMPT, tile_count):

        @pl.when((tile < wb) | (tile >= wb + WINDOW))
        def _(tile=tile):
            zero_copy(tile).wait()

    store_prompt.wait()
    store_window.wait()


def attend(tiles, rewards, seg, qgain, kgain, q, up, kv):
    local = q.shape[0]
    seq_len = kv.shape[0]
    blocks = local // HALF
    tile_count = seq_len // TILE
    cosine, sine = rope_tables(2 * PROMPT * TILE)
    vmem = pl.BlockSpec(memory_space=pltpu.VMEM)
    smem = pl.BlockSpec(memory_space=pltpu.SMEM)
    hbm = pl.BlockSpec(memory_space=pl.ANY)
    rows = local * HEADS
    span_rows = SPAN * TILE * 2 * KV
    cols = GROUP * HALF
    return pl.pallas_call(
        functools.partial(attention_kernel, blocks, tile_count),
        out_shape=(
            jax.ShapeDtypeStruct(q.shape, BF16),
            jax.ShapeDtypeStruct(q.shape, BF16),
            jax.ShapeDtypeStruct((2, WIDTH), F32),
            jax.ShapeDtypeStruct(kv.shape, BF16),
        ),
        in_specs=[smem, smem, vmem, vmem, vmem, vmem, vmem, vmem, vmem, hbm],
        out_specs=(vmem, vmem, vmem, hbm),
        scratch_shapes=[
            pltpu.SMEM((tile_count * tile_count,), jnp.int32),
            pltpu.VMEM((SPAN * TILE, 2 * KV, WIDTH), BF16),
            pltpu.VMEM((span_rows, WIDTH), F32),
            pltpu.VMEM((span_rows, WIDTH), F32),
            pltpu.VMEM((rows, WIDTH), F32),
            pltpu.VMEM((rows, WIDTH), F32),
            pltpu.VMEM((rows, WIDTH), F32),
            pltpu.VMEM((rows, WIDTH), F32),
            pltpu.VMEM((SPAN, TILE, WIDTH), BF16),
            pltpu.VMEM((SPAN, TILE, WIDTH), BF16),
            pltpu.VMEM((SPAN, TILE, WIDTH), BF16),
            pltpu.VMEM((SPAN, TILE, WIDTH), BF16),
            pltpu.VMEM((SPAN, TILE, WIDTH), F32),
            pltpu.VMEM((SPAN, TILE, WIDTH), F32),
            pltpu.VMEM((4, 2 * TILE, cols), F32),
            pltpu.VMEM((4, 2 * TILE, cols), BF16),
            pltpu.VMEM((8, WIDTH), F32),
            pltpu.VMEM((8, WIDTH), F32),
            pltpu.VMEM((TILE, 2 * KV, WIDTH), BF16),
            pltpu.SemaphoreType.DMA((2,)),
            pltpu.SemaphoreType.DMA((2 + tile_count,)),
        ],
        compiler_params=pltpu.CompilerParams(vmem_limit_bytes=48 * 1024 * 1024),
        name="tree_attention",
    )(tiles, rewards, seg, qgain, kgain, jnp.asarray(cosine), jnp.asarray(sine), q, up, kv)


def butterfly_sum(x, axis):
    size = lax.axis_size(axis)
    step = 1
    while step < size:
        x = x + lax.ppermute(x, axis, [(i, i ^ step) for i in range(size)])
        step *= 2
    return x


def per_device(q_proj, k_proj, v_proj, upstream, segment_ids, tree_tiles, rewards, q_gain, k_gain):
    kv = jnp.concatenate([k_proj[0], v_proj[0]], axis=1)
    kv_all = lax.all_gather(kv, "seq", tiled=True)
    out, dq, gains, dkv = attend(
        tree_tiles.reshape(-1),
        rewards[0],
        segment_ids,
        q_gain[None],
        k_gain[None],
        q_proj[0],
        upstream[0],
        kv_all,
    )
    gains = butterfly_sum(butterfly_sum(gains, "dp"), "seq")
    dkv = lax.psum_scatter(dkv, "seq", tiled=True)
    return (out[None], dq[None], dkv[None, :, :KV], dkv[None, :, KV:], gains[0], gains[1])


def solution(mesh):
    whole = P("dp", "seq", None, None)
    return jax.shard_map(
        per_device,
        mesh=mesh,
        in_specs=(whole, whole, whole, whole, P("dp", "seq"), P("dp", None, None), P("dp", None), P(), P()),
        out_specs=(whole, whole, whole, whole, P(), P()),
        check_vma=False,
    )
```

time: 393 us -> 185 us (0.47)
  blocking collectives: 76.4 us -> 0 us
  local copies, waits for them, and re-layouts: 79.6 us -> 10.5 us
  Pallas kernels: 0 us -> 44.2 us
  matrix products: 39.2 us -> 0 us
  other arithmetic: 41 us -> 2 us
  starting transfers between devices: 40.9 us -> 18.4 us
  waiting for transfers between devices: 107 us -> 93.6 us
  between operations: 3.17 us -> 14.1 us
    all_to_all x8 -> x0, waiting for transfers between devices: 107 us -> none  [the longest x1 28.1 us: per_device(): lax.all_to_all(dk_heads, 'seq', split_axis=0, concat_axis=1, tiled=True)]
    psum x1 -> x0, blocking collectives: 76.4 us -> none  [per_device(): q_total, k_total = lax.psum((dq_gain, dk_gain), ('seq', 'dp'))]
    all_gather x0 -> x1, waiting for transfers between devices: none -> 50.4 us  [per_device(): kv_all = lax.all_gather(kv, 'seq', tiled=True)]
    pallas_call x0 -> x1, Pallas kernels: none -> 44.2 us  [attend(): pl.pallas_call(functools.partial(attention_kernel, blocks, tile_count), o...]
    all_to_all x8 -> x0, starting transfers between devices: 40.9 us -> none  [the longest x1 10.1 us: per_device(): lax.all_to_all(query_send, 'seq', split_axis=1, concat_axis=0, tiled=True)]
    unnamed x224 -> x17, local copies, waits for them, and re-layouts: 47.7 us -> 7.77 us
    dot_general x37 -> x0, matrix products: 39.2 us -> none  [the longest x6 11.3 us: block_step(): jnp.einsum('qd,kd->qk', query_rows, key_rows, preferred_element_type=jnp....]
    reduce_scatter x0 -> x1, waiting for transfers between devices: none -> 30.4 us  [per_device(): dkv = lax.psum_scatter(dkv, 'seq', tiled=True)]
  transfers between devices with their start and end apart: 8 -> 10, of which waited for: 7 -> 10; matrix products, arithmetic and copies ran while one was open for 24% -> 1% of each run, Pallas kernels for 0% -> 0%
where the time goes in v1:
time: 185 us; the launch traced here: 183 us
  waiting for transfers between devices  93.6 us (51%)
  Pallas kernels  44.2 us (24%)
  starting transfers between devices  18.4 us (10%)
  between operations  14.1 us (8%)
  local copies, waits for them, and re-layouts  10.5 us (6%)
  other arithmetic  2 us (1%)
    all_gather x1, waiting for transfers between devices, per_device(): kv_all = lax.all_gather(kv, 'seq', tiled=True)  50.4 us
    pallas_call x1, Pallas kernels, attend(): pl.pallas_call(functools.partial(attention_kernel, blocks, tile_count), o...  44.2 us
    reduce_scatter x1, waiting for transfers between devices, per_device(): dkv = lax.psum_scatter(dkv, 'seq', tiled=True)  30.4 us
    ppermute x8, starting transfers between devices, butterfly_sum(): x = x + lax.ppermute(x, axis, [(i, i ^ step) for i in range(size)])  18.3 us
    ppermute x8, waiting for transfers between devices, butterfly_sum(): x = x + lax.ppermute(x, axis, [(i, i ^ step) for i in range(size)])  12.8 us
    unnamed x17, local copies, waits for them, and re-layouts  7.77 us
  transfers between devices with their start and end apart: 10, of which 10 were waited for; matrix products, arithmetic and copies ran while one was open for 1% of the time, Pallas kernels for 0%

profile of v1, /device:TPU:1, one launch (start us, length us, event | category | flops | bytes accessed | tf_op | source)
XLA Modules:
  0.0 182.9 jit_solution(12846967061971151040)
XLA Ops:
  7.2 2.0 %pad_maximum_fusion = bf16[192,8,128]{2,1,0:T(8,128)(2,1)} fusion(bf16[192,4,128]{2,1,0:T(4,128)(2,1)} %bitcast.22, bf16[192,4,128]{2,1,0:T(4,128)(2,1)} %bitcast.23), kind=kLoop, calls=%fused_computation | loop fusion | flops 786432 | bytes 786432 | tf_op jit(solution)/shard_map/concatenate | solution.py:381
  10.3 50.4 %all-gather.2.cloned.1.call-done.kv_hbm = bf16[3072,8,128]{2,1,0:T(8,128)(2,1)} async-done(((bf16[192,8,128]{2,1,0:T(8,128)(2,1)}), bf16[3072,8,128]{2,1,0:T(8,128)(2,1)}) %all-gather.2.cloned.1.call-update) | async-done | bytes 6291472 | tf_op jit(solution)/shard_map/all_gather | solution.py:382
  60.7 1.1 copy-done
  61.8 1.1 copy-done.1
  63.0 1.0 copy-done.2
  64.0 1.0 copy-done.3
  67.7 44.2 %tree_attention.1 = (bf16[192,16,128]{2,1,0:T(8,128)(2,1)}, bf16[192,16,128]{2,1,0:T(8,128)(2,1)}, f32[2,128]{1,0:T(2,128)S(1)}, bf16[3072,8,128]{2,1,0:T(8,128)(2,1)}) custom-call(s32[420]{0:T(512)S(1)} %reshape.15.tiles_ref, f32[5]{0:T(128)S(1)} %bitcast.19, s32[1,192]{1,0:T(1,128)S(1)} %copy-done.4, f32[1,128]{1,0:T(1,128)S(1)} %bitcast.20, ...), custom_call_target="tpu_custom_call" | custom-call | tf_op jit(solution)/shard_map/tree_attention/pallas_call | solution.py:333
  112.0 1.3 collective-permute-start
  113.3 1.2 collective-permute-done
  114.5 2.7 %collective-permute-start.1 = (f32[2,128]{1,0:T(2,128)S(1)}, f32[2,128]{1,0:T(2,128)S(1)}, u32[]{:S(2)}, u32[]{:S(2)}) collective-permute-start(f32[2,128]{1,0:T(2,128)S(1)} %add.26), channel_id=1, source_target_pairs={{0,2},{1,3},{2,0},{3,1},{4,6},{5,7},{6,4},{7,5},{8,10},{9,11},{10,... | collective-permute-start | bytes 3080 | tf_op jit(solution)/shard_map/ppermute | solution.py:375
  117.2 1.2 collective-permute-done.1
  118.4 1.2 collective-permute-start.2
  119.6 1.2 collective-permute-done.2
  120.8 2.7 %collective-permute-start.3 = (f32[2,128]{1,0:T(2,128)S(1)}, f32[2,128]{1,0:T(2,128)S(1)}, u32[]{:S(2)}, u32[]{:S(2)}) collective-permute-start(f32[2,128]{1,0:T(2,128)S(1)} %add.28), channel_id=1, source_target_pairs={{0,8},{1,9},{2,10},{3,11},{4,12},{5,13},{6,14},{7,15},{8,0},{9,1},... | collective-permute-start | bytes 3080 | tf_op jit(solution)/shard_map/ppermute | solution.py:375
  123.5 1.2 collective-permute-done.3
  124.8 4.9 %collective-permute-start.4 = (f32[2,128]{1,0:T(2,128)S(1)}, f32[2,128]{1,0:T(2,128)S(1)}, u32[]{:S(2)}, u32[]{:S(2)}) collective-permute-start(f32[2,128]{1,0:T(2,128)S(1)} %add.29), channel_id=1, source_target_pairs={{0,16},{16,0},{32,48},{48,32},{64,80},{80,64},{96,112},{112,96},{1... | collective-permute-start | bytes 3080 | tf_op jit(solution)/shard_map/ppermute | solution.py:375
  130.4 0.9 collective-permute-start.5
  131.3 1.9 %collective-permute-done.5 = f32[2,128]{1,0:T(2,128)S(1)} collective-permute-done((f32[2,128]{1,0:T(2,128)S(1)}, f32[2,128]{1,0:T(2,128)S(1)}, u32[]{:S(2)}, u32[]{:S(2)}) %collective-permute-start.5) | collective-permute-done | bytes 1056 | tf_op jit(solution)/shard_map/ppermute | solution.py:375
  133.3 1.6 collective-permute-start.6
  134.9 1.8 %collective-permute-done.6 = f32[2,128]{1,0:T(2,128)S(1)} collective-permute-done((f32[2,128]{1,0:T(2,128)S(1)}, f32[2,128]{1,0:T(2,128)S(1)}, u32[]{:S(2)}, u32[]{:S(2)}) %collective-permute-start.6) | collective-permute-done | bytes 1056 | tf_op jit(solution)/shard_map/ppermute | solution.py:375
  136.7 3.0 %collective-permute-start.7 = (f32[2,128]{1,0:T(2,128)S(1)}, f32[2,128]{1,0:T(2,128)S(1)}, u32[]{:S(2)}, u32[]{:S(2)}) collective-permute-start(f32[2,128]{1,0:T(2,128)S(1)} %add.32), channel_id=1, source_target_pairs={{0,128},{16,144},{32,160},{48,176},{64,192},{80,208},{96,224},{112... | collective-permute-start | bytes 3080 | tf_op jit(solution)/shard_map/ppermute | solution.py:375
  139.7 3.3 %collective-permute-done.7 = f32[2,128]{1,0:T(2,128)S(1)} collective-permute-done((f32[2,128]{1,0:T(2,128)S(1)}, f32[2,128]{1,0:T(2,128)S(1)}, u32[]{:S(2)}, u32[]{:S(2)}) %collective-permute-start.7) | collective-permute-done | bytes 1056 | tf_op jit(solution)/shard_map/ppermute | solution.py:375
  143.6 30.4 %reduce-scatter.2.cloned.1.call-done = bf16[192,8,128]{2,1,0:T(8,128)(2,1)} async-done(((bf16[3072,8,128]{2,1,0:T(8,128)(2,1)}), bf16[192,8,128]{2,1,0:T(8,128)(2,1)}) %reduce-scatter.2.cloned.1.call-update) | async-done | bytes 393232 | tf_op jit(solution)/shard_map/reduce_scatter | solution.py:394
  174.0 2.0 %slice_bitcast_fusion = (bf16[1,192,4,128]{3,2,1,0:T(4,128)(2,1)}, bf16[1,192,4,128]{3,2,1,0:T(4,128)(2,1)}) fusion(bf16[192,8,128]{2,1,0:T(8,128)(2,1)} %reduce-scatter.2.cloned.1.call-done), kind=kLoop, calls=%fused_computation.1 | loop fusion | bytes 786432 | tf_op jit(solution)/shard_map/broadcast_in_dim | solution.py:395
  (28 shorter events, 5.1 us)
Async XLA Ops:
  7.2 53.5 %all-gather.2.cloned.1.call-start = ((), (), s32[]{:S(2)}) async-start(), calls=%async_computation.1 | async-start | bytes 6684672 | tf_op jit(solution)/shard_map/all_gather | solution.py:382
  9.2 164.8 %reduce-scatter.2.cloned.1.call-start = ((), (), s32[]{:S(2)}) async-start(), calls=%async_computation.2 | async-start | bytes 6684672 | tf_op jit(solution)/shard_map/reduce_scatter | solution.py:394
  60.7 1.1 copy-start
  61.8 1.1 copy-start.1
  63.0 1.0 copy-start.2
  64.0 1.0 copy-start.3
  65.0 0.7 copy-start.4
  65.7 0.7 copy-start.5
  66.4 0.7 copy-start.6
  67.0 0.7 copy-start.7
  112.0 2.5 %collective-permute-start = (f32[2,128]{1,0:T(2,128)S(1)}, f32[2,128]{1,0:T(2,128)S(1)}, u32[]{:S(2)}, u32[]{:S(2)}) collective-permute-start(f32[2,128]{1,0:T(2,128)S(1)} %get-tuple-element.13), channel_id=1, source_target_pairs={{0,1},{1,0},{2,3},{3,2},{4,5},{5,4},{6,7},{7,6},{8,9},{9,8},{10,11... | collective-permute-start | bytes 3080 | tf_op jit(solution)/shard_map/ppermute | solution.py:375
  114.5 3.9 %collective-permute-start.1 = (f32[2,128]{1,0:T(2,128)S(1)}, f32[2,128]{1,0:T(2,128)S(1)}, u32[]{:S(2)}, u32[]{:S(2)}) collective-permute-start(f32[2,128]{1,0:T(2,128)S(1)} %add.26), channel_id=1, source_target_pairs={{0,2},{1,3},{2,0},{3,1},{4,6},{5,7},{6,4},{7,5},{8,10},{9,11},{10,... | collective-permute-start | bytes 3080 | tf_op jit(solution)/shard_map/ppermute | solution.py:375
  118.4 2.4 %collective-permute-start.2 = (f32[2,128]{1,0:T(2,128)S(1)}, f32[2,128]{1,0:T(2,128)S(1)}, u32[]{:S(2)}, u32[]{:S(2)}) collective-permute-start(f32[2,128]{1,0:T(2,128)S(1)} %add.27), channel_id=1, source_target_pairs={{0,4},{1,5},{2,6},{3,7},{4,0},{5,1},{6,2},{7,3},{8,12},{9,13},{10,... | collective-permute-start | bytes 3080 | tf_op jit(solution)/shard_map/ppermute | solution.py:375
  120.8 3.9 %collective-permute-start.3 = (f32[2,128]{1,0:T(2,128)S(1)}, f32[2,128]{1,0:T(2,128)S(1)}, u32[]{:S(2)}, u32[]{:S(2)}) collective-permute-start(f32[2,128]{1,0:T(2,128)S(1)} %add.28), channel_id=1, source_target_pairs={{0,8},{1,9},{2,10},{3,11},{4,12},{5,13},{6,14},{7,15},{8,0},{9,1},... | collective-permute-start | bytes 3080 | tf_op jit(solution)/shard_map/ppermute | solution.py:375
  124.8 5.7 %collective-permute-start.4 = (f32[2,128]{1,0:T(2,128)S(1)}, f32[2,128]{1,0:T(2,128)S(1)}, u32[]{:S(2)}, u32[]{:S(2)}) collective-permute-start(f32[2,128]{1,0:T(2,128)S(1)} %add.29), channel_id=1, source_target_pairs={{0,16},{16,0},{32,48},{48,32},{64,80},{80,64},{96,112},{112,96},{1... | collective-permute-start | bytes 3080 | tf_op jit(solution)/shard_map/ppermute | solution.py:375
  130.4 2.8 %collective-permute-start.5 = (f32[2,128]{1,0:T(2,128)S(1)}, f32[2,128]{1,0:T(2,128)S(1)}, u32[]{:S(2)}, u32[]{:S(2)}) collective-permute-start(f32[2,128]{1,0:T(2,128)S(1)} %add.30), channel_id=1, source_target_pairs={{0,32},{16,48},{32,0},{48,16},{64,96},{80,112},{96,64},{112,80},{1... | collective-permute-start | bytes 3080 | tf_op jit(solution)/shard_map/ppermute | solution.py:375
  133.3 3.5 %collective-permute-start.6 = (f32[2,128]{1,0:T(2,128)S(1)}, f32[2,128]{1,0:T(2,128)S(1)}, u32[]{:S(2)}, u32[]{:S(2)}) collective-permute-start(f32[2,128]{1,0:T(2,128)S(1)} %add.31), channel_id=1, source_target_pairs={{0,64},{16,80},{32,96},{48,112},{64,0},{80,16},{96,32},{112,48},{1... | collective-permute-start | bytes 3080 | tf_op jit(solution)/shard_map/ppermute | solution.py:375
  136.7 6.3 %collective-permute-start.7 = (f32[2,128]{1,0:T(2,128)S(1)}, f32[2,128]{1,0:T(2,128)S(1)}, u32[]{:S(2)}, u32[]{:S(2)}) collective-permute-start(f32[2,128]{1,0:T(2,128)S(1)} %add.32), channel_id=1, source_target_pairs={{0,128},{16,144},{32,160},{48,176},{64,192},{80,208},{96,224},{112... | collective-permute-start | bytes 3080 | tf_op jit(solution)/shard_map/ppermute | solution.py:375
Sparse Core Ops, SparseCore 0:
  10.4 50.2 all-gather.1
  112.1 61.8 reduce-scatter.1

commit v2 on v0

v2 whole, which is shorter than its diff:
```python
import functools
import math

import jax
import jax.numpy as jnp
import numpy as np
from jax import lax
from jax.experimental import pallas as pl
from jax.experimental.pallas import tpu as pltpu
from jax.sharding import PartitionSpec as P

TILE = 128
PROMPT = 4
WINDOW = 5
SPAN = PROMPT + WINDOW
RESPONSES = 5
HEADS = 16
KV = 4
GROUP = HEADS // KV
WIDTH = 128
HALF = 64
BLOCKS = 3
COLS = GROUP * HALF
ALL = BLOCKS * COLS
LOCAL = BLOCKS * HALF
PAIR = 2 * KV
EPS = 1e-06
ROPE_BASE = 1000000.0
F32 = jnp.float32
BF16 = jnp.bfloat16
VMEM = pl.BlockSpec(memory_space=pltpu.VMEM)
SMEM = pl.BlockSpec(memory_space=pltpu.SMEM)
HBM = pl.BlockSpec(memory_space=pltpu.HBM)


def rope_tables(count):
    freq = np.exp(
        np.arange(WIDTH // 2, dtype=np.float32) * np.float32(-2.0 * math.log(ROPE_BASE) / WIDTH)
    ).astype(np.float32)
    angle = (np.arange(count, dtype=np.float32)[:, None] * freq[None, :]).astype(np.float64)
    cosine, sine = np.cos(angle), np.sin(angle)
    return (
        np.concatenate([cosine, cosine], axis=1).astype(np.float32),
        np.concatenate([-sine, sine], axis=1).astype(np.float32),
    )


def swap_halves(x):
    return pltpu.roll(x, WIDTH // 2, 1)


def mean_lanes(x):
    return jnp.sum(x, axis=1, keepdims=True) * (1.0 / WIDTH)


def rows_to_eight(x):
    return jnp.sum(x.reshape(-1, 8, WIDTH), axis=0)


def head_rows(i, g, h):
    return pl.ds(i * HALF * HEADS + GROUP * g + h, HALF, stride=HEADS)


def swap_rows(x):
    return jnp.concatenate([x[WIDTH // 2 :], x[: WIDTH // 2]], axis=0)


def mean_rows(x):
    return jnp.sum(x, axis=0, keepdims=True) * (1.0 / WIDTH)


def pack_kernel(k_hbm, v_hbm, kv_hbm, *rest):
    targets, (k_ref, v_ref, flat, kv_ref, in_sem, out_sem) = rest[:-6], rest[-6:]
    loads = [
        pltpu.make_async_copy(k_hbm, k_ref, in_sem.at[0]),
        pltpu.make_async_copy(v_hbm, v_ref, in_sem.at[1]),
    ]
    for load in loads:
        load.start()
    for n, ref in enumerate((k_ref, v_ref)):
        loads[n].wait()
        flat[...] = ref[...].astype(F32).reshape(flat.shape)
        for g in range(KV):
            kv_ref[n * KV + g] = flat[pl.ds(g, LOCAL, stride=KV), :].astype(BF16)
    stores = [pltpu.make_async_copy(kv_ref, kv_hbm, out_sem.at[0])]
    for b, target in enumerate(targets):
        size = target.shape[1]
        stores.append(
            pltpu.make_async_copy(kv_ref.at[:, pl.ds(b * size, size), :], target, out_sem.at[1 + b])
        )
    for store in stores:
        store.start()
    for store in stores:
        store.wait()


def prepare_kernel(
    place_ref, rewards_ref, seg_ref, gain_ref, cos_ref, sin_ref, q_ref, up_ref, k_ref,
    query_hbm, query_t_hbm, grad_hbm, grad_t_hbm, unit_hbm, factor_hbm, angle_hbm, own_hbm, xq, xu,
    query_ref, query_t_ref, grad_ref, grad_t_ref, unit_ref, factor_ref, angle_ref, own_ref, out_sem,
):
    xq[...] = q_ref[...].astype(F32).reshape(xq.shape)
    xu[...] = up_ref[...].astype(F32).reshape(xu.shape)
    gain = gain_ref[...]
    reward = [rewards_ref[r] for r in range(RESPONSES)]
    centre = (reward[0] + reward[1] + reward[2] + reward[3] + reward[4]) * (1.0 / RESPONSES)
    seg = seg_ref[...]
    adv_row = jnp.zeros(seg.shape, F32)
    for r in range(RESPONSES):
        adv_row = adv_row + jnp.where(seg == r + 1, reward[r] - centre, 0.0)
    for i in range(BLOCKS):
        block = BLOCKS * lax.axis_index("seq") + i
        start = place_ref[block // 2] * TILE + lax.rem(block, 2) * HALF
        start = pl.multiple_of(start, HALF)
        for n, ref in enumerate((cos_ref, sin_ref)):
            angle = ref[pl.ds(start, HALF), :]
            angle_ref[n, :, i * COLS : (i + 1) * COLS] = jnp.concatenate([angle] * GROUP, axis=0).T
            own_ref[n, i * HALF : (i + 1) * HALF, :] = angle
    for g in range(KV):
        x = k_ref[g].astype(F32)
        factor = lax.rsqrt(mean_lanes(x * x) + EPS)
        own_ref[2 + g] = x * factor
        own_ref[2 + KV + g] = jnp.broadcast_to(factor, (LOCAL, WIDTH))

    def per_kv(g, carry):
        for i in range(BLOCKS):
            span = slice(i * COLS, (i + 1) * COLS)

            def columns(ref):
                rows = [ref[head_rows(i, g, h), :] for h in range(GROUP)]
                return jnp.concatenate(rows, axis=0).T

            x = columns(xq)
            factor = lax.rsqrt(mean_rows(x * x) + EPS)
            unit = x * factor
            normed = unit * gain
            turned = normed * angle_ref[0, :, span] + swap_rows(normed) * angle_ref[1, :, span]
            query_ref[g, span, :] = turned.T.astype(BF16)
            query_t_ref[g, :, span] = turned.astype(BF16)
            unit_ref[g, :, span] = unit
            factor_ref[g, :, span] = jnp.broadcast_to(factor, (8, COLS))
            adv = jnp.concatenate([adv_row[:, i * HALF : (i + 1) * HALF]] * GROUP, axis=1)
            grad = columns(xu) * adv
            grad_t_ref[g, :, span] = grad.astype(BF16)
            grad_ref[g, span, :] = grad.T.astype(BF16)
        return carry

    lax.fori_loop(0, KV, per_kv, 0)
    stores = [
        pltpu.make_async_copy(source, target, out_sem.at[n])
        for n, (source, target) in enumerate(
            [
                (query_ref, query_hbm), (query_t_ref, query_t_hbm), (grad_ref, grad_hbm),
                (grad_t_ref, grad_t_hbm), (unit_ref, unit_hbm), (factor_ref, factor_hbm),
                (angle_ref, angle_hbm), (own_ref, own_hbm),
            ]
        )
    ]
    for store in stores:
        store.start()
    for store in stores:
        store.wait()


def attention_kernel(
    tile_count, table_ref, place_ref, gain_ref, cos_hbm, sin_hbm,
    query_hbm, query_t_hbm, grad_hbm, grad_t_hbm, unit_hbm, angle_hbm,
    parts_hbm, mine_hbm, hop_in_hbm, swap_in_hbm,
    out_hbm, dq_hbm, gain_out_ref, prompt_hbm, swap_hbm, hop_hbm, own_hbm,
    out_ref, dq_ref, cos_ref, sin_ref, query_v, query_t_v, grad_v, grad_t_v, unit_v, angle_v,
    kvb, ybuf, kr, kt, vr, vt, kcos, ksin, ebuf, pbuf, dsbuf, limits, ksum, lsum, qsum,
    in_sem, out_sem,
):
    me = lax.axis_index("seq")
    wb = jnp.clip((BLOCKS * me) // 2 - 3, PROMPT, tile_count - WINDOW)
    prompt_rows = PROMPT * TILE

    def rows_of(back, skip=0):
        return pl.multiple_of((me - back) * LOCAL + skip - wb * TILE + 2 * prompt_rows, HALF)

    kvb[:, 2 * prompt_rows :, :] = jnp.zeros((PAIR, WINDOW * TILE, WIDTH), BF16)
    devices, _, share_rows, _ = parts_hbm.shape
    key_loads = [
        pltpu.make_async_copy(
            parts_hbm.at[n], kvb.at[:, pl.ds(n * share_rows, share_rows), :], in_sem.at[8 + n]
        )
        for n in range(devices)
    ]
    key_loads.append(pltpu.make_async_copy(cos_hbm, cos_ref, in_sem.at[6]))
    key_loads.append(pltpu.make_async_copy(sin_hbm, sin_ref, in_sem.at[7]))
    window_loads = [
        (0, pltpu.make_async_copy(mine_hbm, kvb.at[:, pl.ds(rows_of(0), LOCAL), :], in_sem.at[8 + devices]))
    ]

    def earlier(back, source, skip, size):
        start = jnp.maximum(rows_of(back, skip), prompt_rows)
        target = kvb.at[:, pl.ds(pl.multiple_of(start, HALF), size), :]
        window_loads.append((back, pltpu.make_async_copy(source, target, in_sem.at[8 + devices + back])))

    earlier(1, swap_in_hbm.at[:, pl.ds(0, LOCAL), :], 0, LOCAL)
    earlier(2, hop_in_hbm, 0, LOCAL)
    earlier(3, swap_in_hbm.at[:, pl.ds(LOCAL, HALF), :], LOCAL - HALF, HALF)
    loads = [
        pltpu.make_async_copy(query_t_hbm, query_t_v, in_sem.at[0]),
        pltpu.make_async_copy(grad_t_hbm, grad_t_v, in_sem.at[1]),
        pltpu.make_async_copy(query_hbm, query_v, in_sem.at[2]),
        pltpu.make_async_copy(grad_hbm, grad_v, in_sem.at[3]),
        pltpu.make_async_copy(unit_hbm, unit_v, in_sem.at[4]),
        pltpu.make_async_copy(angle_hbm, angle_v, in_sem.at[5]),
    ]
    for load in key_loads + loads:
        load.start()
    for back, load in window_loads:
        pl.when(me >= back)(load.start)

    gain = gain_ref[...]
    gain_turned = swap_halves(gain)
    ksum[...] = jnp.zeros_like(ksum)
    lsum[...] = jnp.zeros_like(lsum)
    qsum[...] = jnp.zeros_like(qsum)
    ybuf[:, prompt_rows : 2 * prompt_rows] = jnp.zeros((PAIR, prompt_rows, WIDTH), BF16)

    lane = lax.broadcasted_iota(jnp.int32, (1, COLS), 1)
    key_place = [tile * TILE for tile in range(PROMPT)]
    key_place += [pl.multiple_of(place_ref[wb + j] * TILE, TILE) for j in range(WINDOW)]
    for tile in range(SPAN):
        name = tile if tile < PROMPT else wb + tile - PROMPT
        for i in range(BLOCKS):
            block = BLOCKS * me + i
            kind = table_ref[(block // 2) * tile_count + name]
            one = (kind == 1).astype(jnp.int32)
            two = (kind == 2).astype(jnp.int32)
            slot = lax.rem(block, 2) * HALF + lax.rem(lane, HALF)
            limits[tile : tile + 1, i * COLS : (i + 1) * COLS] = (
                two * slot + (one * (TILE + 1) - 1 + two)
            )

    for load in key_loads:
        load.wait()
    for back, load in window_loads:
        pl.when(me >= back)(load.wait)

    def prepare_keys(g, carry):
        for tile in range(SPAN):
            at = slice(tile * TILE, (tile + 1) * TILE)
            source = tile * TILE if tile < PROMPT else tile * TILE + prompt_rows
            source = slice(source, source + TILE)
            x = kvb[g, source, :].astype(F32)
            factor = lax.rsqrt(mean_lanes(x * x) + EPS)
            unit = x * factor
            first = unit * cos_ref[pl.ds(key_place[tile], TILE), :]
            second = swap_halves(unit) * sin_ref[pl.ds(key_place[tile], TILE), :]
            turned = first * gain + second * gain_turned
            kcos[g, at, :] = first
            ksin[g, at, :] = second
            kr[g, at, :] = turned.astype(BF16)
            kt[g, :, at] = turned.T.astype(BF16)
            value = kvb[KV + g, source, :]
            vr[g, at, :] = value
            vt[g, :, at] = value.astype(F32).T.astype(BF16)
        return carry

    lax.fori_loop(0, KV, prepare_keys, 0)
    for load in loads:
        load.wait()

    scale = 1.0 / math.sqrt(WIDTH)
    key_at = lax.broadcasted_iota(jnp.int32, (TILE, ALL), 0)
    third = SPAN // 3

    def per_kv(g, carry):
        query_t = query_t_v[g]
        grad_t = grad_t_v[g]
        total = jnp.zeros((1, ALL), F32)
        for c in range(3):
            rows = slice(c * third * TILE, (c + 1) * third * TILE)
            score = jnp.dot(kr[g, rows, :], query_t, preferred_element_type=F32)
            for t in range(third):
                tile = c * third + t
                raw = jnp.where(
                    key_at <= limits[tile : tile + 1, :],
                    jnp.exp2(score[t * TILE : (t + 1) * TILE] * (scale * math.log2(math.e))),
                    0.0,
                )
                ebuf[tile * TILE : (tile + 1) * TILE, :] = raw
                total = total + jnp.sum(raw, axis=0, keepdims=True)
        share = jnp.where(total > 0, 1.0 / total, 0.0)
        for tile in range(SPAN):
            at = slice(tile * TILE, (tile + 1) * TILE)
            pbuf[at, :] = (ebuf[at, :] * share).astype(BF16)
        out_t = jnp.dot(vt[g], pbuf[...], preferred_element_type=F32)
        out_ref[g] = out_t.astype(BF16)
        delta = jnp.sum(grad_t.astype(F32) * out_t, axis=0, keepdims=True)
        for c in range(3):
            rows = slice(c * third * TILE, (c + 1) * third * TILE)
            dweights = jnp.dot(vr[g, rows, :], grad_t, preferred_element_type=F32)
            dsbuf[rows, :] = (
                pbuf[rows, :].astype(F32) * (dweights - delta)
            ).astype(BF16)
        dv = jnp.dot(pbuf[...], grad_v[g], preferred_element_type=F32)
        dq_t = jnp.dot(kt[g], dsbuf[...], preferred_element_type=F32)
        dq_t = (dq_t * scale).astype(BF16)
        dq_ref[g] = dq_t
        dq_t = dq_t.astype(F32)
        dnormed = (dq_t * angle_v[0] - swap_rows(dq_t) * angle_v[1]) * unit_v[g]
        for n in range(ALL // WIDTH):
            qsum[...] += dnormed[:, n * WIDTH : (n + 1) * WIDTH]
        dk = jnp.dot(dsbuf[...], query_v[g], preferred_element_type=F32) * scale
        ksum[...] += rows_to_eight(dk * kcos[g])
        lsum[...] += rows_to_eight(dk * ksin[g])
        for at, item in ((g, dk), (KV + g, dv)):
            item = item.astype(BF16)
            ybuf[at, :prompt_rows, :] = item[:prompt_rows]
            ybuf[at, 2 * prompt_rows :, :] = item[prompt_rows:]
        pltpu.make_async_copy(out_ref.at[g], out_hbm.at[g], out_sem.at[g]).start()
        pltpu.make_async_copy(dq_ref.at[g], dq_hbm.at[g], out_sem.at[KV + g]).start()
        return carry

    lax.fori_loop(0, KV, per_kv, 0)

    def mine(back, skip=0):
        return pl.multiple_of(jnp.maximum(rows_of(back, skip), prompt_rows), HALF)

    stores = [(n * share_rows, share_rows, prompt_hbm.at[n]) for n in range(devices)]
    stores += [
        (mine(1), LOCAL, swap_hbm.at[:, pl.ds(0, LOCAL), :]),
        (mine(3, LOCAL - HALF), HALF, swap_hbm.at[:, pl.ds(LOCAL, HALF), :]),
        (mine(2), LOCAL, hop_hbm),
        (mine(0), LOCAL, own_hbm),
    ]
    stores = [
        pltpu.make_async_copy(ybuf.at[:, pl.ds(start, size), :], target, out_sem.at[PAIR + n])
        for n, (start, size, target) in enumerate(stores)
    ]
    for store in stores:
        store.start()
    gain_out_ref[0:1, :] = jnp.sum(qsum[...].T, axis=0, keepdims=True)
    second = swap_halves(jnp.sum(lsum[...], axis=0, keepdims=True))
    gain_out_ref[1:2, :] = jnp.sum(ksum[...], axis=0, keepdims=True) + second
    for g in range(KV):
        pltpu.make_async_copy(out_ref.at[g], out_hbm.at[g], out_sem.at[g]).wait()
        pltpu.make_async_copy(dq_ref.at[g], dq_hbm.at[g], out_sem.at[KV + g]).wait()
    for store in stores:
        store.wait()


def finish_kernel(
    gain_ref, angle_ref, out_t_ref, dq_t_ref, unit_ref, factor_ref, out_ref, dq_ref, os_, dqs,
):
    gain = gain_ref[...]

    def per_kv(g, carry):
        for i in range(BLOCKS):
            span = slice(i * COLS, (i + 1) * COLS)
            out = out_t_ref[g, :, span].astype(F32).T
            dturned = dq_t_ref[g, :, span].astype(F32)
            dnormed = dturned * angle_ref[0, :, span] - swap_rows(dturned) * angle_ref[1, :, span]
            unit = unit_ref[g, :, span]
            dunit = dnormed * gain
            dx = (factor_ref[g, 0:1, span] * (dunit - unit * mean_rows(dunit * unit))).T
            for h in range(GROUP):
                os_[head_rows(i, g, h), :] = out[h * HALF : (h + 1) * HALF]
                dqs[head_rows(i, g, h), :] = dx[h * HALF : (h + 1) * HALF]
        return carry

    lax.fori_loop(0, KV, per_kv, 0)
    out_ref[...] = os_[...].reshape(out_ref.shape).astype(BF16)
    dq_ref[...] = dqs[...].reshape(dq_ref.shape).astype(BF16)


def last_kernel(
    gain_ref, key_ref, own_ref, swap_ref, back_ref, *rest,
):
    blocks, (dk_ref, dv_ref, flat) = rest[:-3], rest[-3:]
    gain = gain_ref[...]
    even = (1 - lax.rem(lax.axis_index("seq"), 2)).astype(F32)

    for ref, first in ((dk_ref, 0), (dv_ref, KV)):
        for g in range(KV):
            at = first + g
            prompt = jnp.concatenate([block[at] for block in blocks], axis=0).astype(F32)
            summed = own_ref[at].astype(F32) + back_ref[at].astype(F32) + prompt
            summed = summed + even * swap_ref[at, :LOCAL].astype(F32)
            if first == 0:
                dnormed = summed * key_ref[0] - swap_halves(summed) * key_ref[1]
                unit = key_ref[2 + g]
                dunit = dnormed * gain
                summed = key_ref[2 + KV + g] * (dunit - unit * mean_lanes(dunit * unit))
            flat[pl.ds(g, LOCAL, stride=KV), :] = summed
        ref[...] = flat[...].reshape(ref.shape).astype(BF16)


def shape(dims, dtype=BF16):
    return jax.ShapeDtypeStruct(dims, dtype)


def cost(flops, size):
    return pl.CostEstimate(flops=flops, bytes_accessed=size, transcendentals=0)


def params(mib):
    return pltpu.CompilerParams(vmem_limit_bytes=mib * 1024 * 1024)


def pack(k, v, share):
    blocks = LOCAL // share
    return pl.pallas_call(
        pack_kernel,
        out_shape=[shape((PAIR, LOCAL, WIDTH))] + [shape((PAIR, share, WIDTH))] * blocks,
        in_specs=[HBM] * 2,
        out_specs=[HBM] * (1 + blocks),
        scratch_shapes=[
            pltpu.VMEM(k.shape, BF16), pltpu.VMEM(k.shape, BF16), pltpu.VMEM((LOCAL * KV, WIDTH), F32),
            pltpu.VMEM((PAIR, LOCAL, WIDTH), BF16),
            pltpu.SemaphoreType.DMA((2,)), pltpu.SemaphoreType.DMA((1 + blocks,)),
        ],
        compiler_params=params(32),
        cost_estimate=cost(1_000_000, 2_000_000),
        name="pack_keys",
    )(k, v)


def prepare(place, rewards, seg, gain, cosine, sine, q, up, k):
    rows = (KV, ALL, WIDTH)
    cols = (KV, WIDTH, ALL)
    shapes = [
        (rows, BF16), (cols, BF16), (rows, BF16), (cols, BF16), (cols, F32), ((KV, 8, ALL), F32),
        ((2, WIDTH, ALL), F32), ((2 + PAIR, LOCAL, WIDTH), F32),
    ]
    return pl.pallas_call(
        prepare_kernel,
        out_shape=[shape(*item) for item in shapes],
        in_specs=[SMEM, SMEM] + [VMEM] * 7,
        out_specs=[HBM] * 8,
        scratch_shapes=[pltpu.VMEM((LOCAL * HEADS, WIDTH), F32)] * 2
        + [pltpu.VMEM(*item) for item in shapes]
        + [pltpu.SemaphoreType.DMA((8,))],
        compiler_params=params(32),
        cost_estimate=cost(100_000_000, 16_000_000),
        name="prepare_queries",
    )(place, rewards, seg, gain, cosine, sine, q, up, k)


def attend(table, place, gain, cosine, sine, *operands):
    angle, parts = operands[5:7]
    devices, _, share, _ = parts.shape
    tile_count = devices * LOCAL // TILE
    span_rows = SPAN * TILE
    rows = (KV, ALL, WIDTH)
    cols = (KV, WIDTH, ALL)
    keys = (KV, span_rows, WIDTH)
    keys_t = (KV, WIDTH, span_rows)
    return pl.pallas_call(
        functools.partial(attention_kernel, tile_count),
        out_shape=(
            shape(cols), shape(cols), shape((2, WIDTH), F32),
            shape((devices, PAIR, share, WIDTH)),
            shape((PAIR, LOCAL + HALF, WIDTH)), shape((PAIR, LOCAL, WIDTH)), shape((PAIR, LOCAL, WIDTH)),
        ),
        in_specs=[SMEM, SMEM, VMEM] + [HBM] * 12,
        out_specs=(HBM, HBM, VMEM) + (HBM,) * 4,
        scratch_shapes=[
            pltpu.VMEM(cols, BF16), pltpu.VMEM(cols, BF16),
            pltpu.VMEM(cosine.shape, F32), pltpu.VMEM(cosine.shape, F32),
            pltpu.VMEM(rows, BF16), pltpu.VMEM(cols, BF16), pltpu.VMEM(rows, BF16), pltpu.VMEM(cols, BF16),
            pltpu.VMEM(cols, F32), pltpu.VMEM(angle.shape, F32),
            pltpu.VMEM((PAIR, span_rows + PROMPT * TILE, WIDTH), BF16),
            pltpu.VMEM((PAIR, span_rows + PROMPT * TILE, WIDTH), BF16),
            pltpu.VMEM(keys, BF16), pltpu.VMEM(keys_t, BF16), pltpu.VMEM(keys, BF16), pltpu.VMEM(keys_t, BF16),
            pltpu.VMEM(keys, F32), pltpu.VMEM(keys, F32),
            pltpu.VMEM((span_rows, ALL), F32),
            pltpu.VMEM((span_rows, ALL), BF16), pltpu.VMEM((span_rows, ALL), BF16),
            pltpu.VMEM((16, ALL), jnp.int32),
            pltpu.VMEM((8, WIDTH), F32), pltpu.VMEM((8, WIDTH), F32), pltpu.VMEM((WIDTH, WIDTH), F32),
            pltpu.SemaphoreType.DMA((12 + devices,)), pltpu.SemaphoreType.DMA((devices + 4 + PAIR,)),
        ],
        compiler_params=params(56),
        cost_estimate=cost(12 * span_rows * ALL * WIDTH * KV, 12_000_000),
        name="tree_attention",
    )(table, place, gain, cosine, sine, *operands)


def finish(gain, angle, out_t, dq_t, unit, factor):
    dims = (LOCAL, HEADS, WIDTH)
    return pl.pallas_call(
        finish_kernel,
        out_shape=(shape(dims), shape(dims)),
        in_specs=[VMEM] * 6,
        out_specs=(VMEM,) * 2,
        scratch_shapes=[pltpu.VMEM((LOCAL * HEADS, WIDTH), F32)] * 2,
        compiler_params=params(32),
        cost_estimate=cost(100_000_000, 10_000_000),
        name="finish_queries",
    )(gain, angle, out_t, dq_t, unit, factor)


def last(gain, key, own, swap, back, blocks):
    dims = (LOCAL, KV, WIDTH)
    return pl.pallas_call(
        last_kernel,
        out_shape=(shape(dims), shape(dims)),
        in_specs=[VMEM] * (5 + len(blocks)),
        out_specs=(VMEM,) * 2,
        scratch_shapes=[pltpu.VMEM((LOCAL * KV, WIDTH), F32)],
        compiler_params=params(32),
        cost_estimate=cost(1_000_000, 4_000_000),
        name="finish_keys",
    )(gain, key, own, swap, back, *blocks)


def tile_table(tiles, count):
    ids = jnp.arange(count, dtype=jnp.int32)
    row_hits = (tiles[:, 0, None] == ids).astype(jnp.int32) * tiles[:, 2, None]
    col_hits = (tiles[:, 1, None] == ids).astype(jnp.int32)
    table = jnp.einsum("tq,tk->qk", row_hits, col_hits)
    live = (table > 0) & (ids[None, :] >= PROMPT)
    first = jnp.min(jnp.where(live, ids[None, :], count), axis=1)
    inside = (ids >= PROMPT) & (first < count)
    place = jnp.minimum(jnp.where(inside, PROMPT + ids - first, ids), 2 * PROMPT - 1)
    return table.reshape(-1), place


def sum_four(x, axis, step):
    size = lax.axis_size(axis)
    if size <= step:
        return x
    a, b, c = (
        lax.ppermute(x, axis, [(i, i ^ (n * step)) for i in range(size)]) for n in (1, 2, 3)
    )
    return (x + a) + (b + c)


def prompt_pairs(devices, per_owner):
    routes = []
    for b in range(per_owner):
        pairs = [(owner, owner * per_owner + b) for owner in range(3)]
        routes.append([pair for pair in pairs if pair[1] < devices])
    return routes


def per_device(q_proj, k_proj, v_proj, upstream, segment_ids, tree_tiles, rewards, q_gain, k_gain):
    devices = lax.axis_size("seq")
    share = PROMPT * TILE // devices
    tile_count = devices * LOCAL // TILE
    routes = prompt_pairs(devices, LOCAL // share)
    even = lax.rem(lax.axis_index("seq"), 2) == 0
    cores = [(i, i ^ 1) for i in range(devices)]

    kv, *blocks = pack(k_proj[0], v_proj[0], share)
    mine = [lax.ppermute(block, "seq", pairs) for block, pairs in zip(blocks, routes)]
    hop_in = lax.ppermute(kv, "seq", [(i, i + 2) for i in range(devices - 2)])
    mine = mine[0] + mine[1] + mine[2] + mine[3] + mine[4] + mine[5]
    mine, hop_in = lax.optimization_barrier((mine, hop_in))
    parts = lax.all_to_all(
        jnp.broadcast_to(mine[None], (devices,) + mine.shape), "seq", split_axis=0, concat_axis=0, tiled=True
    )
    swap_in = jnp.where(
        even,
        jnp.concatenate([kv, hop_in[:, LOCAL - HALF :]], axis=1),
        jnp.concatenate([hop_in, hop_in[:, LOCAL - HALF :]], axis=1),
    )
    swap_in = lax.ppermute(swap_in, "seq", cores)

    table, place = tile_table(tree_tiles[0], tile_count)
    cosine, sine = (jnp.asarray(item) for item in rope_tables(2 * PROMPT * TILE))
    query, query_t, grad, grad_t, unit, factor, angle, own_key = prepare(
        place, rewards[0], segment_ids, q_gain[:, None], cosine, sine, q_proj[0], upstream[0],
        kv[:KV],
    )
    out_t, dq_t, gains, prompt, swap, hop, own = attend(
        table, place, k_gain[None], cosine, sine, query, query_t, grad, grad_t, unit, angle,
        parts, kv, hop_in, swap_in,
    )

    parts = lax.all_to_all(prompt, "seq", split_axis=0, concat_axis=0, tiled=True)
    swap = lax.ppermute(swap, "seq", cores)
    far = jnp.concatenate([jnp.zeros((PAIR, LOCAL - HALF, WIDTH), BF16), swap[:, LOCAL:]], axis=1)
    hop = hop + jnp.where(even, far, swap[:, :LOCAL])
    back = lax.ppermute(hop, "seq", [(i, i - 2) for i in range(2, devices)])
    gains = sum_four(gains, "dp", 1)
    gains, out_t, dq_t = lax.optimization_barrier((gains, out_t, dq_t))
    out, dq = finish(q_gain[:, None], angle, out_t, dq_t, unit, factor)
    gains = sum_four(sum_four(gains, "dp", 4), "seq", 1)
    piece = jnp.sum(parts.astype(F32), axis=0).astype(BF16)
    piece, gains, out, dq = lax.optimization_barrier((piece, gains, out, dq))
    blocks = [lax.ppermute(piece, "seq", [(b, a) for a, b in pairs]) for pairs in routes]
    gains = sum_four(gains, "seq", 4)
    dk, dv = last(k_gain[None], own_key, own, swap, back, blocks)
    return (out[None], dq[None], dk[None], dv[None], gains[0], gains[1])


def solution(mesh):
    whole = P("dp", "seq", None, None)
    return jax.shard_map(
        per_device,
        mesh=mesh,
        in_specs=(whole, whole, whole, whole, P("dp", "seq"), P("dp", None, None), P("dp", None), P(), P()),
        out_specs=(whole, whole, whole, whole, P(), P()),
        check_vma=False,
    )
```

time: 393 us -> 142 us (0.36); the launches traced: 387 us -> 141 us
  waiting for transfers between devices: 107 us -> 28.5 us
  blocking collectives: 76.4 us -> 0 us
  local copies, waits for them, and re-layouts: 79.6 us -> 15.7 us
  matrix products: 39.2 us -> 0.33 us
  other arithmetic: 41 us -> 2.48 us
  Pallas kernels: 0 us -> 35.9 us
  starting transfers between devices: 40.9 us -> 57.3 us
    all_to_all x8 -> x2, waiting for transfers between devices: 107 us -> 15 us  [the longest x1 12.5 us: per_device(): lax.all_to_all(jnp.broadcast_to(mine[None], (devices,) + mine.shape), 'se...]
    psum x1 -> x0, blocking collectives: 76.4 us -> none  [per_device(): q_total, k_total = lax.psum((dq_gain, dk_gain), ('seq', 'dp'))]
    ppermute x0 -> x28, starting transfers between devices: none -> 46.5 us  [the longest x12 16.3 us: sum_four(): lax.ppermute(x, axis, [(i, i ^ n * step) for i in range(size)])]
    dot_general x37 -> x1, matrix products: 39.2 us -> 0.33 us  [tile_table(): table = jnp.einsum('tq,tk->qk', row_hits, col_hits)]
    pallas_call x0 -> x5, Pallas kernels: none -> 35.9 us  [the longest x1 25.2 us: attend(): pl.pallas_call(functools.partial(attention_kernel, tile_count), out_shape...]
    unnamed x224 -> x55, local copies, waits for them, and re-layouts: 47.7 us -> 13.1 us
    all_to_all x8 -> x2, starting transfers between devices: 40.9 us -> 10.8 us  [the longest x1 6.48 us: per_device(): lax.all_to_all(jnp.broadcast_to(mine[None], (devices,) + mine.shape), 'se...]
    eq x24 -> x0, local copies, waits for them, and re-layouts: 21.8 us -> none  [block_mask(): return (kinds == 1) | (kinds == 2) & (key_at[None, :] <= query_at[:, None])]
  transfers between devices with their start and end apart: 8 -> 30, of which waited for: 7 -> 12; matrix products, arithmetic and copies ran while one was open for 24% -> 3% of each run, Pallas kernels for 0% -> 6%
where the time goes in v2:
time: 142 us; the launch traced here: 141 us
  starting transfers between devices  57.3 us (40%)
  Pallas kernels  35.9 us (25%)
  waiting for transfers between devices  28.5 us (20%)
  local copies, waits for them, and re-layouts  15.7 us (11%)
  other arithmetic  2.48 us (2%)
    pallas_call x1, Pallas kernels, attend(): pl.pallas_call(functools.partial(attention_kernel, tile_count), out_shape...  25.2 us
    ppermute x12, starting transfers between devices, sum_four(): lax.ppermute(x, axis, [(i, i ^ n * step) for i in range(size)])  16.3 us
    ppermute x6, starting transfers between devices, per_device(): lax.ppermute(block, 'seq', pairs)  15.4 us
    unnamed x55, local copies, waits for them, and re-layouts  13.1 us
    all_to_all x1, waiting for transfers between devices, per_device(): lax.all_to_all(jnp.broadcast_to(mine[None], (devices,) + mine.shape), 'se...  12.5 us
    ppermute x6, starting transfers between devices, per_device(): lax.ppermute(piece, 'seq', [(b, a) for a, b in pairs])  8.88 us
    all_to_all x1, starting transfers between devices, per_device(): lax.all_to_all(jnp.broadcast_to(mine[None], (devices,) + mine.shape), 'se...  6.48 us
    ppermute x12, waiting for transfers between devices, sum_four(): lax.ppermute(x, axis, [(i, i ^ n * step) for i in range(size)])  6.28 us
  transfers between devices with their start and end apart: 30, of which 12 were waited for; matrix products, arithmetic and copies ran while one was open for 3% of the time, Pallas kernels for 6%

profile of v2, /device:TPU:1, one launch (start us, length us, event | category | flops | bytes accessed | tf_op | source)
XLA Modules:
  0.0 141.3 jit_solution(12268657498284181820)
XLA Ops:
  3.5 4.4 %collective-permute-start.6 = (bf16[8,192,128]{2,1,0:T(8,128)(2,1)S(1)}, bf16[8,192,128]{2,1,0:T(8,128)(2,1)S(1)}, u32[]{:S(2)}, u32[]{:S(2)}) collective-permute-start(bf16[8,192,128]{2,1,0:T(8,128)(2,1)S(1)} %get-tuple-element.41.mine_hbm), channel_id=1, source_target_pairs={{0,32},{16,48},{32,64},{48,80},{64,96},{80,112},{96,128},{112,144}... | collective-permute-start | bytes 1179656 | tf_op jit(solution)/shard_map/ppermute | solution.py:551
  7.9 8.3 %collective-permute-start = (bf16[8,32,128]{2,1,0:T(8,128)(2,1)S(1)}, bf16[8,32,128]{2,1,0:T(8,128)(2,1)S(1)}, u32[]{:S(2)}, u32[]{:S(2)}) collective-permute-start(bf16[8,32,128]{2,1,0:T(8,128)(2,1)S(1)} %get-tuple-element.48), channel_id=1, source_target_pairs={{0,0},{16,96},{32,192},{1,1},{17,97},{33,193},{2,2},{18,98},{34,19... | collective-permute-start | bytes 196616 | tf_op jit(solution)/shard_map/ppermute | solution.py:550
  16.2 1.9 %collective-permute-start.1 = (bf16[8,32,128]{2,1,0:T(8,128)(2,1)S(1)}, bf16[8,32,128]{2,1,0:T(8,128)(2,1)S(1)}, u32[]{:S(2)}, u32[]{:S(2)}) collective-permute-start(bf16[8,32,128]{2,1,0:T(8,128)(2,1)S(1)} %get-tuple-element.49), channel_id=1, source_target_pairs={{0,16},{16,112},{32,208},{1,17},{17,113},{33,209},{2,18},{18,114},... | collective-permute-start | bytes 196616 | tf_op jit(solution)/shard_map/ppermute | solution.py:550
  18.1 1.3 collective-permute-start.2
  25.9 6.5 %all-to-all-start = ((bf16[16,8,32,128]{3,2,1,0:T(8,128)(2,1)}), bf16[16,8,32,128]{3,2,1,0:T(8,128)(2,1)}, u32[]{:S(2)}, u32[]{:S(2)}) async-start(bf16[16,8,32,128]{3,2,1,0:T(8,128)(2,1)} %broadcast_in_dim.47), calls=%async_computation | async-start | bytes 2097152 | tf_op jit(solution)/shard_map/all_to_all | solution.py:554
  37.0 5.2 %prepare_queries.1 = (bf16[4,768,128]{2,1,0:T(8,128)(2,1)S(1)}, bf16[4,128,768]{2,1,0:T(8,128)(2,1)S(1)}, bf16[4,768,128]{2,1,0:T(8,128)(2,1)S(1)}, bf16[4,128,7...) custom-call(s32[24]{0:T(128)S(1)} %fusion.8.place_ref, ...), custom_call_target="tpu_custom_call" | custom-call | flops 100000000 | bytes 16000000 | tf_op jit(solution)/shard_map/prepare_queries/pallas_call | solution.py:430
  47.9 12.5 %all-to-all-done.parts_hbm = bf16[16,8,32,128]{3,2,1,0:T(8,128)(2,1)} async-done(((bf16[16,8,32,128]{3,2,1,0:T(8,128)(2,1)}), bf16[16,8,32,128]{3,2,1,0:T(8,128)(2,1)}, u32[]{:S(2)}, u32[]{:S(2)}) %all-to-all-start) | async-done | bytes 1048608 | tf_op jit(solution)/shard_map/all_to_all | solution.py:554
  60.4 25.2 %tree_attention.1 = (bf16[4,128,768]{2,1,0:T(8,128)(2,1)}, bf16[4,128,768]{2,1,0:T(8,128)(2,1)}, f32[2,128]{1,0:T(2,128)}, bf16[16,8,32,128]{3,2,1,0:T(8,128)(2,...) custom-call(s32[576]{0:T(1024)} %reshape.21.table_ref, ...), custom_call_target="tpu_custom_call" | custom-call | flops 5435817984 | bytes 12000000 | tf_op jit(solution)/shard_map/tree_attention/pallas_call | solution.py:453
  85.6 4.4 %all-to-all-start.1 = ((bf16[16,8,32,128]{3,2,1,0:T(8,128)(2,1)}), bf16[16,8,32,128]{3,2,1,0:T(8,128)(2,1)}, u32[]{:S(2)}, u32[]{:S(2)}) async-start(bf16[16,8,32,128]{3,2,1,0:T(8,128)(2,1)} %get-tuple-element.56), calls=%async_computation.1 | async-start | bytes 2097152 | tf_op jit(solution)/shard_map/all_to_all | solution.py:575
  90.1 2.8 %collective-permute-start.10 = (f32[2,128]{1,0:T(2,128)S(1)}, f32[2,128]{1,0:T(2,128)S(1)}, u32[]{:S(2)}, u32[]{:S(2)}) collective-permute-start(f32[2,128]{1,0:T(2,128)S(1)} %copy-done.25), channel_id=1, source_target_pairs={{0,3},{1,2},{2,1},{3,0},{4,7},{5,6},{6,5},{7,4},{8,11},{9,10},{10,... | collective-permute-start | bytes 3080 | tf_op jit(solution)/shard_map/ppermute | solution.py:528
  93.9 3.4 %collective-permute-done.9 = f32[2,128]{1,0:T(2,128)S(1)} collective-permute-done((f32[2,128]{1,0:T(2,128)S(1)}, f32[2,128]{1,0:T(2,128)S(1)}, u32[]{:S(2)}, u32[]{:S(2)}) %collective-permute-start.9) | collective-permute-done | bytes 1056 | tf_op jit(solution)/shard_map/ppermute | solution.py:528
  97.3 2.6 %collective-permute-start.13 = (f32[2,128]{1,0:T(2,128)S(1)}, f32[2,128]{1,0:T(2,128)S(1)}, u32[]{:S(2)}, u32[]{:S(2)}) collective-permute-start(f32[2,128]{1,0:T(2,128)S(1)} %add_add_fusion.4), channel_id=1, source_target_pairs={{0,12},{1,13},{2,14},{3,15},{4,8},{5,9},{6,10},{7,11},{8,4},{9,5},... | collective-permute-start | bytes 3080 | tf_op jit(solution)/shard_map/ppermute | solution.py:528
  104.1 3.0 %finish_queries.1 = (bf16[192,16,128]{2,1,0:T(8,128)(2,1)}, bf16[192,16,128]{2,1,0:T(8,128)(2,1)}) custom-call(f32[128,1]{1,0:T(8,128)S(1)} %copy.20.gain_ref, f32[2,128,768]{2,1,0:T(8,128)S(1)} %copy-done.6, bf16[4,128,768]{2,1,0:T(8,128)(2,1)S(1)} %copy-done.7, bf16[4,128,768]{2,1,0:T(8,128)(2,1)S(1)} %copy-done.8, f32[4,128,768]{2,1,0:T(8,128)S(1)} %copy-done.1, ...), custom_call_target="tpu_custom_call" | custom-call | flops 100000000 | bytes 10000000 | tf_op jit(solution)/shard_map/finish_queries/pallas_call | solution.py:485
  107.2 2.9 %collective-permute-start.16 = (f32[2,128]{1,0:T(2,128)S(1)}, f32[2,128]{1,0:T(2,128)S(1)}, u32[]{:S(2)}, u32[]{:S(2)}) collective-permute-start(f32[2,128]{1,0:T(2,128)S(1)} %add_add_fusion.3), channel_id=1, source_target_pairs={{0,48},{16,32},{32,16},{48,0},{64,112},{80,96},{96,80},{112,64},{1... | collective-permute-start | bytes 3080 | tf_op jit(solution)/shard_map/ppermute | solution.py:528
  112.3 2.6 %collective-permute-done.16 = f32[2,128]{1,0:T(2,128)S(1)} collective-permute-done((f32[2,128]{1,0:T(2,128)S(1)}, f32[2,128]{1,0:T(2,128)S(1)}, u32[]{:S(2)}, u32[]{:S(2)}) %collective-permute-start.16) | collective-permute-done | bytes 1056 | tf_op jit(solution)/shard_map/ppermute | solution.py:528
  114.9 2.5 %all-to-all-done.1 = bf16[16,8,32,128]{3,2,1,0:T(8,128)(2,1)} async-done(((bf16[16,8,32,128]{3,2,1,0:T(8,128)(2,1)}), bf16[16,8,32,128]{3,2,1,0:T(8,128)(2,1)}, u32[]{:S(2)}, u32[]{:S(2)}) %all-to-all-start.1) | async-done | bytes 1048608 | tf_op jit(solution)/shard_map/all_to_all | solution.py:575
  117.5 1.4 reduce_sum.12
  119.2 3.2 %collective-permute-start.26 = (f32[2,128]{1,0:T(2,128)S(1)}, f32[2,128]{1,0:T(2,128)S(1)}, u32[]{:S(2)}, u32[]{:S(2)}) collective-permute-start(f32[2,128]{1,0:T(2,128)S(1)} %add_add_fusion.2), channel_id=1, source_target_pairs={{0,128},{16,144},{32,160},{48,176},{64,192},{80,208},{96,224},{112... | collective-permute-start | bytes 3080 | tf_op jit(solution)/shard_map/ppermute | solution.py:528
  122.4 2.2 %collective-permute-start.25 = (f32[2,128]{1,0:T(2,128)S(1)}, f32[2,128]{1,0:T(2,128)S(1)}, u32[]{:S(2)}, u32[]{:S(2)}) collective-permute-start(f32[2,128]{1,0:T(2,128)S(1)} %add_add_fusion.2), channel_id=1, source_target_pairs={{0,64},{16,80},{32,96},{48,112},{64,0},{80,16},{96,32},{112,48},{1... | collective-permute-start | bytes 3080 | tf_op jit(solution)/shard_map/ppermute | solution.py:528
  129.8 2.4 %collective-permute-start.20 = (bf16[8,32,128]{2,1,0:T(8,128)(2,1)S(1)}, bf16[8,32,128]{2,1,0:T(8,128)(2,1)S(1)}, u32[]{:S(2)}, u32[]{:S(2)}) collective-permute-start(bf16[8,32,128]{2,1,0:T(8,128)(2,1)S(1)} %reduce_sum.12), channel_id=1, source_target_pairs={{16,0},{112,16},{208,32},{17,1},{113,17},{209,33},{18,2},{114,18},... | collective-permute-start | bytes 196616 | tf_op jit(solution)/shard_map/ppermute | solution.py:586
  134.5 1.6 %collective-permute-done.22.rest_3_ = bf16[8,32,128]{2,1,0:T(8,128)(2,1)S(1)} collective-permute-done((bf16[8,32,128]{2,1,0:T(8,128)(2,1)S(1)}, bf16[8,32,128]{2,1,0:T(8,128)(2,1)S(1)}, u32[]{:S(2)}, u32[]{:S(2)}) %collective-permute-start.22) | collective-permute-done | bytes 65568 | tf_op jit(solution)/shard_map/ppermute | solution.py:586
  136.1 1.9 %collective-permute-done.21.rest_2_ = bf16[8,32,128]{2,1,0:T(8,128)(2,1)S(1)} collective-permute-done((bf16[8,32,128]{2,1,0:T(8,128)(2,1)S(1)}, bf16[8,32,128]{2,1,0:T(8,128)(2,1)S(1)}, u32[]{:S(2)}, u32[]{:S(2)}) %collective-permute-start.21) | collective-permute-done | bytes 65568 | tf_op jit(solution)/shard_map/ppermute | solution.py:586
  138.0 2.0 %collective-permute-done.19.rest_0_ = bf16[8,32,128]{2,1,0:T(8,128)(2,1)S(1)} collective-permute-done((bf16[8,32,128]{2,1,0:T(8,128)(2,1)S(1)}, bf16[8,32,128]{2,1,0:T(8,128)(2,1)S(1)}, u32[]{:S(2)}, u32[]{:S(2)}) %collective-permute-start.19) | collective-permute-done | bytes 65568 | tf_op jit(solution)/shard_map/ppermute | solution.py:586
  140.0 1.4 finish_keys.1
  (116 shorter events, 34.6 us)
Async XLA Ops:
  3.5 21.2 %collective-permute-start.6 = (bf16[8,192,128]{2,1,0:T(8,128)(2,1)S(1)}, bf16[8,192,128]{2,1,0:T(8,128)(2,1)S(1)}, u32[]{:S(2)}, u32[]{:S(2)}) collective-permute-start(bf16[8,192,128]{2,1,0:T(8,128)(2,1)S(1)} %get-tuple-element.41.mine_hbm), channel_id=1, source_target_pairs={{0,32},{16,48},{32,64},{48,80},{64,96},{80,112},{96,128},{112,144}... | collective-permute-start | bytes 1179656 | tf_op jit(solution)/shard_map/ppermute | solution.py:551
  7.9 12.8 %collective-permute-start = (bf16[8,32,128]{2,1,0:T(8,128)(2,1)S(1)}, bf16[8,32,128]{2,1,0:T(8,128)(2,1)S(1)}, u32[]{:S(2)}, u32[]{:S(2)}) collective-permute-start(bf16[8,32,128]{2,1,0:T(8,128)(2,1)S(1)} %get-tuple-element.48), channel_id=1, source_target_pairs={{0,0},{16,96},{32,192},{1,1},{17,97},{33,193},{2,2},{18,98},{34,19... | collective-permute-start | bytes 196616 | tf_op jit(solution)/shard_map/ppermute | solution.py:550
  16.2 5.8 %collective-permute-start.1 = (bf16[8,32,128]{2,1,0:T(8,128)(2,1)S(1)}, bf16[8,32,128]{2,1,0:T(8,128)(2,1)S(1)}, u32[]{:S(2)}, u32[]{:S(2)}) collective-permute-start(bf16[8,32,128]{2,1,0:T(8,128)(2,1)S(1)} %get-tuple-element.49), channel_id=1, source_target_pairs={{0,16},{16,112},{32,208},{1,17},{17,113},{33,209},{2,18},{18,114},... | collective-permute-start | bytes 196616 | tf_op jit(solution)/shard_map/ppermute | solution.py:550
  18.1 5.2 %collective-permute-start.2 = (bf16[8,32,128]{2,1,0:T(8,128)(2,1)S(1)}, bf16[8,32,128]{2,1,0:T(8,128)(2,1)S(1)}, u32[]{:S(2)}, u32[]{:S(2)}) collective-permute-start(bf16[8,32,128]{2,1,0:T(8,128)(2,1)S(1)} %get-tuple-element.50), channel_id=1, source_target_pairs={{0,32},{16,128},{32,224},{1,33},{17,129},{33,225},{2,34},{18,130},... | collective-permute-start | bytes 196616 | tf_op jit(solution)/shard_map/ppermute | solution.py:550
  25.9 34.5 %all-to-all-start = ((bf16[16,8,32,128]{3,2,1,0:T(8,128)(2,1)}), bf16[16,8,32,128]{3,2,1,0:T(8,128)(2,1)}, u32[]{:S(2)}, u32[]{:S(2)}) async-start(bf16[16,8,32,128]{3,2,1,0:T(8,128)(2,1)} %broadcast_in_dim.47), calls=%async_computation | async-start | bytes 2097152 | tf_op jit(solution)/shard_map/all_to_all | solution.py:554
  33.4 14.5 %collective-permute-start.7 = (bf16[8,256,128]{2,1,0:T(8,128)(2,1)}, bf16[8,256,128]{2,1,0:T(8,128)(2,1)}, u32[]{:S(2)}, u32[]{:S(2)}) collective-permute-start(bf16[8,256,128]{2,1,0:T(8,128)(2,1)} %fusion), channel_id=1, source_target_pairs={{0,16},{16,0},{32,48},{48,32},{64,80},{80,64},{96,112},{112,96},{1... | collective-permute-start | bytes 1572872 | tf_op jit(solution)/shard_map/ppermute | solution.py:562
  85.6 31.8 %all-to-all-start.1 = ((bf16[16,8,32,128]{3,2,1,0:T(8,128)(2,1)}), bf16[16,8,32,128]{3,2,1,0:T(8,128)(2,1)}, u32[]{:S(2)}, u32[]{:S(2)}) async-start(bf16[16,8,32,128]{3,2,1,0:T(8,128)(2,1)} %get-tuple-element.56), calls=%async_computation.1 | async-start | bytes 2097152 | tf_op jit(solution)/shard_map/all_to_all | solution.py:575
  90.0 20.8 %collective-permute-start.17 = (bf16[8,256,128]{2,1,0:T(8,128)(2,1)}, bf16[8,256,128]{2,1,0:T(8,128)(2,1)S(1)}, u32[]{:S(2)}, u32[]{:S(2)}) collective-permute-start(bf16[8,256,128]{2,1,0:T(8,128)(2,1)} %get-tuple-element.70), channel_id=1, source_target_pairs={{0,16},{16,0},{32,48},{48,32},{64,80},{80,64},{96,112},{112,96},{1... | collective-permute-start | bytes 1572872 | tf_op jit(solution)/shard_map/ppermute | solution.py:576
  92.9 4.3 %collective-permute-start.9 = (f32[2,128]{1,0:T(2,128)S(1)}, f32[2,128]{1,0:T(2,128)S(1)}, u32[]{:S(2)}, u32[]{:S(2)}) collective-permute-start(f32[2,128]{1,0:T(2,128)S(1)} %copy-done.25), channel_id=1, source_target_pairs={{0,2},{1,3},{2,0},{3,1},{4,6},{5,7},{6,4},{7,5},{8,10},{9,11},{10,... | collective-permute-start | bytes 3080 | tf_op jit(solution)/shard_map/ppermute | solution.py:528
  97.3 9.9 %collective-permute-start.13 = (f32[2,128]{1,0:T(2,128)S(1)}, f32[2,128]{1,0:T(2,128)S(1)}, u32[]{:S(2)}, u32[]{:S(2)}) collective-permute-start(f32[2,128]{1,0:T(2,128)S(1)} %add_add_fusion.4), channel_id=1, source_target_pairs={{0,12},{1,13},{2,14},{3,15},{4,8},{5,9},{6,10},{7,11},{8,4},{9,5},... | collective-permute-start | bytes 3080 | tf_op jit(solution)/shard_map/ppermute | solution.py:528
  99.8 7.3 %collective-permute-start.12 = (f32[2,128]{1,0:T(2,128)S(1)}, f32[2,128]{1,0:T(2,128)S(1)}, u32[]{:S(2)}, u32[]{:S(2)}) collective-permute-start(f32[2,128]{1,0:T(2,128)S(1)} %add_add_fusion.4), channel_id=1, source_target_pairs={{0,8},{1,9},{2,10},{3,11},{4,12},{5,13},{6,14},{7,15},{8,0},{9,1},... | collective-permute-start | bytes 3080 | tf_op jit(solution)/shard_map/ppermute | solution.py:528
  100.4 6.8 %collective-permute-start.11 = (f32[2,128]{1,0:T(2,128)S(1)}, f32[2,128]{1,0:T(2,128)S(1)}, u32[]{:S(2)}, u32[]{:S(2)}) collective-permute-start(f32[2,128]{1,0:T(2,128)S(1)} %add_add_fusion.4), channel_id=1, source_target_pairs={{0,4},{1,5},{2,6},{3,7},{4,0},{5,1},{6,2},{7,3},{8,12},{9,13},{10,... | collective-permute-start | bytes 3080 | tf_op jit(solution)/shard_map/ppermute | solution.py:528
  107.2 7.7 %collective-permute-start.16 = (f32[2,128]{1,0:T(2,128)S(1)}, f32[2,128]{1,0:T(2,128)S(1)}, u32[]{:S(2)}, u32[]{:S(2)}) collective-permute-start(f32[2,128]{1,0:T(2,128)S(1)} %add_add_fusion.3), channel_id=1, source_target_pairs={{0,48},{16,32},{32,16},{48,0},{64,112},{80,96},{96,80},{112,64},{1... | collective-permute-start | bytes 3080 | tf_op jit(solution)/shard_map/ppermute | solution.py:528
  110.1 4.8 %collective-permute-start.15 = (f32[2,128]{1,0:T(2,128)S(1)}, f32[2,128]{1,0:T(2,128)S(1)}, u32[]{:S(2)}, u32[]{:S(2)}) collective-permute-start(f32[2,128]{1,0:T(2,128)S(1)} %add_add_fusion.3), channel_id=1, source_target_pairs={{0,32},{16,48},{32,0},{48,16},{64,96},{80,112},{96,64},{112,80},{1... | collective-permute-start | bytes 3080 | tf_op jit(solution)/shard_map/ppermute | solution.py:528
  111.0 18.8 %collective-permute-start.18 = (bf16[8,192,128]{2,1,0:T(8,128)(2,1)S(1)}, bf16[8,192,128]{2,1,0:T(8,128)(2,1)S(1)}, u32[]{:S(2)}, u32[]{:S(2)}) collective-permute-start(bf16[8,192,128]{2,1,0:T(8,128)(2,1)S(1)} %fusion.1), channel_id=1, source_target_pairs={{32,0},{48,16},{64,32},{80,48},{96,64},{112,80},{128,96},{144,112}... | collective-permute-start | bytes 1179656 | tf_op jit(solution)/shard_map/ppermute | solution.py:579
  118.9 7.0 %collective-permute-start.27 = (f32[2,128]{1,0:T(2,128)S(1)}, f32[2,128]{1,0:T(2,128)S(1)}, u32[]{:S(2)}, u32[]{:S(2)}) collective-permute-start(f32[2,128]{1,0:T(2,128)S(1)} %add_add_fusion.2), channel_id=1, source_target_pairs={{0,192},{16,208},{32,224},{48,240},{64,128},{80,144},{96,160},{112... | collective-permute-start | bytes 3080 | tf_op jit(solution)/shard_map/ppermute | solution.py:528
  119.2 8.0 %collective-permute-start.26 = (f32[2,128]{1,0:T(2,128)S(1)}, f32[2,128]{1,0:T(2,128)S(1)}, u32[]{:S(2)}, u32[]{:S(2)}) collective-permute-start(f32[2,128]{1,0:T(2,128)S(1)} %add_add_fusion.2), channel_id=1, source_target_pairs={{0,128},{16,144},{32,160},{48,176},{64,192},{80,208},{96,224},{112... | collective-permute-start | bytes 3080 | tf_op jit(solution)/shard_map/ppermute | solution.py:528
  122.4 6.1 %collective-permute-start.25 = (f32[2,128]{1,0:T(2,128)S(1)}, f32[2,128]{1,0:T(2,128)S(1)}, u32[]{:S(2)}, u32[]{:S(2)}) collective-permute-start(f32[2,128]{1,0:T(2,128)S(1)} %add_add_fusion.2), channel_id=1, source_target_pairs={{0,64},{16,80},{32,96},{48,112},{64,0},{80,16},{96,32},{112,48},{1... | collective-permute-start | bytes 3080 | tf_op jit(solution)/shard_map/ppermute | solution.py:528
  124.6 8.0 %collective-permute-start.24 = (bf16[8,32,128]{2,1,0:T(8,128)(2,1)S(1)}, bf16[8,32,128]{2,1,0:T(8,128)(2,1)S(1)}, u32[]{:S(2)}, u32[]{:S(2)}) collective-permute-start(bf16[8,32,128]{2,1,0:T(8,128)(2,1)S(1)} %reduce_sum.12), channel_id=1, source_target_pairs={{80,0},{176,16},{81,1},{177,17},{82,2},{178,18},{83,3},{179,19},{8... | collective-permute-start | bytes 196616 | tf_op jit(solution)/shard_map/ppermute | solution.py:586
  125.9 8.6 %collective-permute-start.23 = (bf16[8,32,128]{2,1,0:T(8,128)(2,1)S(1)}, bf16[8,32,128]{2,1,0:T(8,128)(2,1)S(1)}, u32[]{:S(2)}, u32[]{:S(2)}) collective-permute-start(bf16[8,32,128]{2,1,0:T(8,128)(2,1)S(1)} %reduce_sum.12), channel_id=1, source_target_pairs={{64,0},{160,16},{65,1},{161,17},{66,2},{162,18},{67,3},{163,19},{6... | collective-permute-start | bytes 196616 | tf_op jit(solution)/shard_map/ppermute | solution.py:586
  127.2 8.9 %collective-permute-start.22 = (bf16[8,32,128]{2,1,0:T(8,128)(2,1)S(1)}, bf16[8,32,128]{2,1,0:T(8,128)(2,1)S(1)}, u32[]{:S(2)}, u32[]{:S(2)}) collective-permute-start(bf16[8,32,128]{2,1,0:T(8,128)(2,1)S(1)} %reduce_sum.12), channel_id=1, source_target_pairs={{48,0},{144,16},{240,32},{49,1},{145,17},{241,33},{50,2},{146,18},... | collective-permute-start | bytes 196616 | tf_op jit(solution)/shard_map/ppermute | solution.py:586
  128.5 9.5 %collective-permute-start.21 = (bf16[8,32,128]{2,1,0:T(8,128)(2,1)S(1)}, bf16[8,32,128]{2,1,0:T(8,128)(2,1)S(1)}, u32[]{:S(2)}, u32[]{:S(2)}) collective-permute-start(bf16[8,32,128]{2,1,0:T(8,128)(2,1)S(1)} %reduce_sum.12), channel_id=1, source_target_pairs={{32,0},{128,16},{224,32},{33,1},{129,17},{225,33},{34,2},{130,18},... | collective-permute-start | bytes 196616 | tf_op jit(solution)/shard_map/ppermute | solution.py:586
  129.8 8.2 %collective-permute-start.20 = (bf16[8,32,128]{2,1,0:T(8,128)(2,1)S(1)}, bf16[8,32,128]{2,1,0:T(8,128)(2,1)S(1)}, u32[]{:S(2)}, u32[]{:S(2)}) collective-permute-start(bf16[8,32,128]{2,1,0:T(8,128)(2,1)S(1)} %reduce_sum.12), channel_id=1, source_target_pairs={{16,0},{112,16},{208,32},{17,1},{113,17},{209,33},{18,2},{114,18},... | collective-permute-start | bytes 196616 | tf_op jit(solution)/shard_map/ppermute | solution.py:586
  132.6 7.4 %collective-permute-start.19 = (bf16[8,32,128]{2,1,0:T(8,128)(2,1)S(1)}, bf16[8,32,128]{2,1,0:T(8,128)(2,1)S(1)}, u32[]{:S(2)}, u32[]{:S(2)}) collective-permute-start(bf16[8,32,128]{2,1,0:T(8,128)(2,1)S(1)} %reduce_sum.12), channel_id=1, source_target_pairs={{0,0},{96,16},{192,32},{1,1},{97,17},{193,33},{2,2},{98,18},{194,3... | collective-permute-start | bytes 196616 | tf_op jit(solution)/shard_map/ppermute | solution.py:586
  (33 other events, 208.6 us)

commit v3 on v2

--- a/solution.py
+++ b/solution.py
@@ -94,11 +94,24 @@
         store.wait()
 
 
+def load_all(pairs, sems):
+    loads = [pltpu.make_async_copy(a, b, sems.at[n]) for n, (a, b) in enumerate(pairs)]
+    for load in loads:
+        load.start()
+    for load in loads:
+        load.wait()
+
+
 def prepare_kernel(
-    place_ref, rewards_ref, seg_ref, gain_ref, cos_ref, sin_ref, q_ref, up_ref, k_ref,
+    place_ref, rewards_ref, seg_ref, gain_ref, cos_hbm, sin_hbm, q_hbm, up_hbm, k_hbm,
     query_hbm, query_t_hbm, grad_hbm, grad_t_hbm, unit_hbm, factor_hbm, angle_hbm, own_hbm, xq, xu,
-    query_ref, query_t_ref, grad_ref, grad_t_ref, unit_ref, factor_ref, angle_ref, own_ref, out_sem,
+    query_ref, query_t_ref, grad_ref, grad_t_ref, unit_ref, factor_ref, angle_ref, own_ref,
+    cos_ref, sin_ref, q_ref, up_ref, k_ref, in_sem, out_sem,
 ):
+    load_all(
+        [(q_hbm, q_ref), (up_hbm, up_ref), (cos_hbm, cos_ref), (sin_hbm, sin_ref), (k_hbm.at[pl.ds(0, KV)], k_ref)],
+        in_sem,
+    )
     xq[...] = q_ref[...].astype(F32).reshape(xq.shape)
     xu[...] = up_ref[...].astype(F32).reshape(xu.shape)
     gain = gain_ref[...]
@@ -165,8 +178,8 @@
 def attention_kernel(
     tile_count, table_ref, place_ref, gain_ref, cos_hbm, sin_hbm,
     query_hbm, query_t_hbm, grad_hbm, grad_t_hbm, unit_hbm, angle_hbm,
-    parts_hbm, mine_hbm, hop_in_hbm, swap_in_hbm,
-    out_hbm, dq_hbm, gain_out_ref, prompt_hbm, swap_hbm, hop_hbm, own_hbm,
+    parts_hbm, others_hbm, mine_hbm, hop_in_hbm, swap_in_hbm,
+    out_hbm, dq_hbm, gain_out_ref, keep_hbm, send_hbm, swap_hbm, hop_hbm, own_hbm,
     out_ref, dq_ref, cos_ref, sin_ref, query_v, query_t_v, grad_v, grad_t_v, unit_v, angle_v,
     kvb, ybuf, kr, kt, vr, vt, kcos, ksin, ebuf, pbuf, dsbuf, limits, ksum, lsum, qsum,
     in_sem, out_sem,
@@ -179,13 +192,15 @@
         return pl.multiple_of((me - back) * LOCAL + skip - wb * TILE + 2 * prompt_rows, HALF)
 
     kvb[:, 2 * prompt_rows :, :] = jnp.zeros((PAIR, WINDOW * TILE, WIDTH), BF16)
-    devices, _, share_rows, _ = parts_hbm.shape
-    key_loads = [
-        pltpu.make_async_copy(
-            parts_hbm.at[n], kvb.at[:, pl.ds(n * share_rows, share_rows), :], in_sem.at[8 + n]
-        )
-        for n in range(devices)
-    ]
+    chips, _, share_rows, _ = parts_hbm.shape
+    devices = 2 * chips
+    parity = lax.rem(me, 2)
+    key_loads = []
+    for n in range(chips):
+        for at, half, source in ((2 * n, parity, parts_hbm), (2 * n + 1, 1 - parity, others_hbm)):
+            start = pl.multiple_of(half * (prompt_rows // 2) + n * share_rows, share_rows)
+            target = kvb.at[:, pl.ds(start, share_rows), :]
+            key_loads.append(pltpu.make_async_copy(source.at[n], target, in_sem.at[8 + at]))
     key_loads.append(pltpu.make_async_copy(cos_hbm, cos_ref, in_sem.at[6]))
     key_loads.append(pltpu.make_async_copy(sin_hbm, sin_ref, in_sem.at[7]))
     window_loads = [
@@ -208,7 +223,7 @@
         pltpu.make_async_copy(unit_hbm, unit_v, in_sem.at[4]),
         pltpu.make_async_copy(angle_hbm, angle_v, in_sem.at[5]),
     ]
-    for load in key_loads + loads:
+    for load in key_loads:
         load.start()
     for back, load in window_loads:
         pl.when(me >= back)(load.start)
@@ -239,6 +254,8 @@
         load.wait()
     for back, load in window_loads:
         pl.when(me >= back)(load.wait)
+    for load in loads:
+        load.start()
 
     def prepare_keys(g, carry):
         for tile in range(SPAN):
@@ -321,7 +338,11 @@
     def mine(back, skip=0):
         return pl.multiple_of(jnp.maximum(rows_of(back, skip), prompt_rows), HALF)
 
-    stores = [(n * share_rows, share_rows, prompt_hbm.at[n]) for n in range(devices)]
+    stores = []
+    for n in range(chips):
+        for half, target in ((parity, keep_hbm), (1 - parity, send_hbm)):
+            start = pl.multiple_of(half * (prompt_rows // 2) + n * share_rows, share_rows)
+            stores.append((start, share_rows, target.at[n]))
     stores += [
         (mine(1), LOCAL, swap_hbm.at[:, pl.ds(0, LOCAL), :]),
         (mine(3, LOCAL - HALF), HALF, swap_hbm.at[:, pl.ds(LOCAL, HALF), :]),
@@ -345,8 +366,16 @@
 
 
 def finish_kernel(
-    gain_ref, angle_ref, out_t_ref, dq_t_ref, unit_ref, factor_ref, out_ref, dq_ref, os_, dqs,
+    gain_ref, angle_hbm, out_t_hbm, dq_t_hbm, unit_hbm, factor_hbm, out_ref, dq_ref, os_, dqs,
+    angle_ref, out_t_ref, dq_t_ref, unit_ref, factor_ref, in_sem,
 ):
+    load_all(
+        [
+            (out_t_hbm, out_t_ref), (dq_t_hbm, dq_t_ref), (unit_hbm, unit_ref), (angle_hbm, angle_ref),
+            (factor_hbm, factor_ref),
+        ],
+        in_sem,
+    )
     gain = gain_ref[...]
 
     def per_kv(g, carry):
@@ -414,7 +443,7 @@
             pltpu.VMEM((PAIR, LOCAL, WIDTH), BF16),
             pltpu.SemaphoreType.DMA((2,)), pltpu.SemaphoreType.DMA((1 + blocks,)),
         ],
-        compiler_params=params(32),
+        compiler_params=params(56),
         cost_estimate=cost(1_000_000, 2_000_000),
         name="pack_keys",
     )(k, v)
@@ -430,12 +459,13 @@
     return pl.pallas_call(
         prepare_kernel,
         out_shape=[shape(*item) for item in shapes],
-        in_specs=[SMEM, SMEM] + [VMEM] * 7,
+        in_specs=[SMEM, SMEM, VMEM, VMEM] + [HBM] * 5,
         out_specs=[HBM] * 8,
         scratch_shapes=[pltpu.VMEM((LOCAL * HEADS, WIDTH), F32)] * 2
         + [pltpu.VMEM(*item) for item in shapes]
-        + [pltpu.SemaphoreType.DMA((8,))],
-        compiler_params=params(32),
+        + [pltpu.VMEM(item.shape, item.dtype) for item in (cosine, sine, q, up)]
+        + [pltpu.VMEM((KV, LOCAL, WIDTH), BF16), pltpu.SemaphoreType.DMA((5,)), pltpu.SemaphoreType.DMA((8,))],
+        compiler_params=params(56),
         cost_estimate=cost(100_000_000, 16_000_000),
         name="prepare_queries",
     )(place, rewards, seg, gain, cosine, sine, q, up, k)
@@ -443,7 +473,7 @@
 
 def attend(table, place, gain, cosine, sine, *operands):
     angle, parts = operands[5:7]
-    devices, _, share, _ = parts.shape
+    devices, share = 2 * parts.shape[0], parts.shape[2]
     tile_count = devices * LOCAL // TILE
     span_rows = SPAN * TILE
     rows = (KV, ALL, WIDTH)
@@ -454,11 +484,11 @@
         functools.partial(attention_kernel, tile_count),
         out_shape=(
             shape(cols), shape(cols), shape((2, WIDTH), F32),
-            shape((devices, PAIR, share, WIDTH)),
+            shape((devices // 2, PAIR, share, WIDTH)), shape((devices // 2, PAIR, share, WIDTH)),
             shape((PAIR, LOCAL + HALF, WIDTH)), shape((PAIR, LOCAL, WIDTH)), shape((PAIR, LOCAL, WIDTH)),
         ),
-        in_specs=[SMEM, SMEM, VMEM] + [HBM] * 12,
-        out_specs=(HBM, HBM, VMEM) + (HBM,) * 4,
+        in_specs=[SMEM, SMEM, VMEM] + [HBM] * 13,
+        out_specs=(HBM, HBM, VMEM) + (HBM,) * 5,
         scratch_shapes=[
             pltpu.VMEM(cols, BF16), pltpu.VMEM(cols, BF16),
             pltpu.VMEM(cosine.shape, F32), pltpu.VMEM(cosine.shape, F32),
@@ -485,10 +515,12 @@
     return pl.pallas_call(
         finish_kernel,
         out_shape=(shape(dims), shape(dims)),
-        in_specs=[VMEM] * 6,
+        in_specs=[VMEM] + [HBM] * 5,
         out_specs=(VMEM,) * 2,
-        scratch_shapes=[pltpu.VMEM((LOCAL * HEADS, WIDTH), F32)] * 2,
-        compiler_params=params(32),
+        scratch_shapes=[pltpu.VMEM((LOCAL * HEADS, WIDTH), F32)] * 2
+        + [pltpu.VMEM(item.shape, item.dtype) for item in (angle, out_t, dq_t, unit, factor)]
+        + [pltpu.SemaphoreType.DMA((5,))],
+        compiler_params=params(56),
         cost_estimate=cost(100_000_000, 10_000_000),
         name="finish_queries",
     )(gain, angle, out_t, dq_t, unit, factor)
@@ -502,7 +534,7 @@
         in_specs=[VMEM] * (5 + len(blocks)),
         out_specs=(VMEM,) * 2,
         scratch_shapes=[pltpu.VMEM((LOCAL * KV, WIDTH), F32)],
-        compiler_params=params(32),
+        compiler_params=params(24),
         cost_estimate=cost(1_000_000, 4_000_000),
         name="finish_keys",
     )(gain, key, own, swap, back, *blocks)
@@ -532,9 +564,10 @@
 
 def prompt_pairs(devices, per_owner):
     routes = []
+    chips = devices // 2
     for b in range(per_owner):
         pairs = [(owner, owner * per_owner + b) for owner in range(3)]
-        routes.append([pair for pair in pairs if pair[1] < devices])
+        routes.append([(owner, 2 * (p % chips) + p // chips) for owner, p in pairs if p < devices])
     return routes
 
 
@@ -551,9 +584,13 @@
     hop_in = lax.ppermute(kv, "seq", [(i, i + 2) for i in range(devices - 2)])
     mine = mine[0] + mine[1] + mine[2] + mine[3] + mine[4] + mine[5]
     mine, hop_in = lax.optimization_barrier((mine, hop_in))
-    parts = lax.all_to_all(
-        jnp.broadcast_to(mine[None], (devices,) + mine.shape), "seq", split_axis=0, concat_axis=0, tiled=True
-    )
+    chips = devices // 2
+    parities = [list(range(j, devices, 2)) for j in range(2)]
+
+    def exchange(x):
+        return lax.all_to_all(x, "seq", split_axis=0, concat_axis=0, tiled=True, axis_index_groups=parities)
+
+    parts = exchange(jnp.broadcast_to(mine[None], (chips,) + mine.shape))
     swap_in = jnp.where(
         even,
         jnp.concatenate([kv, hop_in[:, LOCAL - HALF :]], axis=1),
@@ -565,14 +602,17 @@
     cosine, sine = (jnp.asarray(item) for item in rope_tables(2 * PROMPT * TILE))
     query, query_t, grad, grad_t, unit, factor, angle, own_key = prepare(
         place, rewards[0], segment_ids, q_gain[:, None], cosine, sine, q_proj[0], upstream[0],
-        kv[:KV],
-    )
-    out_t, dq_t, gains, prompt, swap, hop, own = attend(
+        kv,
+    )
+    parts, swap_in, query = lax.optimization_barrier((parts, swap_in, query))
+    others = lax.ppermute(parts, "seq", cores)
+    out_t, dq_t, gains, keep, send, swap, hop, own = attend(
         table, place, k_gain[None], cosine, sine, query, query_t, grad, grad_t, unit, angle,
-        parts, kv, hop_in, swap_in,
-    )
-
-    parts = lax.all_to_all(prompt, "seq", split_axis=0, concat_axis=0, tiled=True)
+        parts, others, kv, hop_in, swap_in,
+    )
+
+    got = lax.ppermute(send, "seq", cores)
+    parts = exchange(keep + got)
     swap = lax.ppermute(swap, "seq", cores)
     far = jnp.concatenate([jnp.zeros((PAIR, LOCAL - HALF, WIDTH), BF16), swap[:, LOCAL:]], axis=1)
     hop = hop + jnp.where(even, far, swap[:, :LOCAL])

time: 142 us -> 128 us (0.901)
  the two profiles are of different devices: /device:TPU:1 before, /device:TPU:42 now
where the time goes in v3:
time: 128 us; the launch traced here: 127 us
  starting transfers between devices  56.3 us (44%)
  Pallas kernels  42.4 us (33%)
  waiting for transfers between devices  19.2 us (15%)
  local copies, waits for them, and re-layouts  5.16 us (4%)
  other arithmetic  2.9 us (2%)
    pallas_call x1, Pallas kernels, attend(): pl.pallas_call(functools.partial(attention_kernel, tile_count), out_shape...  23.7 us
    ppermute x12, starting transfers between devices, sum_four(): lax.ppermute(x, axis, [(i, i ^ n * step) for i in range(size)])  17 us
    all_to_all x2, starting transfers between devices, exchange(): lax.all_to_all(x, 'seq', split_axis=0, concat_axis=0, tiled=True, axis_in...  13.6 us
    ppermute x6, starting transfers between devices, per_device(): lax.ppermute(block, 'seq', pairs)  11.8 us
    pallas_call x1, Pallas kernels, prepare(): pl.pallas_call(prepare_kernel, out_shape=[shape(*item) for item in shapes...  9.17 us
    ppermute x6, starting transfers between devices, per_device(): lax.ppermute(piece, 'seq', [(b, a) for a, b in pairs])  7.09 us
    ppermute x6, waiting for transfers between devices, per_device(): lax.ppermute(piece, 'seq', [(b, a) for a, b in pairs])  6.77 us
    pallas_call x1, Pallas kernels, finish(): pl.pallas_call(finish_kernel, out_shape=(shape(dims), shape(dims)), in_sp...  6.02 us
  transfers between devices with their start and end apart: 32, of which 10 were waited for; matrix products, arithmetic and copies ran while one was open for 5% of the time, Pallas kernels for 12%

profile of v3, /device:TPU:42, one launch (start us, length us, event | category | flops | bytes accessed | tf_op | source)
XLA Modules:
  0.0 127.3 jit_solution(11226956309989440671)
XLA Ops:
  0.6 2.0 %pack_keys.1 = (bf16[8,192,128]{2,1,0:T(8,128)(2,1)}, bf16[8,32,128]{2,1,0:T(8,128)(2,1)}, bf16[8,32,128]{2,1,0:T(8,128)(2,1)}, bf16[8,32,128]{2,1,0:T(8,128)(2,...) custom-call(bf16[192,4,128]{2,1,0:T(4,128)(2,1)} %bitcast.25, ...), custom_call_target="tpu_custom_call" | custom-call | flops 1000000 | bytes 2000000 | tf_op jit(solution)/shard_map/pack_keys/pallas_call | solution.py:436
  2.7 4.0 %collective-permute-start.6 = (bf16[8,192,128]{2,1,0:T(8,128)(2,1)}, bf16[8,192,128]{2,1,0:T(8,128)(2,1)S(1)}, u32[]{:S(2)}, u32[]{:S(2)}) collective-permute-start(bf16[8,192,128]{2,1,0:T(8,128)(2,1)} %get-tuple-element.51.k_hbm.mine_hbm), channel_id=1, source_target_pairs={{0,32},{16,48},{32,64},{48,80},{64,96},{80,112},{96,128},{112,144}... | collective-permute-start | bytes 1179656 | tf_op jit(solution)/shard_map/ppermute | solution.py:584
  6.7 6.0 %collective-permute-start = (bf16[8,32,128]{2,1,0:T(8,128)(2,1)}, bf16[8,32,128]{2,1,0:T(8,128)(2,1)S(1)}, u32[]{:S(2)}, u32[]{:S(2)}) collective-permute-start(bf16[8,32,128]{2,1,0:T(8,128)(2,1)} %get-tuple-element.45), channel_id=1, source_target_pairs={{0,0},{16,192},{32,144},{1,1},{17,193},{33,145},{2,2},{18,194},{34... | collective-permute-start | bytes 196616 | tf_op jit(solution)/shard_map/ppermute | solution.py:583
  12.7 1.9 %collective-permute-start.1 = (bf16[8,32,128]{2,1,0:T(8,128)(2,1)}, bf16[8,32,128]{2,1,0:T(8,128)(2,1)S(1)}, u32[]{:S(2)}, u32[]{:S(2)}) collective-permute-start(bf16[8,32,128]{2,1,0:T(8,128)(2,1)} %get-tuple-element.46), channel_id=1, source_target_pairs={{0,32},{16,224},{32,176},{1,33},{17,225},{33,177},{2,34},{18,226},... | collective-permute-start | bytes 196616 | tf_op jit(solution)/shard_map/ppermute | solution.py:583
  22.8 8.9 %all-to-all-start = ((bf16[8,8,32,128]{3,2,1,0:T(8,128)(2,1)}), bf16[8,8,32,128]{3,2,1,0:T(8,128)(2,1)S(1)}, u32[]{:S(2)}, u32[]{:S(2)}) async-start(bf16[8,8,32,128]{3,2,1,0:T(8,128)(2,1)} %broadcast_in_dim.46), calls=%async_computation | async-start | bytes 1048576 | tf_op jit(solution)/shard_map/all_to_all | solution.py:591
  32.8 9.2 %prepare_queries.1 = (bf16[4,768,128]{2,1,0:T(8,128)(2,1)}, bf16[4,128,768]{2,1,0:T(8,128)(2,1)}, bf16[4,768,128]{2,1,0:T(8,128)(2,1)}, bf16[4,128,768]{2,1,0:T(...) custom-call(s32[24]{0:T(128)} %fusion.8.place_ref, ...), custom_call_target="tpu_custom_call" | custom-call | flops 100000000 | bytes 16000000 | tf_op jit(solution)/shard_map/prepare_queries/pallas_call | solution.py:459
  42.0 3.4 %all-to-all-done.parts_hbm = bf16[8,8,32,128]{3,2,1,0:T(8,128)(2,1)S(1)} async-done(((bf16[8,8,32,128]{3,2,1,0:T(8,128)(2,1)}), bf16[8,8,32,128]{3,2,1,0:T(8,128)(2,1)S(1)}, u32[]{:S(2)}, u32[]{:S(2)}) %all-to-all-start) | async-done | bytes 524320 | tf_op jit(solution)/shard_map/all_to_all | solution.py:591
  48.1 23.7 %tree_attention.1 = (bf16[4,128,768]{2,1,0:T(8,128)(2,1)}, bf16[4,128,768]{2,1,0:T(8,128)(2,1)}, f32[2,128]{1,0:T(2,128)}, bf16[8,8,32,128]{3,2,1,0:T(8,128)(2,1...) custom-call(s32[576]{0:T(1024)} %reshape.21.table_ref, ...), custom_call_target="tpu_custom_call" | custom-call | flops 5435817984 | bytes 12000000 | tf_op jit(solution)/shard_map/tree_attention/pallas_call | solution.py:483
  72.5 1.6 %collective-permute-start.12 = (f32[2,128]{1,0:T(2,128)}, f32[2,128]{1,0:T(2,128)S(1)}, u32[]{:S(2)}, u32[]{:S(2)}) collective-permute-start(f32[2,128]{1,0:T(2,128)} %get-tuple-element.65), channel_id=1, source_target_pairs={{0,3},{1,2},{2,1},{3,0},{4,7},{5,6},{6,5},{7,4},{8,11},{9,10},{10,... | collective-permute-start | bytes 3080 | tf_op jit(solution)/shard_map/ppermute | solution.py:560
  75.0 1.6 %collective-permute-start.10 = (f32[2,128]{1,0:T(2,128)}, f32[2,128]{1,0:T(2,128)S(1)}, u32[]{:S(2)}, u32[]{:S(2)}) collective-permute-start(f32[2,128]{1,0:T(2,128)} %get-tuple-element.65), channel_id=1, source_target_pairs={{0,1},{1,0},{2,3},{3,2},{4,5},{5,4},{6,7},{7,6},{8,9},{9,8},{10,11... | collective-permute-start | bytes 3080 | tf_op jit(solution)/shard_map/ppermute | solution.py:560
  76.6 2.0 %add.68 = bf16[8,8,32,128]{3,2,1,0:T(8,128)(2,1)} add(bf16[8,8,32,128]{3,2,1,0:T(8,128)(2,1)} %get-tuple-element.63, bf16[8,8,32,128]{3,2,1,0:T(8,128)(2,1)S(1)} %collective-permute-done.9) | non-fusion elementwise | flops 262144 | bytes 1572864 | tf_op jit(solution)/shard_map/add | solution.py:615
  78.6 4.6 %all-to-all-start.1 = ((bf16[8,8,32,128]{3,2,1,0:T(8,128)(2,1)}), bf16[8,8,32,128]{3,2,1,0:T(8,128)(2,1)S(1)}, u32[]{:S(2)}, u32[]{:S(2)}) async-start(bf16[8,8,32,128]{3,2,1,0:T(8,128)(2,1)} %add.68), calls=%async_computation.1 | async-start | bytes 1048576 | tf_op jit(solution)/shard_map/all_to_all | solution.py:591
  83.3 1.7 %collective-permute-start.15 = (f32[2,128]{1,0:T(2,128)S(1)}, f32[2,128]{1,0:T(2,128)S(1)}, u32[]{:S(2)}, u32[]{:S(2)}) collective-permute-start(f32[2,128]{1,0:T(2,128)S(1)} %add_add_fusion.4), channel_id=1, source_target_pairs={{0,12},{1,13},{2,14},{3,15},{4,8},{5,9},{6,10},{7,11},{8,4},{9,5},... | collective-permute-start | bytes 3080 | tf_op jit(solution)/shard_map/ppermute | solution.py:560
  86.1 1.5 %collective-permute-start.13 = (f32[2,128]{1,0:T(2,128)S(1)}, f32[2,128]{1,0:T(2,128)S(1)}, u32[]{:S(2)}, u32[]{:S(2)}) collective-permute-start(f32[2,128]{1,0:T(2,128)S(1)} %add_add_fusion.4), channel_id=1, source_target_pairs={{0,4},{1,5},{2,6},{3,7},{4,0},{5,1},{6,2},{7,3},{8,12},{9,13},{10,... | collective-permute-start | bytes 3080 | tf_op jit(solution)/shard_map/ppermute | solution.py:560
  87.6 6.0 %finish_queries.1 = (bf16[192,16,128]{2,1,0:T(8,128)(2,1)}, bf16[192,16,128]{2,1,0:T(8,128)(2,1)}) custom-call(f32[128,1]{1,0:T(8,128)} %copy.20.gain_ref, f32[2,128,768]{2,1,0:T(8,128)} %get-tuple-element.60.angle_hbm, bf16[4,128,768]{2,1,0:T(8,128)(2,1)} %get-tuple-element.69.out_t_hbm, bf16[4,128,768]{2,1,0:T(8,128)(2,1)} %get-tuple-element.70.dq_t_hbm, ...), custom_call_target="tpu_custom_call" | custom-call | flops 100000000 | bytes 10000000 | tf_op jit(solution)/shard_map/finish_queries/pallas_call | solution.py:515
  94.0 1.6 %collective-permute-start.16 = (f32[2,128]{1,0:T(2,128)S(1)}, f32[2,128]{1,0:T(2,128)S(1)}, u32[]{:S(2)}, u32[]{:S(2)}) collective-permute-start(f32[2,128]{1,0:T(2,128)S(1)} %add_add_fusion.3), channel_id=1, source_target_pairs={{0,16},{16,0},{32,48},{48,32},{64,80},{80,64},{96,112},{112,96},{1... | collective-permute-start | bytes 3080 | tf_op jit(solution)/shard_map/ppermute | solution.py:560
  95.9 2.2 %collective-permute-start.20 = (bf16[8,192,128]{2,1,0:T(8,128)(2,1)S(1)}, bf16[8,192,128]{2,1,0:T(8,128)(2,1)S(1)}, u32[]{:S(2)}, u32[]{:S(2)}) collective-permute-start(bf16[8,192,128]{2,1,0:T(8,128)(2,1)S(1)} %fusion.1), channel_id=1, source_target_pairs={{32,0},{48,16},{64,32},{80,48},{96,64},{112,80},{128,96},{144,112}... | collective-permute-start | bytes 1179656 | tf_op jit(solution)/shard_map/ppermute | solution.py:619
  99.2 3.0 %collective-permute-start.29 = (f32[2,128]{1,0:T(2,128)S(1)}, f32[2,128]{1,0:T(2,128)S(1)}, u32[]{:S(2)}, u32[]{:S(2)}) collective-permute-start(f32[2,128]{1,0:T(2,128)S(1)} %add_add_fusion.2), channel_id=1, source_target_pairs={{0,192},{16,208},{32,224},{48,240},{64,128},{80,144},{96,160},{112... | collective-permute-start | bytes 3080 | tf_op jit(solution)/shard_map/ppermute | solution.py:560
  102.2 2.3 %collective-permute-start.28 = (f32[2,128]{1,0:T(2,128)S(1)}, f32[2,128]{1,0:T(2,128)S(1)}, u32[]{:S(2)}, u32[]{:S(2)}) collective-permute-start(f32[2,128]{1,0:T(2,128)S(1)} %add_add_fusion.2), channel_id=1, source_target_pairs={{0,128},{16,144},{32,160},{48,176},{64,192},{80,208},{96,224},{112... | collective-permute-start | bytes 3080 | tf_op jit(solution)/shard_map/ppermute | solution.py:560
  107.8 4.9 %collective-permute-done.28 = f32[2,128]{1,0:T(2,128)S(1)} collective-permute-done((f32[2,128]{1,0:T(2,128)S(1)}, f32[2,128]{1,0:T(2,128)S(1)}, u32[]{:S(2)}, u32[]{:S(2)}) %collective-permute-start.28) | collective-permute-done | bytes 1056 | tf_op jit(solution)/shard_map/ppermute | solution.py:560
  115.4 1.9 %collective-permute-start.22 = (bf16[8,32,128]{2,1,0:T(8,128)(2,1)S(1)}, bf16[8,32,128]{2,1,0:T(8,128)(2,1)S(1)}, u32[]{:S(2)}, u32[]{:S(2)}) collective-permute-start(bf16[8,32,128]{2,1,0:T(8,128)(2,1)S(1)} %reduce_sum.12), channel_id=1, source_target_pairs={{32,0},{224,16},{176,32},{33,1},{225,17},{177,33},{34,2},{226,18},... | collective-permute-start | bytes 196616 | tf_op jit(solution)/shard_map/ppermute | solution.py:626
  119.2 2.0 %collective-permute-done.24.rest_3_ = bf16[8,32,128]{2,1,0:T(8,128)(2,1)S(1)} collective-permute-done((bf16[8,32,128]{2,1,0:T(8,128)(2,1)S(1)}, bf16[8,32,128]{2,1,0:T(8,128)(2,1)S(1)}, u32[]{:S(2)}, u32[]{:S(2)}) %collective-permute-start.24) | collective-permute-done | bytes 65568 | tf_op jit(solution)/shard_map/ppermute | solution.py:626
  121.2 1.5 %collective-permute-done.23.rest_2_ = bf16[8,32,128]{2,1,0:T(8,128)(2,1)S(1)} collective-permute-done((bf16[8,32,128]{2,1,0:T(8,128)(2,1)S(1)}, bf16[8,32,128]{2,1,0:T(8,128)(2,1)S(1)}, u32[]{:S(2)}, u32[]{:S(2)}) %collective-permute-start.23) | collective-permute-done | bytes 65568 | tf_op jit(solution)/shard_map/ppermute | solution.py:626
  122.7 2.2 %collective-permute-done.22.rest_1_ = bf16[8,32,128]{2,1,0:T(8,128)(2,1)S(1)} collective-permute-done((bf16[8,32,128]{2,1,0:T(8,128)(2,1)S(1)}, bf16[8,32,128]{2,1,0:T(8,128)(2,1)S(1)}, u32[]{:S(2)}, u32[]{:S(2)}) %collective-permute-start.22) | collective-permute-done | bytes 65568 | tf_op jit(solution)/shard_map/ppermute | solution.py:626
  (86 shorter events, 26.3 us)
Async XLA Ops:
  2.7 19.1 %collective-permute-start.6 = (bf16[8,192,128]{2,1,0:T(8,128)(2,1)}, bf16[8,192,128]{2,1,0:T(8,128)(2,1)S(1)}, u32[]{:S(2)}, u32[]{:S(2)}) collective-permute-start(bf16[8,192,128]{2,1,0:T(8,128)(2,1)} %get-tuple-element.51.k_hbm.mine_hbm), channel_id=1, source_target_pairs={{0,32},{16,48},{32,64},{48,80},{64,96},{80,112},{96,128},{112,144}... | collective-permute-start | bytes 1179656 | tf_op jit(solution)/shard_map/ppermute | solution.py:584
  6.7 10.5 %collective-permute-start = (bf16[8,32,128]{2,1,0:T(8,128)(2,1)}, bf16[8,32,128]{2,1,0:T(8,128)(2,1)S(1)}, u32[]{:S(2)}, u32[]{:S(2)}) collective-permute-start(bf16[8,32,128]{2,1,0:T(8,128)(2,1)} %get-tuple-element.45), channel_id=1, source_target_pairs={{0,0},{16,192},{32,144},{1,1},{17,193},{33,145},{2,2},{18,194},{34... | collective-permute-start | bytes 196616 | tf_op jit(solution)/shard_map/ppermute | solution.py:583
  12.7 6.4 %collective-permute-start.1 = (bf16[8,32,128]{2,1,0:T(8,128)(2,1)}, bf16[8,32,128]{2,1,0:T(8,128)(2,1)S(1)}, u32[]{:S(2)}, u32[]{:S(2)}) collective-permute-start(bf16[8,32,128]{2,1,0:T(8,128)(2,1)} %get-tuple-element.46), channel_id=1, source_target_pairs={{0,32},{16,224},{32,176},{1,33},{17,225},{33,177},{2,34},{18,226},... | collective-permute-start | bytes 196616 | tf_op jit(solution)/shard_map/ppermute | solution.py:583
  14.6 7.2 %collective-permute-start.2 = (bf16[8,32,128]{2,1,0:T(8,128)(2,1)}, bf16[8,32,128]{2,1,0:T(8,128)(2,1)S(1)}, u32[]{:S(2)}, u32[]{:S(2)}) collective-permute-start(bf16[8,32,128]{2,1,0:T(8,128)(2,1)} %get-tuple-element.47), channel_id=1, source_target_pairs={{0,64},{16,16},{32,208},{1,65},{17,17},{33,209},{2,66},{18,18},{34... | collective-permute-start | bytes 196616 | tf_op jit(solution)/shard_map/ppermute | solution.py:583
  22.8 22.7 %all-to-all-start = ((bf16[8,8,32,128]{3,2,1,0:T(8,128)(2,1)}), bf16[8,8,32,128]{3,2,1,0:T(8,128)(2,1)S(1)}, u32[]{:S(2)}, u32[]{:S(2)}) async-start(bf16[8,8,32,128]{3,2,1,0:T(8,128)(2,1)} %broadcast_in_dim.46), calls=%async_computation | async-start | bytes 1048576 | tf_op jit(solution)/shard_map/all_to_all | solution.py:591
  31.9 10.2 %collective-permute-start.7 = (bf16[8,256,128]{2,1,0:T(8,128)(2,1)S(1)}, bf16[8,256,128]{2,1,0:T(8,128)(2,1)S(1)}, u32[]{:S(2)}, u32[]{:S(2)}) collective-permute-start(bf16[8,256,128]{2,1,0:T(8,128)(2,1)S(1)} %fusion), channel_id=1, source_target_pairs={{0,16},{16,0},{32,48},{48,32},{64,80},{80,64},{96,112},{112,96},{1... | collective-permute-start | bytes 1572872 | tf_op jit(solution)/shard_map/ppermute | solution.py:599
  72.2 23.5 %collective-permute-start.19 = (bf16[8,256,128]{2,1,0:T(8,128)(2,1)}, bf16[8,256,128]{2,1,0:T(8,128)(2,1)S(1)}, u32[]{:S(2)}, u32[]{:S(2)}) collective-permute-start(bf16[8,256,128]{2,1,0:T(8,128)(2,1)} %get-tuple-element.78), channel_id=1, source_target_pairs={{0,16},{16,0},{32,48},{48,32},{64,80},{80,64},{96,112},{112,96},{1... | collective-permute-start | bytes 1572872 | tf_op jit(solution)/shard_map/ppermute | solution.py:616
  72.5 10.7 %collective-permute-start.12 = (f32[2,128]{1,0:T(2,128)}, f32[2,128]{1,0:T(2,128)S(1)}, u32[]{:S(2)}, u32[]{:S(2)}) collective-permute-start(f32[2,128]{1,0:T(2,128)} %get-tuple-element.65), channel_id=1, source_target_pairs={{0,3},{1,2},{2,1},{3,0},{4,7},{5,6},{6,5},{7,4},{8,11},{9,10},{10,... | collective-permute-start | bytes 3080 | tf_op jit(solution)/shard_map/ppermute | solution.py:560
  74.1 9.1 %collective-permute-start.11 = (f32[2,128]{1,0:T(2,128)}, f32[2,128]{1,0:T(2,128)S(1)}, u32[]{:S(2)}, u32[]{:S(2)}) collective-permute-start(f32[2,128]{1,0:T(2,128)} %get-tuple-element.65), channel_id=1, source_target_pairs={{0,2},{1,3},{2,0},{3,1},{4,6},{5,7},{6,4},{7,5},{8,10},{9,11},{10,... | collective-permute-start | bytes 3080 | tf_op jit(solution)/shard_map/ppermute | solution.py:560
  75.0 8.2 %collective-permute-start.10 = (f32[2,128]{1,0:T(2,128)}, f32[2,128]{1,0:T(2,128)S(1)}, u32[]{:S(2)}, u32[]{:S(2)}) collective-permute-start(f32[2,128]{1,0:T(2,128)} %get-tuple-element.65), channel_id=1, source_target_pairs={{0,1},{1,0},{2,3},{3,2},{4,5},{5,4},{6,7},{7,6},{8,9},{9,8},{10,11... | collective-permute-start | bytes 3080 | tf_op jit(solution)/shard_map/ppermute | solution.py:560
  78.6 20.5 %all-to-all-start.1 = ((bf16[8,8,32,128]{3,2,1,0:T(8,128)(2,1)}), bf16[8,8,32,128]{3,2,1,0:T(8,128)(2,1)S(1)}, u32[]{:S(2)}, u32[]{:S(2)}) async-start(bf16[8,8,32,128]{3,2,1,0:T(8,128)(2,1)} %add.68), calls=%async_computation.1 | async-start | bytes 1048576 | tf_op jit(solution)/shard_map/all_to_all | solution.py:591
  83.3 10.4 %collective-permute-start.15 = (f32[2,128]{1,0:T(2,128)S(1)}, f32[2,128]{1,0:T(2,128)S(1)}, u32[]{:S(2)}, u32[]{:S(2)}) collective-permute-start(f32[2,128]{1,0:T(2,128)S(1)} %add_add_fusion.4), channel_id=1, source_target_pairs={{0,12},{1,13},{2,14},{3,15},{4,8},{5,9},{6,10},{7,11},{8,4},{9,5},... | collective-permute-start | bytes 3080 | tf_op jit(solution)/shard_map/ppermute | solution.py:560
  85.0 8.7 %collective-permute-start.14 = (f32[2,128]{1,0:T(2,128)S(1)}, f32[2,128]{1,0:T(2,128)S(1)}, u32[]{:S(2)}, u32[]{:S(2)}) collective-permute-start(f32[2,128]{1,0:T(2,128)S(1)} %add_add_fusion.4), channel_id=1, source_target_pairs={{0,8},{1,9},{2,10},{3,11},{4,12},{5,13},{6,14},{7,15},{8,0},{9,1},... | collective-permute-start | bytes 3080 | tf_op jit(solution)/shard_map/ppermute | solution.py:560
  86.1 7.6 %collective-permute-start.13 = (f32[2,128]{1,0:T(2,128)S(1)}, f32[2,128]{1,0:T(2,128)S(1)}, u32[]{:S(2)}, u32[]{:S(2)}) collective-permute-start(f32[2,128]{1,0:T(2,128)S(1)} %add_add_fusion.4), channel_id=1, source_target_pairs={{0,4},{1,5},{2,6},{3,7},{4,0},{5,1},{6,2},{7,3},{8,12},{9,13},{10,... | collective-permute-start | bytes 3080 | tf_op jit(solution)/shard_map/ppermute | solution.py:560
  95.9 19.5 %collective-permute-start.20 = (bf16[8,192,128]{2,1,0:T(8,128)(2,1)S(1)}, bf16[8,192,128]{2,1,0:T(8,128)(2,1)S(1)}, u32[]{:S(2)}, u32[]{:S(2)}) collective-permute-start(bf16[8,192,128]{2,1,0:T(8,128)(2,1)S(1)} %fusion.1), channel_id=1, source_target_pairs={{32,0},{48,16},{64,32},{80,48},{96,64},{112,80},{128,96},{144,112}... | collective-permute-start | bytes 1179656 | tf_op jit(solution)/shard_map/ppermute | solution.py:619
  99.2 7.9 %collective-permute-start.29 = (f32[2,128]{1,0:T(2,128)S(1)}, f32[2,128]{1,0:T(2,128)S(1)}, u32[]{:S(2)}, u32[]{:S(2)}) collective-permute-start(f32[2,128]{1,0:T(2,128)S(1)} %add_add_fusion.2), channel_id=1, source_target_pairs={{0,192},{16,208},{32,224},{48,240},{64,128},{80,144},{96,160},{112... | collective-permute-start | bytes 3080 | tf_op jit(solution)/shard_map/ppermute | solution.py:560
  102.2 10.6 %collective-permute-start.28 = (f32[2,128]{1,0:T(2,128)S(1)}, f32[2,128]{1,0:T(2,128)S(1)}, u32[]{:S(2)}, u32[]{:S(2)}) collective-permute-start(f32[2,128]{1,0:T(2,128)S(1)} %add_add_fusion.2), channel_id=1, source_target_pairs={{0,128},{16,144},{32,160},{48,176},{64,192},{80,208},{96,224},{112... | collective-permute-start | bytes 3080 | tf_op jit(solution)/shard_map/ppermute | solution.py:560
  104.5 9.6 %collective-permute-start.27 = (f32[2,128]{1,0:T(2,128)S(1)}, f32[2,128]{1,0:T(2,128)S(1)}, u32[]{:S(2)}, u32[]{:S(2)}) collective-permute-start(f32[2,128]{1,0:T(2,128)S(1)} %add_add_fusion.2), channel_id=1, source_target_pairs={{0,64},{16,80},{32,96},{48,112},{64,0},{80,16},{96,32},{112,48},{1... | collective-permute-start | bytes 3080 | tf_op jit(solution)/shard_map/ppermute | solution.py:560
  105.8 11.5 %collective-permute-start.26 = (bf16[8,32,128]{2,1,0:T(8,128)(2,1)S(1)}, bf16[8,32,128]{2,1,0:T(8,128)(2,1)S(1)}, u32[]{:S(2)}, u32[]{:S(2)}) collective-permute-start(bf16[8,32,128]{2,1,0:T(8,128)(2,1)S(1)} %reduce_sum.12), channel_id=1, source_target_pairs={{160,0},{112,16},{161,1},{113,17},{162,2},{114,18},{163,3},{115,19... | collective-permute-start | bytes 196616 | tf_op jit(solution)/shard_map/ppermute | solution.py:626
  107.2 12.0 %collective-permute-start.25 = (bf16[8,32,128]{2,1,0:T(8,128)(2,1)S(1)}, bf16[8,32,128]{2,1,0:T(8,128)(2,1)S(1)}, u32[]{:S(2)}, u32[]{:S(2)}) collective-permute-start(bf16[8,32,128]{2,1,0:T(8,128)(2,1)S(1)} %reduce_sum.12), channel_id=1, source_target_pairs={{128,0},{80,16},{129,1},{81,17},{130,2},{82,18},{131,3},{83,19},{1... | collective-permute-start | bytes 196616 | tf_op jit(solution)/shard_map/ppermute | solution.py:626
  112.8 8.4 %collective-permute-start.24 = (bf16[8,32,128]{2,1,0:T(8,128)(2,1)S(1)}, bf16[8,32,128]{2,1,0:T(8,128)(2,1)S(1)}, u32[]{:S(2)}, u32[]{:S(2)}) collective-permute-start(bf16[8,32,128]{2,1,0:T(8,128)(2,1)S(1)} %reduce_sum.12), channel_id=1, source_target_pairs={{96,0},{48,16},{240,32},{97,1},{49,17},{241,33},{98,2},{50,18},{24... | collective-permute-start | bytes 196616 | tf_op jit(solution)/shard_map/ppermute | solution.py:626
  114.1 8.6 %collective-permute-start.23 = (bf16[8,32,128]{2,1,0:T(8,128)(2,1)S(1)}, bf16[8,32,128]{2,1,0:T(8,128)(2,1)S(1)}, u32[]{:S(2)}, u32[]{:S(2)}) collective-permute-start(bf16[8,32,128]{2,1,0:T(8,128)(2,1)S(1)} %reduce_sum.12), channel_id=1, source_target_pairs={{64,0},{16,16},{208,32},{65,1},{17,17},{209,33},{66,2},{18,18},{21... | collective-permute-start | bytes 196616 | tf_op jit(solution)/shard_map/ppermute | solution.py:626
  115.4 9.5 %collective-permute-start.22 = (bf16[8,32,128]{2,1,0:T(8,128)(2,1)S(1)}, bf16[8,32,128]{2,1,0:T(8,128)(2,1)S(1)}, u32[]{:S(2)}, u32[]{:S(2)}) collective-permute-start(bf16[8,32,128]{2,1,0:T(8,128)(2,1)S(1)} %reduce_sum.12), channel_id=1, source_target_pairs={{32,0},{224,16},{176,32},{33,1},{225,17},{177,33},{34,2},{226,18},... | collective-permute-start | bytes 196616 | tf_op jit(solution)/shard_map/ppermute | solution.py:626
  117.3 8.6 %collective-permute-start.21 = (bf16[8,32,128]{2,1,0:T(8,128)(2,1)S(1)}, bf16[8,32,128]{2,1,0:T(8,128)(2,1)S(1)}, u32[]{:S(2)}, u32[]{:S(2)}) collective-permute-start(bf16[8,32,128]{2,1,0:T(8,128)(2,1)S(1)} %reduce_sum.12), channel_id=1, source_target_pairs={{0,0},{192,16},{144,32},{1,1},{193,17},{145,33},{2,2},{194,18},{14... | collective-permute-start | bytes 196616 | tf_op jit(solution)/shard_map/ppermute | solution.py:626
  (18 other events, 195.8 us)

commit v4 on v3

--- a/solution.py
+++ b/solution.py
@@ -620,11 +620,11 @@
     gains = sum_four(gains, "dp", 1)
     gains, out_t, dq_t = lax.optimization_barrier((gains, out_t, dq_t))
     out, dq = finish(q_gain[:, None], angle, out_t, dq_t, unit, factor)
-    gains = sum_four(sum_four(gains, "dp", 4), "seq", 1)
+    gains = sum_four(sum_four(gains, "dp", 4), "seq", 4)
     piece = jnp.sum(parts.astype(F32), axis=0).astype(BF16)
     piece, gains, out, dq = lax.optimization_barrier((piece, gains, out, dq))
     blocks = [lax.ppermute(piece, "seq", [(b, a) for a, b in pairs]) for pairs in routes]
-    gains = sum_four(gains, "seq", 4)
+    gains = sum_four(gains, "seq", 1)
     dk, dv = last(k_gain[None], own_key, own, swap, back, blocks)
     return (out[None], dq[None], dk[None], dv[None], gains[0], gains[1])
 

time: 128 us -> 127 us (level)
  the two profiles are of different devices: /device:TPU:42 before, /device:TPU:1 now
where the time goes in v4:
time: 127 us; the launch traced here: 126 us
  starting transfers between devices  61.6 us (49%)
  Pallas kernels  42.2 us (33%)
  waiting for transfers between devices  12.8 us (10%)
  local copies, waits for them, and re-layouts  5.13 us (4%)
  other arithmetic  2.89 us (2%)
    pallas_call x1, Pallas kernels, attend(): pl.pallas_call(functools.partial(attention_kernel, tile_count), out_shape...  23.6 us
    ppermute x12, starting transfers between devices, sum_four(): lax.ppermute(x, axis, [(i, i ^ n * step) for i in range(size)])  17.6 us
    ppermute x6, starting transfers between devices, per_device(): lax.ppermute(block, 'seq', pairs)  14.5 us
    pallas_call x1, Pallas kernels, prepare(): pl.pallas_call(prepare_kernel, out_shape=[shape(*item) for item in shapes...  9.17 us
    all_to_all x2, starting transfers between devices, exchange(): lax.all_to_all(x, 'seq', split_axis=0, concat_axis=0, tiled=True, axis_in...  8.37 us
    ppermute x6, starting transfers between devices, per_device(): lax.ppermute(piece, 'seq', [(b, a) for a, b in pairs])  7.1 us
    pallas_call x1, Pallas kernels, finish(): pl.pallas_call(finish_kernel, out_shape=(shape(dims), shape(dims)), in_sp...  6.02 us
    ppermute x6, waiting for transfers between devices, per_device(): lax.ppermute(piece, 'seq', [(b, a) for a, b in pairs])  5.88 us
  transfers between devices with their start and end apart: 32, of which 8 were waited for; matrix products, arithmetic and copies ran while one was open for 5% of the time, Pallas kernels for 12%

profile of v4, /device:TPU:1, one launch (start us, length us, event | category | flops | bytes accessed | tf_op | source)
XLA Modules:
  0.0 126.1 jit_solution(8735802088051527561)
XLA Ops:
  0.6 2.0 %pack_keys.1 = (bf16[8,192,128]{2,1,0:T(8,128)(2,1)}, bf16[8,32,128]{2,1,0:T(8,128)(2,1)}, bf16[8,32,128]{2,1,0:T(8,128)(2,1)}, bf16[8,32,128]{2,1,0:T(8,128)(2,...) custom-call(bf16[192,4,128]{2,1,0:T(4,128)(2,1)} %bitcast.25, ...), custom_call_target="tpu_custom_call" | custom-call | flops 1000000 | bytes 2000000 | tf_op jit(solution)/shard_map/pack_keys/pallas_call | solution.py:436
  2.7 4.5 %collective-permute-start.6 = (bf16[8,192,128]{2,1,0:T(8,128)(2,1)}, bf16[8,192,128]{2,1,0:T(8,128)(2,1)S(1)}, u32[]{:S(2)}, u32[]{:S(2)}) collective-permute-start(bf16[8,192,128]{2,1,0:T(8,128)(2,1)} %get-tuple-element.51.k_hbm.mine_hbm), channel_id=1, source_target_pairs={{0,32},{16,48},{32,64},{48,80},{64,96},{80,112},{96,128},{112,144}... | collective-permute-start | bytes 1179656 | tf_op jit(solution)/shard_map/ppermute | solution.py:584
  7.2 7.8 %collective-permute-start = (bf16[8,32,128]{2,1,0:T(8,128)(2,1)}, bf16[8,32,128]{2,1,0:T(8,128)(2,1)S(1)}, u32[]{:S(2)}, u32[]{:S(2)}) collective-permute-start(bf16[8,32,128]{2,1,0:T(8,128)(2,1)} %get-tuple-element.45), channel_id=1, source_target_pairs={{0,0},{16,192},{32,144},{1,1},{17,193},{33,145},{2,2},{18,194},{34... | collective-permute-start | bytes 196616 | tf_op jit(solution)/shard_map/ppermute | solution.py:583
  15.1 1.3 %collective-permute-start.1 = (bf16[8,32,128]{2,1,0:T(8,128)(2,1)}, bf16[8,32,128]{2,1,0:T(8,128)(2,1)S(1)}, u32[]{:S(2)}, u32[]{:S(2)}) collective-permute-start(bf16[8,32,128]{2,1,0:T(8,128)(2,1)} %get-tuple-element.46), channel_id=1, source_target_pairs={{0,32},{16,224},{32,176},{1,33},{17,225},{33,177},{2,34},{18,226},... | collective-permute-start | bytes 196616 | tf_op jit(solution)/shard_map/ppermute | solution.py:583
  16.4 1.5 %collective-permute-start.2 = (bf16[8,32,128]{2,1,0:T(8,128)(2,1)}, bf16[8,32,128]{2,1,0:T(8,128)(2,1)S(1)}, u32[]{:S(2)}, u32[]{:S(2)}) collective-permute-start(bf16[8,32,128]{2,1,0:T(8,128)(2,1)} %get-tuple-element.47), channel_id=1, source_target_pairs={{0,64},{16,16},{32,208},{1,65},{17,17},{33,209},{2,66},{18,18},{34... | collective-permute-start | bytes 196616 | tf_op jit(solution)/shard_map/ppermute | solution.py:583
  22.5 1.4 %copy.20.gain_ref = f32[128,1]{1,0:T(8,128)} copy(f32[128,1]{0,1:T(1,128)} %bitcast.31) | data formatting | bytes 1024 | tf_op jit(solution)/shard_map/broadcast_in_dim | solution.py:604
  25.0 4.9 %all-to-all-start = ((bf16[8,8,32,128]{3,2,1,0:T(8,128)(2,1)}), bf16[8,8,32,128]{3,2,1,0:T(8,128)(2,1)S(1)}, u32[]{:S(2)}, u32[]{:S(2)}) async-start(bf16[8,8,32,128]{3,2,1,0:T(8,128)(2,1)} %broadcast_in_dim.46), calls=%async_computation | async-start | bytes 1048576 | tf_op jit(solution)/shard_map/all_to_all | solution.py:591
  30.0 3.4 %collective-permute-start.7 = (bf16[8,256,128]{2,1,0:T(8,128)(2,1)S(1)}, bf16[8,256,128]{2,1,0:T(8,128)(2,1)S(1)}, u32[]{:S(2)}, u32[]{:S(2)}) collective-permute-start(bf16[8,256,128]{2,1,0:T(8,128)(2,1)S(1)} %fusion), channel_id=1, source_target_pairs={{0,16},{16,0},{32,48},{48,32},{64,80},{80,64},{96,112},{112,96},{1... | collective-permute-start | bytes 1572872 | tf_op jit(solution)/shard_map/ppermute | solution.py:599
  34.2 9.2 %prepare_queries.1 = (bf16[4,768,128]{2,1,0:T(8,128)(2,1)}, bf16[4,128,768]{2,1,0:T(8,128)(2,1)}, bf16[4,768,128]{2,1,0:T(8,128)(2,1)}, bf16[4,128,768]{2,1,0:T(...) custom-call(s32[24]{0:T(128)} %fusion.8.place_ref, ...), custom_call_target="tpu_custom_call" | custom-call | flops 100000000 | bytes 16000000 | tf_op jit(solution)/shard_map/prepare_queries/pallas_call | solution.py:459
  44.0 4.3 %collective-permute-start.8 = (bf16[8,8,32,128]{3,2,1,0:T(8,128)(2,1)S(1)}, bf16[8,8,32,128]{3,2,1,0:T(8,128)(2,1)S(1)}, u32[]{:S(2)}, u32[]{:S(2)}) collective-permute-start(bf16[8,8,32,128]{3,2,1,0:T(8,128)(2,1)S(1)} %all-to-all-done.parts_hbm), channel_id=1, source_target_pairs={{0,16},{16,0},{32,48},{48,32},{64,80},{80,64},{96,112},{112,96},{1... | collective-permute-start | bytes 1572872 | tf_op jit(solution)/shard_map/ppermute | solution.py:608
  50.6 23.6 %tree_attention.1 = (bf16[4,128,768]{2,1,0:T(8,128)(2,1)}, bf16[4,128,768]{2,1,0:T(8,128)(2,1)}, f32[2,128]{1,0:T(2,128)}, bf16[8,8,32,128]{3,2,1,0:T(8,128)(2,1...) custom-call(s32[576]{0:T(1024)} %reshape.21.table_ref, ...), custom_call_target="tpu_custom_call" | custom-call | flops 5435817984 | bytes 12000000 | tf_op jit(solution)/shard_map/tree_attention/pallas_call | solution.py:483
  74.9 2.7 %collective-permute-start.12 = (f32[2,128]{1,0:T(2,128)}, f32[2,128]{1,0:T(2,128)S(1)}, u32[]{:S(2)}, u32[]{:S(2)}) collective-permute-start(f32[2,128]{1,0:T(2,128)} %get-tuple-element.65), channel_id=1, source_target_pairs={{0,3},{1,2},{2,1},{3,0},{4,7},{5,6},{6,5},{7,4},{8,11},{9,10},{10,... | collective-permute-start | bytes 3080 | tf_op jit(solution)/shard_map/ppermute | solution.py:560
  78.2 2.0 %add.68 = bf16[8,8,32,128]{3,2,1,0:T(8,128)(2,1)} add(bf16[8,8,32,128]{3,2,1,0:T(8,128)(2,1)} %get-tuple-element.63, bf16[8,8,32,128]{3,2,1,0:T(8,128)(2,1)S(1)} %collective-permute-done.9) | non-fusion elementwise | flops 262144 | bytes 1572864 | tf_op jit(solution)/shard_map/add | solution.py:615
  80.2 3.5 %all-to-all-start.1 = ((bf16[8,8,32,128]{3,2,1,0:T(8,128)(2,1)}), bf16[8,8,32,128]{3,2,1,0:T(8,128)(2,1)S(1)}, u32[]{:S(2)}, u32[]{:S(2)}) async-start(bf16[8,8,32,128]{3,2,1,0:T(8,128)(2,1)} %add.68), calls=%async_computation.1 | async-start | bytes 1048576 | tf_op jit(solution)/shard_map/all_to_all | solution.py:591
  83.7 2.7 %collective-permute-start.15 = (f32[2,128]{1,0:T(2,128)S(1)}, f32[2,128]{1,0:T(2,128)S(1)}, u32[]{:S(2)}, u32[]{:S(2)}) collective-permute-start(f32[2,128]{1,0:T(2,128)S(1)} %add_add_fusion.4), channel_id=1, source_target_pairs={{0,12},{1,13},{2,14},{3,15},{4,8},{5,9},{6,10},{7,11},{8,4},{9,5},... | collective-permute-start | bytes 3080 | tf_op jit(solution)/shard_map/ppermute | solution.py:560
  87.3 6.0 %finish_queries.1 = (bf16[192,16,128]{2,1,0:T(8,128)(2,1)}, bf16[192,16,128]{2,1,0:T(8,128)(2,1)}) custom-call(f32[128,1]{1,0:T(8,128)} %copy.20.gain_ref, f32[2,128,768]{2,1,0:T(8,128)} %get-tuple-element.60.angle_hbm, bf16[4,128,768]{2,1,0:T(8,128)(2,1)} %get-tuple-element.69.out_t_hbm, bf16[4,128,768]{2,1,0:T(8,128)(2,1)} %get-tuple-element.70.dq_t_hbm, ...), custom_call_target="tpu_custom_call" | custom-call | flops 100000000 | bytes 10000000 | tf_op jit(solution)/shard_map/finish_queries/pallas_call | solution.py:515
  93.4 3.6 %collective-permute-start.18 = (f32[2,128]{1,0:T(2,128)S(1)}, f32[2,128]{1,0:T(2,128)S(1)}, u32[]{:S(2)}, u32[]{:S(2)}) collective-permute-start(f32[2,128]{1,0:T(2,128)S(1)} %add_add_fusion.3), channel_id=1, source_target_pairs={{0,192},{16,208},{32,224},{48,240},{64,128},{80,144},{96,160},{112... | collective-permute-start | bytes 3080 | tf_op jit(solution)/shard_map/ppermute | solution.py:560
  96.9 2.1 %collective-permute-start.17 = (f32[2,128]{1,0:T(2,128)S(1)}, f32[2,128]{1,0:T(2,128)S(1)}, u32[]{:S(2)}, u32[]{:S(2)}) collective-permute-start(f32[2,128]{1,0:T(2,128)S(1)} %add_add_fusion.3), channel_id=1, source_target_pairs={{0,128},{16,144},{32,160},{48,176},{64,192},{80,208},{96,224},{112... | collective-permute-start | bytes 3080 | tf_op jit(solution)/shard_map/ppermute | solution.py:560
  100.6 2.7 %collective-permute-done.17 = f32[2,128]{1,0:T(2,128)S(1)} collective-permute-done((f32[2,128]{1,0:T(2,128)S(1)}, f32[2,128]{1,0:T(2,128)S(1)}, u32[]{:S(2)}, u32[]{:S(2)}) %collective-permute-start.17) | collective-permute-done | bytes 1056 | tf_op jit(solution)/shard_map/ppermute | solution.py:560
  103.4 4.1 %collective-permute-start.29 = (f32[2,128]{1,0:T(2,128)S(1)}, f32[2,128]{1,0:T(2,128)S(1)}, u32[]{:S(2)}, u32[]{:S(2)}) collective-permute-start(f32[2,128]{1,0:T(2,128)S(1)} %add_add_fusion.2), channel_id=1, source_target_pairs={{0,48},{16,32},{32,16},{48,0},{64,112},{80,96},{96,80},{112,64},{1... | collective-permute-start | bytes 3080 | tf_op jit(solution)/shard_map/ppermute | solution.py:560
  109.7 2.7 %collective-permute-done.29 = f32[2,128]{1,0:T(2,128)S(1)} collective-permute-done((f32[2,128]{1,0:T(2,128)S(1)}, f32[2,128]{1,0:T(2,128)S(1)}, u32[]{:S(2)}, u32[]{:S(2)}) %collective-permute-start.29) | collective-permute-done | bytes 1056 | tf_op jit(solution)/shard_map/ppermute | solution.py:560
  119.3 3.2 %collective-permute-done.22.rest_1_ = bf16[8,32,128]{2,1,0:T(8,128)(2,1)S(1)} collective-permute-done((bf16[8,32,128]{2,1,0:T(8,128)(2,1)S(1)}, bf16[8,32,128]{2,1,0:T(8,128)(2,1)S(1)}, u32[]{:S(2)}, u32[]{:S(2)}) %collective-permute-start.22) | collective-permute-done | bytes 65568 | tf_op jit(solution)/shard_map/ppermute | solution.py:626
  122.5 2.2 %collective-permute-done.21.rest_0_ = bf16[8,32,128]{2,1,0:T(8,128)(2,1)S(1)} collective-permute-done((bf16[8,32,128]{2,1,0:T(8,128)(2,1)S(1)}, bf16[8,32,128]{2,1,0:T(8,128)(2,1)S(1)}, u32[]{:S(2)}, u32[]{:S(2)}) %collective-permute-start.21) | collective-permute-done | bytes 65568 | tf_op jit(solution)/shard_map/ppermute | solution.py:626
  124.7 1.4 %finish_keys.1 = (bf16[192,4,128]{2,1,0:T(4,128)(2,1)}, bf16[192,4,128]{2,1,0:T(4,128)(2,1)}) custom-call(f32[1,128]{1,0:T(1,128)S(1)} %bitcast.22, f32[10,192,128]{2,1,0:T(8,128)S(1)} %copy-done, bf16[8,192,128]{2,1,0:T(8,128)(2,1)S(1)} %copy-done.1, bf16[8,256,128]{2,1,0:T(8,128)(2,1)S(1)} %collective-permute-done.19.swap_ref, ...), custom_call_target="tpu_custom_call" | custom-call | flops 1000000 | bytes 4000000 | tf_op jit(solution)/shard_map/finish_keys/pallas_call | solution.py:531
  (86 shorter events, 22.3 us)
Async XLA Ops:
  2.7 21.3 %collective-permute-start.6 = (bf16[8,192,128]{2,1,0:T(8,128)(2,1)}, bf16[8,192,128]{2,1,0:T(8,128)(2,1)S(1)}, u32[]{:S(2)}, u32[]{:S(2)}) collective-permute-start(bf16[8,192,128]{2,1,0:T(8,128)(2,1)} %get-tuple-element.51.k_hbm.mine_hbm), channel_id=1, source_target_pairs={{0,32},{16,48},{32,64},{48,80},{64,96},{80,112},{96,128},{112,144}... | collective-permute-start | bytes 1179656 | tf_op jit(solution)/shard_map/ppermute | solution.py:584
  7.2 11.9 %collective-permute-start = (bf16[8,32,128]{2,1,0:T(8,128)(2,1)}, bf16[8,32,128]{2,1,0:T(8,128)(2,1)S(1)}, u32[]{:S(2)}, u32[]{:S(2)}) collective-permute-start(bf16[8,32,128]{2,1,0:T(8,128)(2,1)} %get-tuple-element.45), channel_id=1, source_target_pairs={{0,0},{16,192},{32,144},{1,1},{17,193},{33,145},{2,2},{18,194},{34... | collective-permute-start | bytes 196616 | tf_op jit(solution)/shard_map/ppermute | solution.py:583
  16.4 7.5 %collective-permute-start.2 = (bf16[8,32,128]{2,1,0:T(8,128)(2,1)}, bf16[8,32,128]{2,1,0:T(8,128)(2,1)S(1)}, u32[]{:S(2)}, u32[]{:S(2)}) collective-permute-start(bf16[8,32,128]{2,1,0:T(8,128)(2,1)} %get-tuple-element.47), channel_id=1, source_target_pairs={{0,64},{16,16},{32,208},{1,65},{17,17},{33,209},{2,66},{18,18},{34... | collective-permute-start | bytes 196616 | tf_op jit(solution)/shard_map/ppermute | solution.py:583
  17.9 6.0 %collective-permute-start.3 = (bf16[8,32,128]{2,1,0:T(8,128)(2,1)}, bf16[8,32,128]{2,1,0:T(8,128)(2,1)S(1)}, u32[]{:S(2)}, u32[]{:S(2)}) collective-permute-start(bf16[8,32,128]{2,1,0:T(8,128)(2,1)} %get-tuple-element.48), channel_id=1, source_target_pairs={{0,96},{16,48},{32,240},{1,97},{17,49},{33,241},{2,98},{18,50},{34... | collective-permute-start | bytes 196616 | tf_op jit(solution)/shard_map/ppermute | solution.py:583
  25.0 19.1 %all-to-all-start = ((bf16[8,8,32,128]{3,2,1,0:T(8,128)(2,1)}), bf16[8,8,32,128]{3,2,1,0:T(8,128)(2,1)S(1)}, u32[]{:S(2)}, u32[]{:S(2)}) async-start(bf16[8,8,32,128]{3,2,1,0:T(8,128)(2,1)} %broadcast_in_dim.46), calls=%async_computation | async-start | bytes 1048576 | tf_op jit(solution)/shard_map/all_to_all | solution.py:591
  30.0 13.4 %collective-permute-start.7 = (bf16[8,256,128]{2,1,0:T(8,128)(2,1)S(1)}, bf16[8,256,128]{2,1,0:T(8,128)(2,1)S(1)}, u32[]{:S(2)}, u32[]{:S(2)}) collective-permute-start(bf16[8,256,128]{2,1,0:T(8,128)(2,1)S(1)} %fusion), channel_id=1, source_target_pairs={{0,16},{16,0},{32,48},{48,32},{64,80},{80,64},{96,112},{112,96},{1... | collective-permute-start | bytes 1572872 | tf_op jit(solution)/shard_map/ppermute | solution.py:599
  44.0 5.8 %collective-permute-start.8 = (bf16[8,8,32,128]{3,2,1,0:T(8,128)(2,1)S(1)}, bf16[8,8,32,128]{3,2,1,0:T(8,128)(2,1)S(1)}, u32[]{:S(2)}, u32[]{:S(2)}) collective-permute-start(bf16[8,8,32,128]{3,2,1,0:T(8,128)(2,1)S(1)} %all-to-all-done.parts_hbm), channel_id=1, source_target_pairs={{0,16},{16,0},{32,48},{48,32},{64,80},{80,64},{96,112},{112,96},{1... | collective-permute-start | bytes 1572872 | tf_op jit(solution)/shard_map/ppermute | solution.py:608
  74.6 24.5 %collective-permute-start.19 = (bf16[8,256,128]{2,1,0:T(8,128)(2,1)}, bf16[8,256,128]{2,1,0:T(8,128)(2,1)S(1)}, u32[]{:S(2)}, u32[]{:S(2)}) collective-permute-start(bf16[8,256,128]{2,1,0:T(8,128)(2,1)} %get-tuple-element.78), channel_id=1, source_target_pairs={{0,16},{16,0},{32,48},{48,32},{64,80},{80,64},{96,112},{112,96},{1... | collective-permute-start | bytes 1572872 | tf_op jit(solution)/shard_map/ppermute | solution.py:616
  74.9 8.8 %collective-permute-start.12 = (f32[2,128]{1,0:T(2,128)}, f32[2,128]{1,0:T(2,128)S(1)}, u32[]{:S(2)}, u32[]{:S(2)}) collective-permute-start(f32[2,128]{1,0:T(2,128)} %get-tuple-element.65), channel_id=1, source_target_pairs={{0,3},{1,2},{2,1},{3,0},{4,7},{5,6},{6,5},{7,4},{8,11},{9,10},{10,... | collective-permute-start | bytes 3080 | tf_op jit(solution)/shard_map/ppermute | solution.py:560
  77.6 6.1 %collective-permute-start.11 = (f32[2,128]{1,0:T(2,128)}, f32[2,128]{1,0:T(2,128)S(1)}, u32[]{:S(2)}, u32[]{:S(2)}) collective-permute-start(f32[2,128]{1,0:T(2,128)} %get-tuple-element.65), channel_id=1, source_target_pairs={{0,2},{1,3},{2,0},{3,1},{4,6},{5,7},{6,4},{7,5},{8,10},{9,11},{10,... | collective-permute-start | bytes 3080 | tf_op jit(solution)/shard_map/ppermute | solution.py:560
  80.2 23.1 %all-to-all-start.1 = ((bf16[8,8,32,128]{3,2,1,0:T(8,128)(2,1)}), bf16[8,8,32,128]{3,2,1,0:T(8,128)(2,1)S(1)}, u32[]{:S(2)}, u32[]{:S(2)}) async-start(bf16[8,8,32,128]{3,2,1,0:T(8,128)(2,1)} %add.68), calls=%async_computation.1 | async-start | bytes 1048576 | tf_op jit(solution)/shard_map/all_to_all | solution.py:591
  83.7 9.6 %collective-permute-start.15 = (f32[2,128]{1,0:T(2,128)S(1)}, f32[2,128]{1,0:T(2,128)S(1)}, u32[]{:S(2)}, u32[]{:S(2)}) collective-permute-start(f32[2,128]{1,0:T(2,128)S(1)} %add_add_fusion.4), channel_id=1, source_target_pairs={{0,12},{1,13},{2,14},{3,15},{4,8},{5,9},{6,10},{7,11},{8,4},{9,5},... | collective-permute-start | bytes 3080 | tf_op jit(solution)/shard_map/ppermute | solution.py:560
  86.5 6.8 %collective-permute-start.14 = (f32[2,128]{1,0:T(2,128)S(1)}, f32[2,128]{1,0:T(2,128)S(1)}, u32[]{:S(2)}, u32[]{:S(2)}) collective-permute-start(f32[2,128]{1,0:T(2,128)S(1)} %add_add_fusion.4), channel_id=1, source_target_pairs={{0,8},{1,9},{2,10},{3,11},{4,12},{5,13},{6,14},{7,15},{8,0},{9,1},... | collective-permute-start | bytes 3080 | tf_op jit(solution)/shard_map/ppermute | solution.py:560
  87.0 6.3 %collective-permute-start.13 = (f32[2,128]{1,0:T(2,128)S(1)}, f32[2,128]{1,0:T(2,128)S(1)}, u32[]{:S(2)}, u32[]{:S(2)}) collective-permute-start(f32[2,128]{1,0:T(2,128)S(1)} %add_add_fusion.4), channel_id=1, source_target_pairs={{0,4},{1,5},{2,6},{3,7},{4,0},{5,1},{6,2},{7,3},{8,12},{9,13},{10,... | collective-permute-start | bytes 3080 | tf_op jit(solution)/shard_map/ppermute | solution.py:560
  93.4 7.2 %collective-permute-start.18 = (f32[2,128]{1,0:T(2,128)S(1)}, f32[2,128]{1,0:T(2,128)S(1)}, u32[]{:S(2)}, u32[]{:S(2)}) collective-permute-start(f32[2,128]{1,0:T(2,128)S(1)} %add_add_fusion.3), channel_id=1, source_target_pairs={{0,192},{16,208},{32,224},{48,240},{64,128},{80,144},{96,160},{112... | collective-permute-start | bytes 3080 | tf_op jit(solution)/shard_map/ppermute | solution.py:560
  96.9 6.3 %collective-permute-start.17 = (f32[2,128]{1,0:T(2,128)S(1)}, f32[2,128]{1,0:T(2,128)S(1)}, u32[]{:S(2)}, u32[]{:S(2)}) collective-permute-start(f32[2,128]{1,0:T(2,128)S(1)} %add_add_fusion.3), channel_id=1, source_target_pairs={{0,128},{16,144},{32,160},{48,176},{64,192},{80,208},{96,224},{112... | collective-permute-start | bytes 3080 | tf_op jit(solution)/shard_map/ppermute | solution.py:560
  99.3 16.4 %collective-permute-start.20 = (bf16[8,192,128]{2,1,0:T(8,128)(2,1)S(1)}, bf16[8,192,128]{2,1,0:T(8,128)(2,1)S(1)}, u32[]{:S(2)}, u32[]{:S(2)}) collective-permute-start(bf16[8,192,128]{2,1,0:T(8,128)(2,1)S(1)} %fusion.1), channel_id=1, source_target_pairs={{32,0},{48,16},{64,32},{80,48},{96,64},{112,80},{128,96},{144,112}... | collective-permute-start | bytes 1179656 | tf_op jit(solution)/shard_map/ppermute | solution.py:619
  103.4 9.0 %collective-permute-start.29 = (f32[2,128]{1,0:T(2,128)S(1)}, f32[2,128]{1,0:T(2,128)S(1)}, u32[]{:S(2)}, u32[]{:S(2)}) collective-permute-start(f32[2,128]{1,0:T(2,128)S(1)} %add_add_fusion.2), channel_id=1, source_target_pairs={{0,48},{16,32},{32,16},{48,0},{64,112},{80,96},{96,80},{112,64},{1... | collective-permute-start | bytes 3080 | tf_op jit(solution)/shard_map/ppermute | solution.py:560
  107.4 6.2 %collective-permute-start.28 = (f32[2,128]{1,0:T(2,128)S(1)}, f32[2,128]{1,0:T(2,128)S(1)}, u32[]{:S(2)}, u32[]{:S(2)}) collective-permute-start(f32[2,128]{1,0:T(2,128)S(1)} %add_add_fusion.2), channel_id=1, source_target_pairs={{0,32},{16,48},{32,0},{48,16},{64,96},{80,112},{96,64},{112,80},{1... | collective-permute-start | bytes 3080 | tf_op jit(solution)/shard_map/ppermute | solution.py:560
  108.4 6.6 %collective-permute-start.27 = (f32[2,128]{1,0:T(2,128)S(1)}, f32[2,128]{1,0:T(2,128)S(1)}, u32[]{:S(2)}, u32[]{:S(2)}) collective-permute-start(f32[2,128]{1,0:T(2,128)S(1)} %add_add_fusion.2), channel_id=1, source_target_pairs={{0,16},{16,0},{32,48},{48,32},{64,80},{80,64},{96,112},{112,96},{1... | collective-permute-start | bytes 3080 | tf_op jit(solution)/shard_map/ppermute | solution.py:560
  108.4 8.6 %collective-permute-start.26 = (bf16[8,32,128]{2,1,0:T(8,128)(2,1)S(1)}, bf16[8,32,128]{2,1,0:T(8,128)(2,1)S(1)}, u32[]{:S(2)}, u32[]{:S(2)}) collective-permute-start(bf16[8,32,128]{2,1,0:T(8,128)(2,1)S(1)} %reduce_sum.12), channel_id=1, source_target_pairs={{160,0},{112,16},{161,1},{113,17},{162,2},{114,18},{163,3},{115,19... | collective-permute-start | bytes 196616 | tf_op jit(solution)/shard_map/ppermute | solution.py:626
  112.4 6.4 %collective-permute-start.25 = (bf16[8,32,128]{2,1,0:T(8,128)(2,1)S(1)}, bf16[8,32,128]{2,1,0:T(8,128)(2,1)S(1)}, u32[]{:S(2)}, u32[]{:S(2)}) collective-permute-start(bf16[8,32,128]{2,1,0:T(8,128)(2,1)S(1)} %reduce_sum.12), channel_id=1, source_target_pairs={{128,0},{80,16},{129,1},{81,17},{130,2},{82,18},{131,3},{83,19},{1... | collective-permute-start | bytes 196616 | tf_op jit(solution)/shard_map/ppermute | solution.py:626
  115.7 6.8 %collective-permute-start.22 = (bf16[8,32,128]{2,1,0:T(8,128)(2,1)S(1)}, bf16[8,32,128]{2,1,0:T(8,128)(2,1)S(1)}, u32[]{:S(2)}, u32[]{:S(2)}) collective-permute-start(bf16[8,32,128]{2,1,0:T(8,128)(2,1)S(1)} %reduce_sum.12), channel_id=1, source_target_pairs={{32,0},{224,16},{176,32},{33,1},{225,17},{177,33},{34,2},{226,18},... | collective-permute-start | bytes 196616 | tf_op jit(solution)/shard_map/ppermute | solution.py:626
  117.0 7.7 %collective-permute-start.21 = (bf16[8,32,128]{2,1,0:T(8,128)(2,1)S(1)}, bf16[8,32,128]{2,1,0:T(8,128)(2,1)S(1)}, u32[]{:S(2)}, u32[]{:S(2)}) collective-permute-start(bf16[8,32,128]{2,1,0:T(8,128)(2,1)S(1)} %reduce_sum.12), channel_id=1, source_target_pairs={{0,0},{192,16},{144,32},{1,1},{193,17},{145,33},{2,2},{194,18},{14... | collective-permute-start | bytes 196616 | tf_op jit(solution)/shard_map/ppermute | solution.py:626
  (18 other events, 199.2 us)

commit v5 on v4

--- a/solution.py
+++ b/solution.py
@@ -369,16 +369,23 @@
     gain_ref, angle_hbm, out_t_hbm, dq_t_hbm, unit_hbm, factor_hbm, out_ref, dq_ref, os_, dqs,
     angle_ref, out_t_ref, dq_t_ref, unit_ref, factor_ref, in_sem,
 ):
-    load_all(
-        [
-            (out_t_hbm, out_t_ref), (dq_t_hbm, dq_t_ref), (unit_hbm, unit_ref), (angle_hbm, angle_ref),
-            (factor_hbm, factor_ref),
-        ],
-        in_sem,
-    )
+    pairs = [(out_t_hbm, out_t_ref), (dq_t_hbm, dq_t_ref), (unit_hbm, unit_ref), (factor_hbm, factor_ref)]
+
+    def load(n, g):
+        source, target = pairs[n]
+        return pltpu.make_async_copy(source.at[g], target.at[g], in_sem.at[1 + n * KV + g])
+
+    angles = pltpu.make_async_copy(angle_hbm, angle_ref, in_sem.at[0])
+    angles.start()
+    for g in range(KV):
+        for n in range(len(pairs)):
+            load(n, g).start()
+    angles.wait()
     gain = gain_ref[...]
 
     def per_kv(g, carry):
+        for n in range(len(pairs)):
+            load(n, g).wait()
         for i in range(BLOCKS):
             span = slice(i * COLS, (i + 1) * COLS)
             out = out_t_ref[g, :, span].astype(F32).T
@@ -519,7 +526,7 @@
         out_specs=(VMEM,) * 2,
         scratch_shapes=[pltpu.VMEM((LOCAL * HEADS, WIDTH), F32)] * 2
         + [pltpu.VMEM(item.shape, item.dtype) for item in (angle, out_t, dq_t, unit, factor)]
-        + [pltpu.SemaphoreType.DMA((5,))],
+        + [pltpu.SemaphoreType.DMA((1 + 4 * KV,))],
         compiler_params=params(56),
         cost_estimate=cost(100_000_000, 10_000_000),
         name="finish_queries",

time: 127 us -> 126 us (level)
  no operation moved by 1% of the time
where the time goes in v5:
time: 126 us; the launch traced here: 125 us
  starting transfers between devices  61.6 us (49%)
  Pallas kernels  41.6 us (33%)
  waiting for transfers between devices  12.8 us (10%)
  local copies, waits for them, and re-layouts  5.13 us (4%)
  other arithmetic  2.89 us (2%)
    pallas_call x1, Pallas kernels, attend(): pl.pallas_call(functools.partial(attention_kernel, tile_count), out_shape...  23.6 us
    ppermute x12, starting transfers between devices, sum_four(): lax.ppermute(x, axis, [(i, i ^ n * step) for i in range(size)])  17.6 us
    ppermute x6, starting transfers between devices, per_device(): lax.ppermute(block, 'seq', pairs)  14.5 us
    pallas_call x1, Pallas kernels, prepare(): pl.pallas_call(prepare_kernel, out_shape=[shape(*item) for item in shapes...  9.17 us
    all_to_all x2, starting transfers between devices, exchange(): lax.all_to_all(x, 'seq', split_axis=0, concat_axis=0, tiled=True, axis_in...  8.37 us
    ppermute x6, starting transfers between devices, per_device(): lax.ppermute(piece, 'seq', [(b, a) for a, b in pairs])  7.1 us
    ppermute x6, waiting for transfers between devices, per_device(): lax.ppermute(piece, 'seq', [(b, a) for a, b in pairs])  5.88 us
    pallas_call x1, Pallas kernels, finish(): pl.pallas_call(finish_kernel, out_shape=(shape(dims), shape(dims)), in_sp...  5.38 us
  transfers between devices with their start and end apart: 32, of which 8 were waited for; matrix products, arithmetic and copies ran while one was open for 5% of the time, Pallas kernels for 12%

profile of v5, /device:TPU:1, one launch (start us, length us, event | category | flops | bytes accessed | tf_op | source)
XLA Modules:
  0.0 125.4 jit_solution(1916714622355157448)
XLA Ops:
  0.6 2.0 %pack_keys.1 = (bf16[8,192,128]{2,1,0:T(8,128)(2,1)}, bf16[8,32,128]{2,1,0:T(8,128)(2,1)}, bf16[8,32,128]{2,1,0:T(8,128)(2,1)}, bf16[8,32,128]{2,1,0:T(8,128)(2,...) custom-call(bf16[192,4,128]{2,1,0:T(4,128)(2,1)} %bitcast.25, ...), custom_call_target="tpu_custom_call" | custom-call | flops 1000000 | bytes 2000000 | tf_op jit(solution)/shard_map/pack_keys/pallas_call | solution.py:443
  2.7 4.5 %collective-permute-start.6 = (bf16[8,192,128]{2,1,0:T(8,128)(2,1)}, bf16[8,192,128]{2,1,0:T(8,128)(2,1)S(1)}, u32[]{:S(2)}, u32[]{:S(2)}) collective-permute-start(bf16[8,192,128]{2,1,0:T(8,128)(2,1)} %get-tuple-element.51.k_hbm.mine_hbm), channel_id=1, source_target_pairs={{0,32},{16,48},{32,64},{48,80},{64,96},{80,112},{96,128},{112,144}... | collective-permute-start | bytes 1179656 | tf_op jit(solution)/shard_map/ppermute | solution.py:591
  7.2 7.8 %collective-permute-start = (bf16[8,32,128]{2,1,0:T(8,128)(2,1)}, bf16[8,32,128]{2,1,0:T(8,128)(2,1)S(1)}, u32[]{:S(2)}, u32[]{:S(2)}) collective-permute-start(bf16[8,32,128]{2,1,0:T(8,128)(2,1)} %get-tuple-element.45), channel_id=1, source_target_pairs={{0,0},{16,192},{32,144},{1,1},{17,193},{33,145},{2,2},{18,194},{34... | collective-permute-start | bytes 196616 | tf_op jit(solution)/shard_map/ppermute | solution.py:590
  15.1 1.3 %collective-permute-start.1 = (bf16[8,32,128]{2,1,0:T(8,128)(2,1)}, bf16[8,32,128]{2,1,0:T(8,128)(2,1)S(1)}, u32[]{:S(2)}, u32[]{:S(2)}) collective-permute-start(bf16[8,32,128]{2,1,0:T(8,128)(2,1)} %get-tuple-element.46), channel_id=1, source_target_pairs={{0,32},{16,224},{32,176},{1,33},{17,225},{33,177},{2,34},{18,226},... | collective-permute-start | bytes 196616 | tf_op jit(solution)/shard_map/ppermute | solution.py:590
  16.4 1.5 %collective-permute-start.2 = (bf16[8,32,128]{2,1,0:T(8,128)(2,1)}, bf16[8,32,128]{2,1,0:T(8,128)(2,1)S(1)}, u32[]{:S(2)}, u32[]{:S(2)}) collective-permute-start(bf16[8,32,128]{2,1,0:T(8,128)(2,1)} %get-tuple-element.47), channel_id=1, source_target_pairs={{0,64},{16,16},{32,208},{1,65},{17,17},{33,209},{2,66},{18,18},{34... | collective-permute-start | bytes 196616 | tf_op jit(solution)/shard_map/ppermute | solution.py:590
  22.5 1.4 %copy.20.gain_ref = f32[128,1]{1,0:T(8,128)} copy(f32[128,1]{0,1:T(1,128)} %bitcast.31) | data formatting | bytes 1024 | tf_op jit(solution)/shard_map/broadcast_in_dim | solution.py:611
  25.0 4.9 %all-to-all-start = ((bf16[8,8,32,128]{3,2,1,0:T(8,128)(2,1)}), bf16[8,8,32,128]{3,2,1,0:T(8,128)(2,1)S(1)}, u32[]{:S(2)}, u32[]{:S(2)}) async-start(bf16[8,8,32,128]{3,2,1,0:T(8,128)(2,1)} %broadcast_in_dim.46), calls=%async_computation | async-start | bytes 1048576 | tf_op jit(solution)/shard_map/all_to_all | solution.py:598
  30.0 3.4 %collective-permute-start.7 = (bf16[8,256,128]{2,1,0:T(8,128)(2,1)S(1)}, bf16[8,256,128]{2,1,0:T(8,128)(2,1)S(1)}, u32[]{:S(2)}, u32[]{:S(2)}) collective-permute-start(bf16[8,256,128]{2,1,0:T(8,128)(2,1)S(1)} %fusion), channel_id=1, source_target_pairs={{0,16},{16,0},{32,48},{48,32},{64,80},{80,64},{96,112},{112,96},{1... | collective-permute-start | bytes 1572872 | tf_op jit(solution)/shard_map/ppermute | solution.py:606
  34.2 9.2 %prepare_queries.1 = (bf16[4,768,128]{2,1,0:T(8,128)(2,1)}, bf16[4,128,768]{2,1,0:T(8,128)(2,1)}, bf16[4,768,128]{2,1,0:T(8,128)(2,1)}, bf16[4,128,768]{2,1,0:T(...) custom-call(s32[24]{0:T(128)} %fusion.8.place_ref, ...), custom_call_target="tpu_custom_call" | custom-call | flops 100000000 | bytes 16000000 | tf_op jit(solution)/shard_map/prepare_queries/pallas_call | solution.py:466
  44.0 4.3 %collective-permute-start.8 = (bf16[8,8,32,128]{3,2,1,0:T(8,128)(2,1)S(1)}, bf16[8,8,32,128]{3,2,1,0:T(8,128)(2,1)S(1)}, u32[]{:S(2)}, u32[]{:S(2)}) collective-permute-start(bf16[8,8,32,128]{3,2,1,0:T(8,128)(2,1)S(1)} %all-to-all-done.parts_hbm), channel_id=1, source_target_pairs={{0,16},{16,0},{32,48},{48,32},{64,80},{80,64},{96,112},{112,96},{1... | collective-permute-start | bytes 1572872 | tf_op jit(solution)/shard_map/ppermute | solution.py:615
  50.6 23.6 %tree_attention.1 = (bf16[4,128,768]{2,1,0:T(8,128)(2,1)}, bf16[4,128,768]{2,1,0:T(8,128)(2,1)}, f32[2,128]{1,0:T(2,128)}, bf16[8,8,32,128]{3,2,1,0:T(8,128)(2,1...) custom-call(s32[576]{0:T(1024)} %reshape.21.table_ref, ...), custom_call_target="tpu_custom_call" | custom-call | flops 5435817984 | bytes 12000000 | tf_op jit(solution)/shard_map/tree_attention/pallas_call | solution.py:490
  74.9 2.7 %collective-permute-start.12 = (f32[2,128]{1,0:T(2,128)}, f32[2,128]{1,0:T(2,128)S(1)}, u32[]{:S(2)}, u32[]{:S(2)}) collective-permute-start(f32[2,128]{1,0:T(2,128)} %get-tuple-element.65), channel_id=1, source_target_pairs={{0,3},{1,2},{2,1},{3,0},{4,7},{5,6},{6,5},{7,4},{8,11},{9,10},{10,... | collective-permute-start | bytes 3080 | tf_op jit(solution)/shard_map/ppermute | solution.py:567
  78.2 2.0 %add.68 = bf16[8,8,32,128]{3,2,1,0:T(8,128)(2,1)} add(bf16[8,8,32,128]{3,2,1,0:T(8,128)(2,1)} %get-tuple-element.63, bf16[8,8,32,128]{3,2,1,0:T(8,128)(2,1)S(1)} %collective-permute-done.9) | non-fusion elementwise | flops 262144 | bytes 1572864 | tf_op jit(solution)/shard_map/add | solution.py:622
  80.2 3.5 %all-to-all-start.1 = ((bf16[8,8,32,128]{3,2,1,0:T(8,128)(2,1)}), bf16[8,8,32,128]{3,2,1,0:T(8,128)(2,1)S(1)}, u32[]{:S(2)}, u32[]{:S(2)}) async-start(bf16[8,8,32,128]{3,2,1,0:T(8,128)(2,1)} %add.68), calls=%async_computation.1 | async-start | bytes 1048576 | tf_op jit(solution)/shard_map/all_to_all | solution.py:598
  83.7 2.7 %collective-permute-start.15 = (f32[2,128]{1,0:T(2,128)S(1)}, f32[2,128]{1,0:T(2,128)S(1)}, u32[]{:S(2)}, u32[]{:S(2)}) collective-permute-start(f32[2,128]{1,0:T(2,128)S(1)} %add_add_fusion.4), channel_id=1, source_target_pairs={{0,12},{1,13},{2,14},{3,15},{4,8},{5,9},{6,10},{7,11},{8,4},{9,5},... | collective-permute-start | bytes 3080 | tf_op jit(solution)/shard_map/ppermute | solution.py:567
  87.3 5.4 %finish_queries.1 = (bf16[192,16,128]{2,1,0:T(8,128)(2,1)}, bf16[192,16,128]{2,1,0:T(8,128)(2,1)}) custom-call(f32[128,1]{1,0:T(8,128)} %copy.20.gain_ref, f32[2,128,768]{2,1,0:T(8,128)} %get-tuple-element.60.angle_hbm, bf16[4,128,768]{2,1,0:T(8,128)(2,1)} %get-tuple-element.69.out_t_hbm, bf16[4,128,768]{2,1,0:T(8,128)(2,1)} %get-tuple-element.70.dq_t_hbm, ...), custom_call_target="tpu_custom_call" | custom-call | flops 100000000 | bytes 10000000 | tf_op jit(solution)/shard_map/finish_queries/pallas_call | solution.py:522
  92.7 3.6 %collective-permute-start.18 = (f32[2,128]{1,0:T(2,128)S(1)}, f32[2,128]{1,0:T(2,128)S(1)}, u32[]{:S(2)}, u32[]{:S(2)}) collective-permute-start(f32[2,128]{1,0:T(2,128)S(1)} %add_add_fusion.3), channel_id=1, source_target_pairs={{0,192},{16,208},{32,224},{48,240},{64,128},{80,144},{96,160},{112... | collective-permute-start | bytes 3080 | tf_op jit(solution)/shard_map/ppermute | solution.py:567
  96.3 2.1 %collective-permute-start.17 = (f32[2,128]{1,0:T(2,128)S(1)}, f32[2,128]{1,0:T(2,128)S(1)}, u32[]{:S(2)}, u32[]{:S(2)}) collective-permute-start(f32[2,128]{1,0:T(2,128)S(1)} %add_add_fusion.3), channel_id=1, source_target_pairs={{0,128},{16,144},{32,160},{48,176},{64,192},{80,208},{96,224},{112... | collective-permute-start | bytes 3080 | tf_op jit(solution)/shard_map/ppermute | solution.py:567
  100.0 2.7 %collective-permute-done.17 = f32[2,128]{1,0:T(2,128)S(1)} collective-permute-done((f32[2,128]{1,0:T(2,128)S(1)}, f32[2,128]{1,0:T(2,128)S(1)}, u32[]{:S(2)}, u32[]{:S(2)}) %collective-permute-start.17) | collective-permute-done | bytes 1056 | tf_op jit(solution)/shard_map/ppermute | solution.py:567
  102.7 4.1 %collective-permute-start.29 = (f32[2,128]{1,0:T(2,128)S(1)}, f32[2,128]{1,0:T(2,128)S(1)}, u32[]{:S(2)}, u32[]{:S(2)}) collective-permute-start(f32[2,128]{1,0:T(2,128)S(1)} %add_add_fusion.2), channel_id=1, source_target_pairs={{0,48},{16,32},{32,16},{48,0},{64,112},{80,96},{96,80},{112,64},{1... | collective-permute-start | bytes 3080 | tf_op jit(solution)/shard_map/ppermute | solution.py:567
  109.1 2.7 %collective-permute-done.29 = f32[2,128]{1,0:T(2,128)S(1)} collective-permute-done((f32[2,128]{1,0:T(2,128)S(1)}, f32[2,128]{1,0:T(2,128)S(1)}, u32[]{:S(2)}, u32[]{:S(2)}) %collective-permute-start.29) | collective-permute-done | bytes 1056 | tf_op jit(solution)/shard_map/ppermute | solution.py:567
  118.6 3.2 %collective-permute-done.22.rest_1_ = bf16[8,32,128]{2,1,0:T(8,128)(2,1)S(1)} collective-permute-done((bf16[8,32,128]{2,1,0:T(8,128)(2,1)S(1)}, bf16[8,32,128]{2,1,0:T(8,128)(2,1)S(1)}, u32[]{:S(2)}, u32[]{:S(2)}) %collective-permute-start.22) | collective-permute-done | bytes 65568 | tf_op jit(solution)/shard_map/ppermute | solution.py:633
  121.9 2.2 %collective-permute-done.21.rest_0_ = bf16[8,32,128]{2,1,0:T(8,128)(2,1)S(1)} collective-permute-done((bf16[8,32,128]{2,1,0:T(8,128)(2,1)S(1)}, bf16[8,32,128]{2,1,0:T(8,128)(2,1)S(1)}, u32[]{:S(2)}, u32[]{:S(2)}) %collective-permute-start.21) | collective-permute-done | bytes 65568 | tf_op jit(solution)/shard_map/ppermute | solution.py:633
  124.1 1.4 %finish_keys.1 = (bf16[192,4,128]{2,1,0:T(4,128)(2,1)}, bf16[192,4,128]{2,1,0:T(4,128)(2,1)}) custom-call(f32[1,128]{1,0:T(1,128)S(1)} %bitcast.22, f32[10,192,128]{2,1,0:T(8,128)S(1)} %copy-done, bf16[8,192,128]{2,1,0:T(8,128)(2,1)S(1)} %copy-done.1, bf16[8,256,128]{2,1,0:T(8,128)(2,1)S(1)} %collective-permute-done.19.swap_ref, ...), custom_call_target="tpu_custom_call" | custom-call | flops 1000000 | bytes 4000000 | tf_op jit(solution)/shard_map/finish_keys/pallas_call | solution.py:538
  (86 shorter events, 22.3 us)
Async XLA Ops:
  2.7 21.3 %collective-permute-start.6 = (bf16[8,192,128]{2,1,0:T(8,128)(2,1)}, bf16[8,192,128]{2,1,0:T(8,128)(2,1)S(1)}, u32[]{:S(2)}, u32[]{:S(2)}) collective-permute-start(bf16[8,192,128]{2,1,0:T(8,128)(2,1)} %get-tuple-element.51.k_hbm.mine_hbm), channel_id=1, source_target_pairs={{0,32},{16,48},{32,64},{48,80},{64,96},{80,112},{96,128},{112,144}... | collective-permute-start | bytes 1179656 | tf_op jit(solution)/shard_map/ppermute | solution.py:591
  7.2 11.9 %collective-permute-start = (bf16[8,32,128]{2,1,0:T(8,128)(2,1)}, bf16[8,32,128]{2,1,0:T(8,128)(2,1)S(1)}, u32[]{:S(2)}, u32[]{:S(2)}) collective-permute-start(bf16[8,32,128]{2,1,0:T(8,128)(2,1)} %get-tuple-element.45), channel_id=1, source_target_pairs={{0,0},{16,192},{32,144},{1,1},{17,193},{33,145},{2,2},{18,194},{34... | collective-permute-start | bytes 196616 | tf_op jit(solution)/shard_map/ppermute | solution.py:590
  16.4 7.5 %collective-permute-start.2 = (bf16[8,32,128]{2,1,0:T(8,128)(2,1)}, bf16[8,32,128]{2,1,0:T(8,128)(2,1)S(1)}, u32[]{:S(2)}, u32[]{:S(2)}) collective-permute-start(bf16[8,32,128]{2,1,0:T(8,128)(2,1)} %get-tuple-element.47), channel_id=1, source_target_pairs={{0,64},{16,16},{32,208},{1,65},{17,17},{33,209},{2,66},{18,18},{34... | collective-permute-start | bytes 196616 | tf_op jit(solution)/shard_map/ppermute | solution.py:590
  17.9 6.0 %collective-permute-start.3 = (bf16[8,32,128]{2,1,0:T(8,128)(2,1)}, bf16[8,32,128]{2,1,0:T(8,128)(2,1)S(1)}, u32[]{:S(2)}, u32[]{:S(2)}) collective-permute-start(bf16[8,32,128]{2,1,0:T(8,128)(2,1)} %get-tuple-element.48), channel_id=1, source_target_pairs={{0,96},{16,48},{32,240},{1,97},{17,49},{33,241},{2,98},{18,50},{34... | collective-permute-start | bytes 196616 | tf_op jit(solution)/shard_map/ppermute | solution.py:590
  25.0 19.1 %all-to-all-start = ((bf16[8,8,32,128]{3,2,1,0:T(8,128)(2,1)}), bf16[8,8,32,128]{3,2,1,0:T(8,128)(2,1)S(1)}, u32[]{:S(2)}, u32[]{:S(2)}) async-start(bf16[8,8,32,128]{3,2,1,0:T(8,128)(2,1)} %broadcast_in_dim.46), calls=%async_computation | async-start | bytes 1048576 | tf_op jit(solution)/shard_map/all_to_all | solution.py:598
  30.0 13.4 %collective-permute-start.7 = (bf16[8,256,128]{2,1,0:T(8,128)(2,1)S(1)}, bf16[8,256,128]{2,1,0:T(8,128)(2,1)S(1)}, u32[]{:S(2)}, u32[]{:S(2)}) collective-permute-start(bf16[8,256,128]{2,1,0:T(8,128)(2,1)S(1)} %fusion), channel_id=1, source_target_pairs={{0,16},{16,0},{32,48},{48,32},{64,80},{80,64},{96,112},{112,96},{1... | collective-permute-start | bytes 1572872 | tf_op jit(solution)/shard_map/ppermute | solution.py:606
  44.0 5.8 %collective-permute-start.8 = (bf16[8,8,32,128]{3,2,1,0:T(8,128)(2,1)S(1)}, bf16[8,8,32,128]{3,2,1,0:T(8,128)(2,1)S(1)}, u32[]{:S(2)}, u32[]{:S(2)}) collective-permute-start(bf16[8,8,32,128]{3,2,1,0:T(8,128)(2,1)S(1)} %all-to-all-done.parts_hbm), channel_id=1, source_target_pairs={{0,16},{16,0},{32,48},{48,32},{64,80},{80,64},{96,112},{112,96},{1... | collective-permute-start | bytes 1572872 | tf_op jit(solution)/shard_map/ppermute | solution.py:615
  74.6 23.9 %collective-permute-start.19 = (bf16[8,256,128]{2,1,0:T(8,128)(2,1)}, bf16[8,256,128]{2,1,0:T(8,128)(2,1)S(1)}, u32[]{:S(2)}, u32[]{:S(2)}) collective-permute-start(bf16[8,256,128]{2,1,0:T(8,128)(2,1)} %get-tuple-element.78), channel_id=1, source_target_pairs={{0,16},{16,0},{32,48},{48,32},{64,80},{80,64},{96,112},{112,96},{1... | collective-permute-start | bytes 1572872 | tf_op jit(solution)/shard_map/ppermute | solution.py:623
  74.9 8.8 %collective-permute-start.12 = (f32[2,128]{1,0:T(2,128)}, f32[2,128]{1,0:T(2,128)S(1)}, u32[]{:S(2)}, u32[]{:S(2)}) collective-permute-start(f32[2,128]{1,0:T(2,128)} %get-tuple-element.65), channel_id=1, source_target_pairs={{0,3},{1,2},{2,1},{3,0},{4,7},{5,6},{6,5},{7,4},{8,11},{9,10},{10,... | collective-permute-start | bytes 3080 | tf_op jit(solution)/shard_map/ppermute | solution.py:567
  77.6 6.1 %collective-permute-start.11 = (f32[2,128]{1,0:T(2,128)}, f32[2,128]{1,0:T(2,128)S(1)}, u32[]{:S(2)}, u32[]{:S(2)}) collective-permute-start(f32[2,128]{1,0:T(2,128)} %get-tuple-element.65), channel_id=1, source_target_pairs={{0,2},{1,3},{2,0},{3,1},{4,6},{5,7},{6,4},{7,5},{8,10},{9,11},{10,... | collective-permute-start | bytes 3080 | tf_op jit(solution)/shard_map/ppermute | solution.py:567
  78.0 5.7 %collective-permute-start.10 = (f32[2,128]{1,0:T(2,128)}, f32[2,128]{1,0:T(2,128)S(1)}, u32[]{:S(2)}, u32[]{:S(2)}) collective-permute-start(f32[2,128]{1,0:T(2,128)} %get-tuple-element.65), channel_id=1, source_target_pairs={{0,1},{1,0},{2,3},{3,2},{4,5},{5,4},{6,7},{7,6},{8,9},{9,8},{10,11... | collective-permute-start | bytes 3080 | tf_op jit(solution)/shard_map/ppermute | solution.py:567
  80.2 22.5 %all-to-all-start.1 = ((bf16[8,8,32,128]{3,2,1,0:T(8,128)(2,1)}), bf16[8,8,32,128]{3,2,1,0:T(8,128)(2,1)S(1)}, u32[]{:S(2)}, u32[]{:S(2)}) async-start(bf16[8,8,32,128]{3,2,1,0:T(8,128)(2,1)} %add.68), calls=%async_computation.1 | async-start | bytes 1048576 | tf_op jit(solution)/shard_map/all_to_all | solution.py:598
  83.7 9.0 %collective-permute-start.15 = (f32[2,128]{1,0:T(2,128)S(1)}, f32[2,128]{1,0:T(2,128)S(1)}, u32[]{:S(2)}, u32[]{:S(2)}) collective-permute-start(f32[2,128]{1,0:T(2,128)S(1)} %add_add_fusion.4), channel_id=1, source_target_pairs={{0,12},{1,13},{2,14},{3,15},{4,8},{5,9},{6,10},{7,11},{8,4},{9,5},... | collective-permute-start | bytes 3080 | tf_op jit(solution)/shard_map/ppermute | solution.py:567
  86.5 6.2 %collective-permute-start.14 = (f32[2,128]{1,0:T(2,128)S(1)}, f32[2,128]{1,0:T(2,128)S(1)}, u32[]{:S(2)}, u32[]{:S(2)}) collective-permute-start(f32[2,128]{1,0:T(2,128)S(1)} %add_add_fusion.4), channel_id=1, source_target_pairs={{0,8},{1,9},{2,10},{3,11},{4,12},{5,13},{6,14},{7,15},{8,0},{9,1},... | collective-permute-start | bytes 3080 | tf_op jit(solution)/shard_map/ppermute | solution.py:567
  92.7 7.2 %collective-permute-start.18 = (f32[2,128]{1,0:T(2,128)S(1)}, f32[2,128]{1,0:T(2,128)S(1)}, u32[]{:S(2)}, u32[]{:S(2)}) collective-permute-start(f32[2,128]{1,0:T(2,128)S(1)} %add_add_fusion.3), channel_id=1, source_target_pairs={{0,192},{16,208},{32,224},{48,240},{64,128},{80,144},{96,160},{112... | collective-permute-start | bytes 3080 | tf_op jit(solution)/shard_map/ppermute | solution.py:567
  96.3 6.3 %collective-permute-start.17 = (f32[2,128]{1,0:T(2,128)S(1)}, f32[2,128]{1,0:T(2,128)S(1)}, u32[]{:S(2)}, u32[]{:S(2)}) collective-permute-start(f32[2,128]{1,0:T(2,128)S(1)} %add_add_fusion.3), channel_id=1, source_target_pairs={{0,128},{16,144},{32,160},{48,176},{64,192},{80,208},{96,224},{112... | collective-permute-start | bytes 3080 | tf_op jit(solution)/shard_map/ppermute | solution.py:567
  98.7 16.4 %collective-permute-start.20 = (bf16[8,192,128]{2,1,0:T(8,128)(2,1)S(1)}, bf16[8,192,128]{2,1,0:T(8,128)(2,1)S(1)}, u32[]{:S(2)}, u32[]{:S(2)}) collective-permute-start(bf16[8,192,128]{2,1,0:T(8,128)(2,1)S(1)} %fusion.1), channel_id=1, source_target_pairs={{32,0},{48,16},{64,32},{80,48},{96,64},{112,80},{128,96},{144,112}... | collective-permute-start | bytes 1179656 | tf_op jit(solution)/shard_map/ppermute | solution.py:626
  102.7 9.0 %collective-permute-start.29 = (f32[2,128]{1,0:T(2,128)S(1)}, f32[2,128]{1,0:T(2,128)S(1)}, u32[]{:S(2)}, u32[]{:S(2)}) collective-permute-start(f32[2,128]{1,0:T(2,128)S(1)} %add_add_fusion.2), channel_id=1, source_target_pairs={{0,48},{16,32},{32,16},{48,0},{64,112},{80,96},{96,80},{112,64},{1... | collective-permute-start | bytes 3080 | tf_op jit(solution)/shard_map/ppermute | solution.py:567
  106.8 6.2 %collective-permute-start.28 = (f32[2,128]{1,0:T(2,128)S(1)}, f32[2,128]{1,0:T(2,128)S(1)}, u32[]{:S(2)}, u32[]{:S(2)}) collective-permute-start(f32[2,128]{1,0:T(2,128)S(1)} %add_add_fusion.2), channel_id=1, source_target_pairs={{0,32},{16,48},{32,0},{48,16},{64,96},{80,112},{96,64},{112,80},{1... | collective-permute-start | bytes 3080 | tf_op jit(solution)/shard_map/ppermute | solution.py:567
  107.8 6.6 %collective-permute-start.27 = (f32[2,128]{1,0:T(2,128)S(1)}, f32[2,128]{1,0:T(2,128)S(1)}, u32[]{:S(2)}, u32[]{:S(2)}) collective-permute-start(f32[2,128]{1,0:T(2,128)S(1)} %add_add_fusion.2), channel_id=1, source_target_pairs={{0,16},{16,0},{32,48},{48,32},{64,80},{80,64},{96,112},{112,96},{1... | collective-permute-start | bytes 3080 | tf_op jit(solution)/shard_map/ppermute | solution.py:567
  107.8 8.6 %collective-permute-start.26 = (bf16[8,32,128]{2,1,0:T(8,128)(2,1)S(1)}, bf16[8,32,128]{2,1,0:T(8,128)(2,1)S(1)}, u32[]{:S(2)}, u32[]{:S(2)}) collective-permute-start(bf16[8,32,128]{2,1,0:T(8,128)(2,1)S(1)} %reduce_sum.12), channel_id=1, source_target_pairs={{160,0},{112,16},{161,1},{113,17},{162,2},{114,18},{163,3},{115,19... | collective-permute-start | bytes 196616 | tf_op jit(solution)/shard_map/ppermute | solution.py:633
  111.8 6.4 %collective-permute-start.25 = (bf16[8,32,128]{2,1,0:T(8,128)(2,1)S(1)}, bf16[8,32,128]{2,1,0:T(8,128)(2,1)S(1)}, u32[]{:S(2)}, u32[]{:S(2)}) collective-permute-start(bf16[8,32,128]{2,1,0:T(8,128)(2,1)S(1)} %reduce_sum.12), channel_id=1, source_target_pairs={{128,0},{80,16},{129,1},{81,17},{130,2},{82,18},{131,3},{83,19},{1... | collective-permute-start | bytes 196616 | tf_op jit(solution)/shard_map/ppermute | solution.py:633
  115.1 6.8 %collective-permute-start.22 = (bf16[8,32,128]{2,1,0:T(8,128)(2,1)S(1)}, bf16[8,32,128]{2,1,0:T(8,128)(2,1)S(1)}, u32[]{:S(2)}, u32[]{:S(2)}) collective-permute-start(bf16[8,32,128]{2,1,0:T(8,128)(2,1)S(1)} %reduce_sum.12), channel_id=1, source_target_pairs={{32,0},{224,16},{176,32},{33,1},{225,17},{177,33},{34,2},{226,18},... | collective-permute-start | bytes 196616 | tf_op jit(solution)/shard_map/ppermute | solution.py:633
  116.4 7.7 %collective-permute-start.21 = (bf16[8,32,128]{2,1,0:T(8,128)(2,1)S(1)}, bf16[8,32,128]{2,1,0:T(8,128)(2,1)S(1)}, u32[]{:S(2)}, u32[]{:S(2)}) collective-permute-start(bf16[8,32,128]{2,1,0:T(8,128)(2,1)S(1)} %reduce_sum.12), channel_id=1, source_target_pairs={{0,0},{192,16},{144,32},{1,1},{193,17},{145,33},{2,2},{194,18},{14... | collective-permute-start | bytes 196616 | tf_op jit(solution)/shard_map/ppermute | solution.py:633
  (18 other events, 198.5 us)
